TPU v7x, 256 devices: a whole 4x4x8 slice. The times are simulated.
256 devices in a mesh: seq: 64 (over y, z_lo, x), tensor: 4 (over z_hi, core).
Axes of the slice: x: 4, y: 4, z: 8 (z_hi: 2, z_lo: 4; z = z_hi * 4 + z_lo), core: 2. Of those that a mesh axis runs over, the one named last changes fastest.
Arguments:
- queries: bfloat16 [32768, 3072], P('seq', 'tensor'), may hold values from -180 to 180, as said below
- ref_keys: bfloat16 [1024, 3072], P('seq', 'tensor'), may hold values from -6 to 6
- ref_values: bfloat16 [1024, 3072], P('seq', 'tensor'), may hold values from -6 to 6
- grad_out: bfloat16 [32768, 3072], P('seq', 'tensor'), may hold values from -12 to 12
- key_weight: bfloat16 [3072, 3072], P(None, 'tensor'), may hold values from -0.109375 to 0.109375
- value_weight: bfloat16 [3072, 3072], P(None, 'tensor'), may hold values from -0.109375 to 0.109375
Outputs:
- grad_queries: bfloat16 [32768, 3072], P('seq', 'tensor')
- grad_ref_rows: bfloat16 [1024, 3072], P('seq', 'tensor')
Inputs may be any that keep to these rules, and one draw needn't show every extreme that they name: `queries`: queries of order one, some rows larger.
All inputs are finite; a program needn't handle non-finite values.
Results may differ from a plain program's by a relative error of at most 0.015.
Values may be sent and summed in bfloat16 or wider, within the bound.
No kernel may reach another device: no remote copies, remote signals or barrier semaphores. Data moves between devices by JAX's collectives and lax.ppermute only.
A program may use at most 128 MiB of HBM per device.

v0:
```python
import jax
import jax.numpy as jnp
from jax import lax
from jax.sharding import PartitionSpec as P

HD = 128


def head_terms(queries, keys_all, values_all, grad_out, head):
    scale = 1.0 / HD**0.5
    lo_col = head * HD
    query_h = queries[:, lo_col : lo_col + HD]
    key_h = keys_all[:, lo_col : lo_col + HD]
    value_h = values_all[:, lo_col : lo_col + HD]
    grad_h = grad_out[:, lo_col : lo_col + HD]
    scores = jnp.dot(query_h, key_h.T, preferred_element_type=jnp.float32) * scale
    probs = jax.nn.softmax(scores, axis=-1)
    probs_b = probs.astype(jnp.bfloat16)
    grad_probs = jnp.dot(grad_h, value_h.T, preferred_element_type=jnp.float32)
    delta = jnp.sum(probs * grad_probs, axis=-1, keepdims=True)
    grad_scores = (probs * (grad_probs - delta)).astype(jnp.bfloat16)
    grad_query = (jnp.dot(grad_scores, key_h, preferred_element_type=jnp.float32) * scale).astype(
        jnp.bfloat16
    )
    grad_key = jnp.dot(grad_scores.T, query_h, preferred_element_type=jnp.float32) * scale
    grad_value = jnp.dot(probs_b.T, grad_h, preferred_element_type=jnp.float32)
    return (grad_query, grad_key, grad_value)


def head_range(queries, keys_all, values_all, grad_out, first, count):
    query_list, key_list, value_list = ([], [], [])
    for head in range(first, first + count):
        grad_query, grad_key, grad_value = head_terms(queries, keys_all, values_all, grad_out, head)
        query_list.append(grad_query)
        key_list.append(grad_key)
        value_list.append(grad_value)
    return (query_list, jnp.concatenate(key_list, axis=1), jnp.concatenate(value_list, axis=1))


def project_exact(keys_own, values_own, key_weight, value_weight):
    key_cols = key_weight.astype(jnp.float32)
    value_cols = value_weight.astype(jnp.float32)
    rows = jnp.dot(
        keys_own, key_cols.T, precision=lax.Precision.HIGHEST, preferred_element_type=jnp.float32
    )
    return rows + jnp.dot(
        values_own,
        value_cols.T,
        precision=lax.Precision.HIGHEST,
        preferred_element_type=jnp.float32,
    )


def shards(queries, ref_keys, ref_values, grad_out, key_weight, value_weight):
    keys_all, values_all = (
        lax.all_gather(ref_keys, "seq", axis=0, tiled=True),
        lax.all_gather(ref_values, "seq", axis=0, tiled=True),
    )
    local_heads = queries.shape[1] // HD
    ranges = (0, local_heads)
    query_list = []
    first, count = ranges
    group_queries, key_terms, value_terms = head_range(
        queries, keys_all, values_all, grad_out, first, count
    )
    query_list = query_list + group_queries
    key_part = key_terms.astype(jnp.bfloat16)
    value_part = value_terms.astype(jnp.bfloat16)
    key_held, value_held = lax.optimization_barrier((key_part, value_part))
    key_wide = key_held.astype(jnp.float32)
    value_wide = value_held.astype(jnp.float32)
    keys_own = lax.psum_scatter(key_wide, "seq", scatter_dimension=0, tiled=True)
    values_own = lax.psum_scatter(value_wide, "seq", scatter_dimension=0, tiled=True)
    partial_value = project_exact(keys_own, values_own, key_weight, value_weight)
    grad_queries = jnp.concatenate(query_list, axis=1)
    grad_rows = lax.psum_scatter(
        partial_value.astype(jnp.bfloat16), "tensor", scatter_dimension=1, tiled=True
    )
    return (grad_queries, grad_rows)


def solution(mesh):
    placed = (
        P("seq", "tensor"),
        P("seq", "tensor"),
        P("seq", "tensor"),
        P("seq", "tensor"),
        P(None, "tensor"),
        P(None, "tensor"),
    )
    return jax.shard_map(
        shards,
        mesh=mesh,
        in_specs=placed,
        out_specs=(P("seq", "tensor"), P("seq", "tensor")),
        check_vma=False,
    )
```

profile of v0, /device:TPU:1, one launch (start us, length us, event | category | flops | bytes accessed | tf_op | source)
XLA Modules:
  0.0 1526.0 jit_solution(15675450137437767035)
XLA Ops:
  7.2 0.7 all-gather.3.cloned.1.call-update
  7.9 0.7 all-gather.5.cloned.1.call-update
  8.7 308.8 %all-gather.3.cloned.1.call-done = bf16[1024,768]{1,0:T(8,128)(2,1)} async-done(((bf16[16,768]{1,0:T(8,128)(2,1)}), bf16[1024,768]{1,0:T(8,128)(2,1)}) %all-gather.3.cloned.1.call-update) | async-done | bytes 1572880 | tf_op jit(solution)/shard_map/all_gather | solution.py:56
  317.5 1.5 multiply_reduce_fusion.11
  319.5 2.3 fusion.25
  321.8 344.2 %all-gather.5.cloned.1.call-done = bf16[1024,768]{1,0:T(8,128)(2,1)} async-done(((bf16[16,768]{1,0:T(8,128)(2,1)}), bf16[1024,768]{1,0:T(8,128)(2,1)}) %all-gather.5.cloned.1.call-update) | async-done | bytes 1572880 | tf_op jit(solution)/shard_map/all_gather | solution.py:57
  666.0 1.7 multiply_reduce_fusion.5
  667.7 0.6 multiply_convert_fusion.5
  671.0 0.7 fusion.26
  672.7 0.7 fusion.27
  674.4 0.7 fusion.28
  676.2 0.7 fusion.29
  677.9 0.7 fusion.30
  678.6 0.7 copy-done.15
  679.3 0.7 multiply_reduce_fusion.4
  681.6 0.7 multiply_reduce_fusion.3
  683.3 0.7 multiply_reduce_fusion.2
  684.0 0.6 multiply_convert_fusion.2
  685.0 0.7 multiply_reduce_fusion.1
  686.7 0.7 multiply_reduce_fusion
  688.1 1.1 copy-done.5
  689.5 2.1 copy.10
  691.7 1.3 copy-done.13
  693.0 2.1 copy.12
  695.4 1.1 copy-done.1
  697.0 1.9 fusion.34
  700.3 361.1 %reduce-scatter.10.cloned.1.call-done = f32[16,768]{1,0:T(8,128)} async-done(((f32[1024,768]{1,0:T(8,128)}), f32[16,768]{1,0:T(8,128)}) %reduce-scatter.10.cloned.1.call-update) | async-done | bytes 49168
  1061.5 6.8 fusion.109
  1068.3 366.2 %reduce-scatter.12.cloned.1.call-done = f32[16,768]{1,0:T(8,128)} async-done(((f32[1024,768]{1,0:T(8,128)}), f32[16,768]{1,0:T(8,128)}) %reduce-scatter.12.cloned.1.call-update) | async-done | bytes 49168
  1434.5 6.7 fusion
  1441.8 1.2 copy.9
  1442.9 76.6 %reduce-scatter.8.cloned.1.call-done = bf16[16,768]{1,0:T(8,128)(2,1)} async-done(((bf16[16,3072]{1,0:T(8,128)(2,1)}), bf16[16,768]{1,0:T(8,128)(2,1)}) %reduce-scatter.8.cloned.1.call-update) | async-done | bytes 24592 | tf_op jit(solution)/shard_map/reduce_scatter | solution.py:76
  (64 shorter events, 15.0 us)
Async XLA Ops:
  7.2 310.3 %all-gather.3.cloned.1.call-start = ((), (), s32[]{:S(2)}) async-start(), calls=%async_computation.3 | async-start | bytes 1597440 | tf_op jit(solution)/shard_map/all_gather | solution.py:56
  7.9 658.1 %all-gather.5.cloned.1.call-start = ((), (), s32[]{:S(2)}) async-start(), calls=%async_computation.4 | async-start | bytes 1597440 | tf_op jit(solution)/shard_map/all_gather | solution.py:57
  8.6 1052.8 %reduce-scatter.10.cloned.1.call-start = ((), (), s32[]{:S(2)}) async-start(), calls=%async_computation.6 | async-start | bytes 3194880
  667.7 1.1 copy-start.14
  667.7 1.7 copy-start
  669.4 1.4 copy-start.11
  669.4 1.6 copy-start.16
  677.9 1.4 copy-start.15
  679.3 1.1 copy-start.12
  681.1 1.3 copy-start.2
  683.0 1.1 copy-start.3
  684.7 1.1 copy-start.7
  686.4 1.1 copy-start.9
  688.1 1.1 copy-start.5
  691.6 1.4 copy-start.13
  691.6 742.9 %reduce-scatter.12.cloned.1.call-start = ((), (), s32[]{:S(2)}) async-start(), calls=%async_computation.7 | async-start | bytes 3194880
  695.1 1.4 copy-start.1
  695.1 824.4 %reduce-scatter.8.cloned.1.call-start = ((), (), s32[]{:S(2)}) async-start(), calls=%async_computation.5 | async-start | bytes 122880 | tf_op jit(solution)/shard_map/reduce_scatter | solution.py:76
  696.5 2.4 copy-start.4
  696.5 2.9 copy-start.8
  697.0 2.9 copy-start.10
  1068.3 373.0 %copy-start.6 = (bf16[512,1024]{1,0:T(8,128)(2,1)S(1)}, bf16[512,1024]{1,0:T(8,128)(2,1)}, u32[]{:S(2)}) copy-start(bf16[512,1024]{1,0:T(8,128)(2,1)} %copy-done.5) | copy-start | bytes 3145732
Sparse Core Ops, SparseCore 0:
  9.8 307.6 all-gather.2
  319.3 346.6 all-gather.4
  691.7 369.6 reduce-scatter.9
  1064.0 370.4 reduce-scatter.11
  1441.4 78.0 reduce-scatter.7
where the time goes:
time: 1530 us
  waiting for transfers between devices  1460 us (95%)
  matrix products  35.2 us (2%)
    unnamed x7, waiting for transfers between devices  729 us
    all_gather x1, waiting for transfers between devices, shards(): lax.all_gather(ref_values, 'seq', axis=0, tiled=True)  344 us
    all_gather x1, waiting for transfers between devices, shards(): lax.all_gather(ref_keys, 'seq', axis=0, tiled=True)  309 us
    reduce_scatter x1, waiting for transfers between devices, shards(): lax.psum_scatter(partial_value.astype(jnp.bfloat16), 'tensor', scatter_di...  76.6 us
  transfers between devices with their start and end apart: 5, of which 5 were waited for; matrix products, arithmetic and copies ran while one was open for 1% of the time, Pallas kernels for 0%

commit v1 on v0

v1 whole, which is shorter than its diff:
```python
import functools
import math

import jax
import jax.numpy as jnp
from jax import lax
from jax.experimental import pallas as pl
from jax.experimental.pallas import tpu as pltpu
from jax.sharding import PartitionSpec as P

HD = 128
SCALE = 1.0 / HD**0.5
NN = (((1,), (0,)), ((), ()))
NT = (((1,), (1,)), ((), ()))
TN = (((0,), (0,)), ((), ()))

SIDE = 4
CORES = 2
TENSOR = 4
BOTH = ("seq", "tensor")


def dot(a, b, dims=NN):
    return lax.dot_general(a, b, dims, preferred_element_type=jnp.float32)


def ring_pairs(axes, step):
    pairs = []
    for y in range(SIDE):
        for z in range(SIDE):
            for x in range(SIDE):
                for t in range(TENSOR):
                    place = {"y": y, "z": z, "x": x}
                    to = dict(place)
                    along = axes[t % CORES]
                    to[along] = (place[along] + step) % SIDE
                    pairs.append(
                        tuple(
                            ((p["y"] * SIDE + p["z"]) * SIDE + p["x"]) * TENSOR + t
                            for p in (place, to)
                        )
                    )
    return pairs


def ring_send(block, axes, step):
    return lax.ppermute(block, BOTH, ring_pairs(axes, step))


def flip_send(block, flip):
    pairs = [(i, i ^ flip) for i in range(SIDE**3 * TENSOR)]
    return lax.ppermute(block, BOTH, pairs)


STEPS = (1, 3, 2)


def gather(block, axes):
    return [block] + [ring_send(block, axes, step) for step in STEPS]


def scatter(blocks, axes):
    back = [(SIDE - step) % SIDE for step in STEPS]
    return [ring_send(block, axes, step) for block, step in zip(blocks[1:], back)]


def attention_kernel(chunk, q_ref, g_ref, *refs):
    keys, values = refs[0:SIDE], refs[SIDE : 2 * SIDE]
    dq_ref, parts = refs[2 * SIDE], refs[2 * SIDE + 1 : 3 * SIDE + 1]
    probs_ref, grads_ref = refs[3 * SIDE + 1 :]
    rows = keys[0].shape[0]
    tokens = q_ref.shape[0]
    for at in range(0, tokens, chunk):
        some = pl.ds(at, chunk)
        q, g = q_ref[some, :], g_ref[some, :]
        scores = [dot(k[...], q, NT) for k in keys]
        top = functools.reduce(
            jnp.maximum, [jnp.max(s, axis=0, keepdims=True) for s in scores]
        )
        raised = [jnp.exp2((s - top) * (SCALE * math.log2(math.e))) for s in scores]
        inverse = 1.0 / sum(jnp.sum(e, axis=0, keepdims=True) for e in raised)
        probs = [e * inverse for e in raised]
        grad_probs = [dot(v[...], g, NT) for v in values]
        delta = sum(
            jnp.sum(p * d, axis=0, keepdims=True) for p, d in zip(probs, grad_probs)
        )
        for i, (p, d) in enumerate(zip(probs, grad_probs)):
            here = pl.ds(i * rows, rows)
            probs_ref[here, some] = p.astype(jnp.bfloat16)
            grads_ref[here, some] = (p * (d - delta)).astype(jnp.bfloat16)
    q, g = q_ref[...], g_ref[...]
    dq = jnp.zeros((HD, tokens), jnp.float32)
    for i in range(SIDE):
        here = pl.ds(i * rows, rows)
        grads = grads_ref[here, :]
        parts[i][:, :HD] = (dot(grads, q) * SCALE).astype(jnp.bfloat16)
        parts[i][:, HD:] = dot(probs_ref[here, :], g).astype(jnp.bfloat16)
        dq += dot(keys[i][...], grads, TN)
    dq_ref[...] = (dq.T * SCALE).astype(jnp.bfloat16)


def attention(queries, grad_out, blocks):
    tokens, width = queries.shape
    heads = width // HD
    rows = blocks[0].shape[0]
    token_spec = pl.BlockSpec((tokens, HD), lambda h: (0, h))
    key_spec = pl.BlockSpec((rows, HD), lambda h: (0, h))
    value_spec = pl.BlockSpec((rows, HD), lambda h: (0, heads + h))
    part_spec = pl.BlockSpec((rows, 2 * HD), lambda h: (0, h))
    return pl.pallas_call(
        functools.partial(attention_kernel, tokens // 2),
        grid=(heads,),
        in_specs=[token_spec] * 2 + [key_spec] * SIDE + [value_spec] * SIDE,
        out_specs=[token_spec] + [part_spec] * SIDE,
        out_shape=[jax.ShapeDtypeStruct(queries.shape, jnp.bfloat16)]
        + [jax.ShapeDtypeStruct((rows, 2 * width), jnp.bfloat16)] * SIDE,
        scratch_shapes=[pltpu.VMEM((SIDE * rows, tokens), jnp.bfloat16)] * 2,
        compiler_params=pltpu.CompilerParams(vmem_limit_bytes=32 * 2**20),
        name="attention_grads",
    )(queries, grad_out, *blocks, *blocks)


def project_kernel(own_ref, a_ref, b_ref, c_ref, key_ref, value_ref, out_ref):
    total = own_ref[...]
    for ref in (a_ref, b_ref, c_ref):
        total += ref[...].astype(jnp.float32)
    rows, width = total.shape
    high = total.astype(jnp.bfloat16)
    low = (total - high.astype(jnp.float32)).astype(jnp.bfloat16)
    both = jnp.concatenate([high, low], axis=0)
    pieces = [both[:, at : at + HD] for at in range(0, width, HD)]
    result = dot(jnp.concatenate(pieces[0::2], axis=1), key_ref[...], NT)
    result += dot(jnp.concatenate(pieces[1::2], axis=1), value_ref[...], NT)
    out_ref[...] = (result[:rows] + result[rows:]).astype(jnp.bfloat16)


def project(own, received, key_weight, value_weight):
    rows, width = own.shape
    features, columns = key_weight.shape
    block = 512
    sum_spec = pl.BlockSpec((rows, width), lambda n: (0, 0))
    weight_spec = pl.BlockSpec((block, columns), lambda n: (n, 0))
    return pl.pallas_call(
        project_kernel,
        grid=(features // block,),
        in_specs=[sum_spec] * 4 + [weight_spec] * 2,
        out_specs=pl.BlockSpec((rows, block), lambda n: (0, n)),
        out_shape=jax.ShapeDtypeStruct((rows, features), jnp.bfloat16),
        compiler_params=pltpu.CompilerParams(vmem_limit_bytes=16 * 2**20),
        name="project_rows",
    )(own, *received, key_weight, value_weight)


def shards(queries, ref_keys, ref_values, grad_out, key_weight, value_weight):
    rows = jnp.concatenate([ref_keys, ref_values], axis=1)
    rows = jnp.concatenate(gather(rows, ("z", "z")), axis=0)
    rows = jnp.concatenate(gather(rows, ("x", "y")), axis=0)
    blocks = gather(rows, ("y", "x"))

    grad_queries, *parts = attention(queries, grad_out, blocks)

    total = parts[0].astype(jnp.float32)
    received = scatter(parts, ("y", "x"))
    for axes in (("x", "y"), ("z", "z")):
        for r in received:
            total += r.astype(jnp.float32)
        cut = jnp.split(total, SIDE, axis=0)
        total = cut[0]
        received = scatter([c.astype(jnp.bfloat16) for c in cut], axes)
    result = project(total, received, key_weight, value_weight)

    columns = result.shape[1] // TENSOR
    me = lax.axis_index("tensor")

    def block_of(flip):
        return lax.dynamic_slice_in_dim(result, (me ^ flip) * columns, columns, axis=1)

    grad_rows = block_of(0).astype(jnp.float32)
    for r in [flip_send(block_of(flip), flip) for flip in (1, 2, 3)]:
        grad_rows += r.astype(jnp.float32)
    return grad_queries, grad_rows.astype(jnp.bfloat16)


def solution(mesh):
    placed = (
        P("seq", "tensor"),
        P("seq", "tensor"),
        P("seq", "tensor"),
        P("seq", "tensor"),
        P(None, "tensor"),
        P(None, "tensor"),
    )
    return jax.shard_map(
        shards,
        mesh=mesh,
        in_specs=placed,
        out_specs=(P("seq", "tensor"), P("seq", "tensor")),
        check_vma=False,
    )
```

time: 1530 us -> 130 us (0.08)
  waiting for transfers between devices: 1460 us -> 63.9 us
  starting transfers between devices: 0.42 us -> 38.4 us
  matrix products: 35.2 us -> 0 us
  Pallas kernels: 0 us -> 18.9 us
    unnamed x7 -> x0, waiting for transfers between devices: 729 us -> none
    all_gather x2 -> x0, waiting for transfers between devices: 653 us -> none  [the longest x1 344 us: shards(): lax.all_gather(ref_values, 'seq', axis=0, tiled=True)]
    reduce_scatter x1 -> x0, waiting for transfers between devices: 76.6 us -> none  [shards(): lax.psum_scatter(partial_value.astype(jnp.bfloat16), 'tensor', scatter_di...]
    ppermute x0 -> x21, waiting for transfers between devices: none -> 63.9 us  [the longest x18 56.8 us: ring_send(): return lax.ppermute(block, BOTH, ring_pairs(axes, step))]
    ppermute x0 -> x21, starting transfers between devices: none -> 38.4 us  [the longest x18 22.8 us: ring_send(): return lax.ppermute(block, BOTH, ring_pairs(axes, step))]
    dot_general x32 -> x0, matrix products: 35.2 us -> none  [the longest x1 6.8 us: project_exact(): jnp.dot(keys_own, key_cols.T, precision=lax.Precision.HIGHEST, preferred_...]
    pallas_call x0 -> x2, Pallas kernels: none -> 18.9 us  [the longest x1 15.5 us: attention(): pl.pallas_call(functools.partial(attention_kernel, tokens // 2), grid=(he...]
  transfers between devices with their start and end apart: 5 -> 21, of which waited for: 5 -> 17; matrix products, arithmetic and copies ran while one was open for 1% -> 0% of each run, Pallas kernels for 0% -> 0%
where the time goes in v1:
time: 130 us; the launch traced here: 129 us
  waiting for transfers between devices  63.9 us (49%)
  starting transfers between devices  38.4 us (30%)
  Pallas kernels  18.9 us (15%)
  local copies, waits for them, and re-layouts  6.42 us (5%)
    ppermute x18, waiting for transfers between devices, ring_send(): return lax.ppermute(block, BOTH, ring_pairs(axes, step))  56.8 us
    ppermute x18, starting transfers between devices, ring_send(): return lax.ppermute(block, BOTH, ring_pairs(axes, step))  22.8 us
    ppermute x3, starting transfers between devices, flip_send(): return lax.ppermute(block, BOTH, pairs)  15.6 us
    pallas_call x1, Pallas kernels, attention(): pl.pallas_call(functools.partial(attention_kernel, tokens // 2), grid=(he...  15.5 us
    ppermute x3, waiting for transfers between devices, flip_send(): return lax.ppermute(block, BOTH, pairs)  7.09 us
    unnamed x14, local copies, waits for them, and re-layouts  5.58 us
    pallas_call x1, Pallas kernels, project(): pl.pallas_call(project_kernel, grid=(features // block,), in_specs=[sum_s...  3.44 us
  transfers between devices with their start and end apart: 21, of which 17 were waited for; matrix products, arithmetic and copies ran while one was open for 0% of the time, Pallas kernels for 0%

profile of v1, /device:TPU:1, one launch (start us, length us, event | category | flops | bytes accessed | tf_op | source)
XLA Modules:
  0.0 129.5 jit_solution(2451228889453655009)
XLA Ops:
  0.6 0.9 constant_dynamic-update-slice_fusion.1
  2.2 2.5 %collective-permute-start = (bf16[16,1536]{1,0:T(8,128)(2,1)S(1)}, bf16[16,1536]{1,0:T(8,128)(2,1)S(1)}, u32[]{:S(2)}, u32[]{:S(2)}) collective-permute-start(bf16[16,1536]{1,0:T(8,128)(2,1)S(1)} %get-tuple-element.25), channel_id=1, source_target_pairs={{0,16},{1,17},{2,18},{3,19},{4,20},{5,21},{6,22},{7,23},{8,24},{9,... | collective-permute-start | bytes 147464 | tf_op jit(solution)/shard_map/ppermute | solution.py:47
  4.7 2.7 %collective-permute-start.1 = (bf16[16,1536]{1,0:T(8,128)(2,1)S(1)}, bf16[16,1536]{1,0:T(8,128)(2,1)S(1)}, u32[]{:S(2)}, u32[]{:S(2)}) collective-permute-start(bf16[16,1536]{1,0:T(8,128)(2,1)S(1)} %get-tuple-element.25), channel_id=1, source_target_pairs={{0,48},{1,49},{2,50},{3,51},{4,52},{5,53},{6,54},{7,55},{8,56},{9,... | collective-permute-start | bytes 147464 | tf_op jit(solution)/shard_map/ppermute | solution.py:47
  7.7 1.2 collective-permute-done
  8.9 3.6 %collective-permute-done.2 = bf16[16,1536]{1,0:T(8,128)(2,1)S(1)} collective-permute-done((bf16[16,1536]{1,0:T(8,128)(2,1)S(1)}, bf16[16,1536]{1,0:T(8,128)(2,1)S(1)}, u32[]{:S(2)}, u32[]{:S(2)}) %collective-permute-start.2) | collective-permute-done | bytes 49184 | tf_op jit(solution)/shard_map/ppermute | solution.py:47
  12.9 2.4 %collective-permute-start.4 = (bf16[64,1536]{1,0:T(8,128)(2,1)S(1)}, bf16[64,1536]{1,0:T(8,128)(2,1)S(1)}, u32[]{:S(2)}, u32[]{:S(2)}) collective-permute-start(bf16[64,1536]{1,0:T(8,128)(2,1)S(1)} %pad_maximum_fusion), channel_id=1, source_target_pairs={{0,12},{1,193},{2,14},{3,195},{4,0},{5,197},{6,2},{7,199},{8,4},{9... | collective-permute-start | bytes 589832 | tf_op jit(solution)/shard_map/ppermute | solution.py:47
  16.0 2.3 %collective-permute-done.3 = bf16[64,1536]{1,0:T(8,128)(2,1)S(1)} collective-permute-done((bf16[64,1536]{1,0:T(8,128)(2,1)S(1)}, bf16[64,1536]{1,0:T(8,128)(2,1)S(1)}, u32[]{:S(2)}, u32[]{:S(2)}) %collective-permute-start.3) | collective-permute-done | bytes 196640 | tf_op jit(solution)/shard_map/ppermute | solution.py:47
  18.4 1.6 %collective-permute-done.4 = bf16[64,1536]{1,0:T(8,128)(2,1)S(1)} collective-permute-done((bf16[64,1536]{1,0:T(8,128)(2,1)S(1)}, bf16[64,1536]{1,0:T(8,128)(2,1)S(1)}, u32[]{:S(2)}, u32[]{:S(2)}) %collective-permute-start.4) | collective-permute-done | bytes 196640 | tf_op jit(solution)/shard_map/ppermute | solution.py:47
  20.0 1.3 collective-permute-done.5
  22.0 2.1 %collective-permute-start.7 = (bf16[256,1536]{1,0:T(8,128)(2,1)S(1)}, bf16[256,1536]{1,0:T(8,128)(2,1)S(1)}, u32[]{:S(2)}, u32[]{:S(2)}) collective-permute-start(bf16[256,1536]{1,0:T(8,128)(2,1)S(1)} %constant_dynamic-update-slice_fusion.2.refs_0_.refs_4_), channel_id=1, source_target_pairs={{0,192},{1,13},{2,194},{3,15},{4,196},{5,1},{6,198},{7,3},{8,200},... | collective-permute-start | bytes 2359304 | tf_op jit(solution)/shard_map/ppermute | solution.py:47
  24.1 0.9 collective-permute-start.8
  25.0 8.8 %collective-permute-done.6.refs_1_.refs_5_ = bf16[256,1536]{1,0:T(8,128)(2,1)S(1)} collective-permute-done((bf16[256,1536]{1,0:T(8,128)(2,1)S(1)}, bf16[256,1536]{1,0:T(8,128)(2,1)S(1)}, u32[]{:S(2)}, u32[]{:S(2)}) %collective-permute-start.6) | collective-permute-done | bytes 786464 | tf_op jit(solution)/shard_map/ppermute | solution.py:47
  33.8 7.7 %collective-permute-done.7.refs_2_.refs_6_ = bf16[256,1536]{1,0:T(8,128)(2,1)S(1)} collective-permute-done((bf16[256,1536]{1,0:T(8,128)(2,1)S(1)}, bf16[256,1536]{1,0:T(8,128)(2,1)S(1)}, u32[]{:S(2)}, u32[]{:S(2)}) %collective-permute-start.7) | collective-permute-done | bytes 786464 | tf_op jit(solution)/shard_map/ppermute | solution.py:47
  41.5 1.4 %collective-permute-done.8.refs_3_.refs_7_ = bf16[256,1536]{1,0:T(8,128)(2,1)S(1)} collective-permute-done((bf16[256,1536]{1,0:T(8,128)(2,1)S(1)}, bf16[256,1536]{1,0:T(8,128)(2,1)S(1)}, u32[]{:S(2)}, u32[]{:S(2)}) %collective-permute-start.8) | collective-permute-done | bytes 786464 | tf_op jit(solution)/shard_map/ppermute | solution.py:47
  42.9 15.5 %attention_grads.1 = (bf16[512,768]{1,0:T(8,128)(2,1)}, bf16[256,1536]{1,0:T(8,128)(2,1)S(1)}, bf16[256,1536]{1,0:T(8,128)(2,1)S(1)}, bf16[256,1536]{1,0:T(8,128)(2,1)S(1)}, bf16[256,1536]{1,0:T(8,128)(2,1)S(1)}) custom-call(bf16[512,768]{1,0:T(8,128)(2,1)S(1)} %copy-done.2, bf16[512,768]{1,0:T(8,128)(2,1)S(1)} %copy-done.3, ...), custom_call_target="tpu_custom_call" | custom-call | tf_op jit(solution)/shard_map/attention_grads/pallas_call | solution.py:110
  58.3 0.9 collective-permute-start.10
  59.2 2.4 %collective-permute-start.11 = (bf16[256,1536]{1,0:T(8,128)(2,1)S(1)}, bf16[256,1536]{1,0:T(8,128)(2,1)S(1)}, u32[]{:S(2)}, u32[]{:S(2)}) collective-permute-start(bf16[256,1536]{1,0:T(8,128)(2,1)S(1)} %get-tuple-element.11), channel_id=1, source_target_pairs={{0,128},{1,9},{2,130},{3,11},{4,132},{5,13},{6,134},{7,15},{8,136}... | collective-permute-start | bytes 2359304 | tf_op jit(solution)/shard_map/ppermute | solution.py:47
  61.6 9.1 %collective-permute-done.10 = bf16[256,1536]{1,0:T(8,128)(2,1)S(1)} collective-permute-done((bf16[256,1536]{1,0:T(8,128)(2,1)S(1)}, bf16[256,1536]{1,0:T(8,128)(2,1)S(1)}, u32[]{:S(2)}, u32[]{:S(2)}) %collective-permute-start.10) | collective-permute-done | bytes 786464 | tf_op jit(solution)/shard_map/ppermute | solution.py:47
  70.7 9.0 %collective-permute-done.11 = bf16[256,1536]{1,0:T(8,128)(2,1)S(1)} collective-permute-done((bf16[256,1536]{1,0:T(8,128)(2,1)S(1)}, bf16[256,1536]{1,0:T(8,128)(2,1)S(1)}, u32[]{:S(2)}, u32[]{:S(2)}) %collective-permute-start.11) | collective-permute-done | bytes 786464 | tf_op jit(solution)/shard_map/ppermute | solution.py:47
  80.2 1.7 %collective-permute-start.12 = (bf16[64,1536]{1,0:T(8,128)(2,1)S(1)}, bf16[64,1536]{1,0:T(8,128)(2,1)S(1)}, u32[]{:S(2)}, u32[]{:S(2)}) collective-permute-start(bf16[64,1536]{1,0:T(8,128)(2,1)S(1)} %get-tuple-element.16), channel_id=1, source_target_pairs={{0,12},{1,193},{2,14},{3,195},{4,0},{5,197},{6,2},{7,199},{8,4},{9... | collective-permute-start | bytes 589832 | tf_op jit(solution)/shard_map/ppermute | solution.py:47
  81.9 1.5 %collective-permute-start.14 = (bf16[64,1536]{1,0:T(8,128)(2,1)S(1)}, bf16[64,1536]{1,0:T(8,128)(2,1)S(1)}, u32[]{:S(2)}, u32[]{:S(2)}) collective-permute-start(bf16[64,1536]{1,0:T(8,128)(2,1)S(1)} %get-tuple-element.17), channel_id=1, source_target_pairs={{0,8},{1,129},{2,10},{3,131},{4,12},{5,133},{6,14},{7,135},{8,0},{... | collective-permute-start | bytes 589832 | tf_op jit(solution)/shard_map/ppermute | solution.py:47
  83.3 3.1 %collective-permute-done.12 = bf16[64,1536]{1,0:T(8,128)(2,1)S(1)} collective-permute-done((bf16[64,1536]{1,0:T(8,128)(2,1)S(1)}, bf16[64,1536]{1,0:T(8,128)(2,1)S(1)}, u32[]{:S(2)}, u32[]{:S(2)}) %collective-permute-start.12) | collective-permute-done | bytes 196640 | tf_op jit(solution)/shard_map/ppermute | solution.py:47
  86.4 3.3 %collective-permute-done.13 = bf16[64,1536]{1,0:T(8,128)(2,1)S(1)} collective-permute-done((bf16[64,1536]{1,0:T(8,128)(2,1)S(1)}, bf16[64,1536]{1,0:T(8,128)(2,1)S(1)}, u32[]{:S(2)}, u32[]{:S(2)}) %collective-permute-start.13) | collective-permute-done | bytes 196640 | tf_op jit(solution)/shard_map/ppermute | solution.py:47
  89.8 3.4 %collective-permute-start.15 = (bf16[16,1536]{1,0:T(8,128)(2,1)S(1)}, bf16[16,1536]{1,0:T(8,128)(2,1)S(1)}, u32[]{:S(2)}, u32[]{:S(2)}) collective-permute-start(bf16[16,1536]{1,0:T(8,128)(2,1)S(1)} %get-tuple-element.21), channel_id=1, source_target_pairs={{0,48},{1,49},{2,50},{3,51},{4,52},{5,53},{6,54},{7,55},{8,56},{9,... | collective-permute-start | bytes 147464 | tf_op jit(solution)/shard_map/ppermute | solution.py:47
  94.4 3.6 %collective-permute-done.16.b_ref = bf16[16,1536]{1,0:T(8,128)(2,1)S(1)} collective-permute-done((bf16[16,1536]{1,0:T(8,128)(2,1)S(1)}, bf16[16,1536]{1,0:T(8,128)(2,1)S(1)}, u32[]{:S(2)}, u32[]{:S(2)}) %collective-permute-start.16) | collective-permute-done | bytes 49184 | tf_op jit(solution)/shard_map/ppermute | solution.py:47
  98.0 2.3 %copy-done = bf16[3072,768]{1,0:T(8,128)(2,1)S(1)} copy-done((bf16[3072,768]{1,0:T(8,128)(2,1)S(1)}, bf16[3072,768]{1,0:T(8,128)(2,1)}, u32[]{:S(2)}) %copy-start) | copy-done | bytes 4718616
  100.3 2.3 %copy-done.1 = bf16[3072,768]{1,0:T(8,128)(2,1)S(1)} copy-done((bf16[3072,768]{1,0:T(8,128)(2,1)S(1)}, bf16[3072,768]{1,0:T(8,128)(2,1)}, u32[]{:S(2)}) %copy-start.1) | copy-done | bytes 4718616
  102.7 3.4 %project_rows.1 = bf16[16,3072]{1,0:T(8,128)(2,1)S(1)} custom-call(f32[16,1536]{1,0:T(8,128)S(1)} %split.42.own_ref, bf16[16,1536]{1,0:T(8,128)(2,1)S(1)} %collective-permute-done.15.a_ref, bf16[16,1536]{1,0:T(8,128)(2,1)S(1)} %collective-permute-done.16.b_ref, bf16[16,1536]{1,0:T(8,128)(2,1)S(1)} %collective-permute-done.17.c_ref, ...), custom_call_target="tpu_custom_call" | custom-call | tf_op jit(solution)/shard_map/project_rows/pallas_call | solution.py:143
  106.1 7.5 %collective-permute-start.18 = (bf16[16,768]{1,0:T(8,128)(2,1)S(1)}, bf16[16,768]{1,0:T(8,128)(2,1)S(1)}, u32[]{:S(2)}, u32[]{:S(2)}) collective-permute-start(bf16[16,768]{1,0:T(8,128)(2,1)S(1)} %get-tuple-element.22), channel_id=1, source_target_pairs={{0,1},{1,0},{2,3},{3,2},{4,5},{5,4},{6,7},{7,6},{8,9},{9,8},{10,11... | collective-permute-start | bytes 73736 | tf_op jit(solution)/shard_map/ppermute | solution.py:52
  113.7 8.0 %collective-permute-start.19 = (bf16[16,768]{1,0:T(8,128)(2,1)S(1)}, bf16[16,768]{1,0:T(8,128)(2,1)S(1)}, u32[]{:S(2)}, u32[]{:S(2)}) collective-permute-start(bf16[16,768]{1,0:T(8,128)(2,1)S(1)} %get-tuple-element.24), channel_id=1, source_target_pairs={{0,2},{1,3},{2,0},{3,1},{4,6},{5,7},{6,4},{7,5},{8,10},{9,11},{10,... | collective-permute-start | bytes 73736 | tf_op jit(solution)/shard_map/ppermute | solution.py:52
  121.7 1.1 collective-permute-done.19
  122.9 6.0 %collective-permute-done.20 = bf16[16,768]{1,0:T(8,128)(2,1)S(1)} collective-permute-done((bf16[16,768]{1,0:T(8,128)(2,1)S(1)}, bf16[16,768]{1,0:T(8,128)(2,1)S(1)}, u32[]{:S(2)}, u32[]{:S(2)}) %collective-permute-start.20) | collective-permute-done | bytes 24608 | tf_op jit(solution)/shard_map/ppermute | solution.py:52
  (36 shorter events, 5.4 us)
Async XLA Ops:
  0.6 42.2 %copy-start.2 = (bf16[512,768]{1,0:T(8,128)(2,1)S(1)}, bf16[512,768]{1,0:T(8,128)(2,1)}, u32[]{:S(2)}) copy-start(bf16[512,768]{1,0:T(8,128)(2,1)} %q_ref.1) | copy-start | bytes 2359300
  0.6 42.2 %copy-start.3 = (bf16[512,768]{1,0:T(8,128)(2,1)S(1)}, bf16[512,768]{1,0:T(8,128)(2,1)}, u32[]{:S(2)}) copy-start(bf16[512,768]{1,0:T(8,128)(2,1)} %g_ref.1) | copy-start | bytes 2359300
  2.2 6.7 %collective-permute-start = (bf16[16,1536]{1,0:T(8,128)(2,1)S(1)}, bf16[16,1536]{1,0:T(8,128)(2,1)S(1)}, u32[]{:S(2)}, u32[]{:S(2)}) collective-permute-start(bf16[16,1536]{1,0:T(8,128)(2,1)S(1)} %get-tuple-element.25), channel_id=1, source_target_pairs={{0,16},{1,17},{2,18},{3,19},{4,20},{5,21},{6,22},{7,23},{8,24},{9,... | collective-permute-start | bytes 147464 | tf_op jit(solution)/shard_map/ppermute | solution.py:47
  4.7 4.2 %collective-permute-start.1 = (bf16[16,1536]{1,0:T(8,128)(2,1)S(1)}, bf16[16,1536]{1,0:T(8,128)(2,1)S(1)}, u32[]{:S(2)}, u32[]{:S(2)}) collective-permute-start(bf16[16,1536]{1,0:T(8,128)(2,1)S(1)} %get-tuple-element.25), channel_id=1, source_target_pairs={{0,48},{1,49},{2,50},{3,51},{4,52},{5,53},{6,54},{7,55},{8,56},{9,... | collective-permute-start | bytes 147464 | tf_op jit(solution)/shard_map/ppermute | solution.py:47
  7.4 5.1 %collective-permute-start.2 = (bf16[16,1536]{1,0:T(8,128)(2,1)S(1)}, bf16[16,1536]{1,0:T(8,128)(2,1)S(1)}, u32[]{:S(2)}, u32[]{:S(2)}) collective-permute-start(bf16[16,1536]{1,0:T(8,128)(2,1)S(1)} %get-tuple-element.25), channel_id=1, source_target_pairs={{0,32},{1,33},{2,34},{3,35},{4,36},{5,37},{6,38},{7,39},{8,40},{9,... | collective-permute-start | bytes 147464 | tf_op jit(solution)/shard_map/ppermute | solution.py:47
  12.6 5.8 %collective-permute-start.3 = (bf16[64,1536]{1,0:T(8,128)(2,1)S(1)}, bf16[64,1536]{1,0:T(8,128)(2,1)S(1)}, u32[]{:S(2)}, u32[]{:S(2)}) collective-permute-start(bf16[64,1536]{1,0:T(8,128)(2,1)S(1)} %pad_maximum_fusion), channel_id=1, source_target_pairs={{0,4},{1,65},{2,6},{3,67},{4,8},{5,69},{6,10},{7,71},{8,12},{9,73}... | collective-permute-start | bytes 589832 | tf_op jit(solution)/shard_map/ppermute | solution.py:47
  12.9 7.1 %collective-permute-start.4 = (bf16[64,1536]{1,0:T(8,128)(2,1)S(1)}, bf16[64,1536]{1,0:T(8,128)(2,1)S(1)}, u32[]{:S(2)}, u32[]{:S(2)}) collective-permute-start(bf16[64,1536]{1,0:T(8,128)(2,1)S(1)} %pad_maximum_fusion), channel_id=1, source_target_pairs={{0,12},{1,193},{2,14},{3,195},{4,0},{5,197},{6,2},{7,199},{8,4},{9... | collective-permute-start | bytes 589832 | tf_op jit(solution)/shard_map/ppermute | solution.py:47
  15.3 6.0 %collective-permute-start.5 = (bf16[64,1536]{1,0:T(8,128)(2,1)S(1)}, bf16[64,1536]{1,0:T(8,128)(2,1)S(1)}, u32[]{:S(2)}, u32[]{:S(2)}) collective-permute-start(bf16[64,1536]{1,0:T(8,128)(2,1)S(1)} %pad_maximum_fusion), channel_id=1, source_target_pairs={{0,8},{1,129},{2,10},{3,131},{4,12},{5,133},{6,14},{7,135},{8,0},{... | collective-permute-start | bytes 589832 | tf_op jit(solution)/shard_map/ppermute | solution.py:47
  21.3 12.4 %collective-permute-start.6 = (bf16[256,1536]{1,0:T(8,128)(2,1)S(1)}, bf16[256,1536]{1,0:T(8,128)(2,1)S(1)}, u32[]{:S(2)}, u32[]{:S(2)}) collective-permute-start(bf16[256,1536]{1,0:T(8,128)(2,1)S(1)} %constant_dynamic-update-slice_fusion.2.refs_0_.refs_4_), channel_id=1, source_target_pairs={{0,64},{1,5},{2,66},{3,7},{4,68},{5,9},{6,70},{7,11},{8,72},{9,13}... | collective-permute-start | bytes 2359304 | tf_op jit(solution)/shard_map/ppermute | solution.py:47
  22.0 19.4 %collective-permute-start.7 = (bf16[256,1536]{1,0:T(8,128)(2,1)S(1)}, bf16[256,1536]{1,0:T(8,128)(2,1)S(1)}, u32[]{:S(2)}, u32[]{:S(2)}) collective-permute-start(bf16[256,1536]{1,0:T(8,128)(2,1)S(1)} %constant_dynamic-update-slice_fusion.2.refs_0_.refs_4_), channel_id=1, source_target_pairs={{0,192},{1,13},{2,194},{3,15},{4,196},{5,1},{6,198},{7,3},{8,200},... | collective-permute-start | bytes 2359304 | tf_op jit(solution)/shard_map/ppermute | solution.py:47
  24.1 18.8 %collective-permute-start.8 = (bf16[256,1536]{1,0:T(8,128)(2,1)S(1)}, bf16[256,1536]{1,0:T(8,128)(2,1)S(1)}, u32[]{:S(2)}, u32[]{:S(2)}) collective-permute-start(bf16[256,1536]{1,0:T(8,128)(2,1)S(1)} %constant_dynamic-update-slice_fusion.2.refs_0_.refs_4_), channel_id=1, source_target_pairs={{0,128},{1,9},{2,130},{3,11},{4,132},{5,13},{6,134},{7,15},{8,136}... | collective-permute-start | bytes 2359304 | tf_op jit(solution)/shard_map/ppermute | solution.py:47
  58.3 12.3 %collective-permute-start.10 = (bf16[256,1536]{1,0:T(8,128)(2,1)S(1)}, bf16[256,1536]{1,0:T(8,128)(2,1)S(1)}, u32[]{:S(2)}, u32[]{:S(2)}) collective-permute-start(bf16[256,1536]{1,0:T(8,128)(2,1)S(1)} %get-tuple-element.10), channel_id=1, source_target_pairs={{0,64},{1,5},{2,66},{3,7},{4,68},{5,9},{6,70},{7,11},{8,72},{9,13}... | collective-permute-start | bytes 2359304 | tf_op jit(solution)/shard_map/ppermute | solution.py:47
  59.2 20.5 %collective-permute-start.11 = (bf16[256,1536]{1,0:T(8,128)(2,1)S(1)}, bf16[256,1536]{1,0:T(8,128)(2,1)S(1)}, u32[]{:S(2)}, u32[]{:S(2)}) collective-permute-start(bf16[256,1536]{1,0:T(8,128)(2,1)S(1)} %get-tuple-element.11), channel_id=1, source_target_pairs={{0,128},{1,9},{2,130},{3,11},{4,132},{5,13},{6,134},{7,15},{8,136}... | collective-permute-start | bytes 2359304 | tf_op jit(solution)/shard_map/ppermute | solution.py:47
  61.6 18.2 %collective-permute-start.9 = (bf16[256,1536]{1,0:T(8,128)(2,1)S(1)}, bf16[256,1536]{1,0:T(8,128)(2,1)S(1)}, u32[]{:S(2)}, u32[]{:S(2)}) collective-permute-start(bf16[256,1536]{1,0:T(8,128)(2,1)S(1)} %get-tuple-element.9), channel_id=1, source_target_pairs={{0,192},{1,13},{2,194},{3,15},{4,196},{5,1},{6,198},{7,3},{8,200},... | collective-permute-start | bytes 2359304 | tf_op jit(solution)/shard_map/ppermute | solution.py:47
  80.2 6.2 %collective-permute-start.12 = (bf16[64,1536]{1,0:T(8,128)(2,1)S(1)}, bf16[64,1536]{1,0:T(8,128)(2,1)S(1)}, u32[]{:S(2)}, u32[]{:S(2)}) collective-permute-start(bf16[64,1536]{1,0:T(8,128)(2,1)S(1)} %get-tuple-element.16), channel_id=1, source_target_pairs={{0,12},{1,193},{2,14},{3,195},{4,0},{5,197},{6,2},{7,199},{8,4},{9... | collective-permute-start | bytes 589832 | tf_op jit(solution)/shard_map/ppermute | solution.py:47
  81.9 7.8 %collective-permute-start.13 = (bf16[64,1536]{1,0:T(8,128)(2,1)S(1)}, bf16[64,1536]{1,0:T(8,128)(2,1)S(1)}, u32[]{:S(2)}, u32[]{:S(2)}) collective-permute-start(bf16[64,1536]{1,0:T(8,128)(2,1)S(1)} %get-tuple-element.18), channel_id=1, source_target_pairs={{0,4},{1,65},{2,6},{3,67},{4,8},{5,69},{6,10},{7,71},{8,12},{9,73}... | collective-permute-start | bytes 589832 | tf_op jit(solution)/shard_map/ppermute | solution.py:47
  81.9 7.8 %collective-permute-start.14 = (bf16[64,1536]{1,0:T(8,128)(2,1)S(1)}, bf16[64,1536]{1,0:T(8,128)(2,1)S(1)}, u32[]{:S(2)}, u32[]{:S(2)}) collective-permute-start(bf16[64,1536]{1,0:T(8,128)(2,1)S(1)} %get-tuple-element.17), channel_id=1, source_target_pairs={{0,8},{1,129},{2,10},{3,131},{4,12},{5,133},{6,14},{7,135},{8,0},{... | collective-permute-start | bytes 589832 | tf_op jit(solution)/shard_map/ppermute | solution.py:47
  89.8 4.6 %collective-permute-start.15 = (bf16[16,1536]{1,0:T(8,128)(2,1)S(1)}, bf16[16,1536]{1,0:T(8,128)(2,1)S(1)}, u32[]{:S(2)}, u32[]{:S(2)}) collective-permute-start(bf16[16,1536]{1,0:T(8,128)(2,1)S(1)} %get-tuple-element.21), channel_id=1, source_target_pairs={{0,48},{1,49},{2,50},{3,51},{4,52},{5,53},{6,54},{7,55},{8,56},{9,... | collective-permute-start | bytes 147464 | tf_op jit(solution)/shard_map/ppermute | solution.py:47
  93.2 4.7 %collective-permute-start.16 = (bf16[16,1536]{1,0:T(8,128)(2,1)S(1)}, bf16[16,1536]{1,0:T(8,128)(2,1)S(1)}, u32[]{:S(2)}, u32[]{:S(2)}) collective-permute-start(bf16[16,1536]{1,0:T(8,128)(2,1)S(1)} %get-tuple-element.20), channel_id=1, source_target_pairs={{0,16},{1,17},{2,18},{3,19},{4,20},{5,21},{6,22},{7,23},{8,24},{9,... | collective-permute-start | bytes 147464 | tf_op jit(solution)/shard_map/ppermute | solution.py:47
  93.2 4.7 %collective-permute-start.17 = (bf16[16,1536]{1,0:T(8,128)(2,1)S(1)}, bf16[16,1536]{1,0:T(8,128)(2,1)S(1)}, u32[]{:S(2)}, u32[]{:S(2)}) collective-permute-start(bf16[16,1536]{1,0:T(8,128)(2,1)S(1)} %get-tuple-element.19), channel_id=1, source_target_pairs={{0,32},{1,33},{2,34},{3,35},{4,36},{5,37},{6,38},{7,39},{8,40},{9,... | collective-permute-start | bytes 147464 | tf_op jit(solution)/shard_map/ppermute | solution.py:47
  98.0 2.3 %copy-start = (bf16[3072,768]{1,0:T(8,128)(2,1)S(1)}, bf16[3072,768]{1,0:T(8,128)(2,1)}, u32[]{:S(2)}) copy-start(bf16[3072,768]{1,0:T(8,128)(2,1)} %key_ref.1) | copy-start | bytes 14155780
  100.3 2.3 %copy-start.1 = (bf16[3072,768]{1,0:T(8,128)(2,1)S(1)}, bf16[3072,768]{1,0:T(8,128)(2,1)}, u32[]{:S(2)}) copy-start(bf16[3072,768]{1,0:T(8,128)(2,1)} %value_ref.1) | copy-start | bytes 14155780
  106.1 15.6 %collective-permute-start.18 = (bf16[16,768]{1,0:T(8,128)(2,1)S(1)}, bf16[16,768]{1,0:T(8,128)(2,1)S(1)}, u32[]{:S(2)}, u32[]{:S(2)}) collective-permute-start(bf16[16,768]{1,0:T(8,128)(2,1)S(1)} %get-tuple-element.22), channel_id=1, source_target_pairs={{0,1},{1,0},{2,3},{3,2},{4,5},{5,4},{6,7},{7,6},{8,9},{9,8},{10,11... | collective-permute-start | bytes 73736 | tf_op jit(solution)/shard_map/ppermute | solution.py:52
  113.7 9.2 %collective-permute-start.19 = (bf16[16,768]{1,0:T(8,128)(2,1)S(1)}, bf16[16,768]{1,0:T(8,128)(2,1)S(1)}, u32[]{:S(2)}, u32[]{:S(2)}) collective-permute-start(bf16[16,768]{1,0:T(8,128)(2,1)S(1)} %get-tuple-element.24), channel_id=1, source_target_pairs={{0,2},{1,3},{2,0},{3,1},{4,6},{5,7},{6,4},{7,5},{8,10},{9,11},{10,... | collective-permute-start | bytes 73736 | tf_op jit(solution)/shard_map/ppermute | solution.py:52
  121.7 7.2 %collective-permute-start.20 = (bf16[16,768]{1,0:T(8,128)(2,1)S(1)}, bf16[16,768]{1,0:T(8,128)(2,1)S(1)}, u32[]{:S(2)}, u32[]{:S(2)}) collective-permute-start(bf16[16,768]{1,0:T(8,128)(2,1)S(1)} %get-tuple-element.23), channel_id=1, source_target_pairs={{0,3},{1,2},{2,1},{3,0},{4,7},{5,6},{6,5},{7,4},{8,11},{9,10},{10,... | collective-permute-start | bytes 73736 | tf_op jit(solution)/shard_map/ppermute | solution.py:52

commit v2 on v1

--- a/solution.py
+++ b/solution.py
@@ -66,8 +66,8 @@
 
 def attention_kernel(chunk, q_ref, g_ref, *refs):
     keys, values = refs[0:SIDE], refs[SIDE : 2 * SIDE]
-    dq_ref, parts = refs[2 * SIDE], refs[2 * SIDE + 1 : 3 * SIDE + 1]
-    probs_ref, grads_ref = refs[3 * SIDE + 1 :]
+    *_, probs_ref, grads_ref = refs
+    dq_ref, parts = refs[-SIDE - 3], refs[-SIDE - 2 : -2]
     rows = keys[0].shape[0]
     tokens = q_ref.shape[0]
     for at in range(0, tokens, chunk):
@@ -99,25 +99,39 @@
     dq_ref[...] = (dq.T * SCALE).astype(jnp.bfloat16)
 
 
-def attention(queries, grad_out, blocks):
+def attention(queries, grad_out, blocks, first, grad_queries=None):
     tokens, width = queries.shape
-    heads = width // HD
-    rows = blocks[0].shape[0]
-    token_spec = pl.BlockSpec((tokens, HD), lambda h: (0, h))
+    rows, columns = blocks[0].shape
+    heads = columns // (2 * HD)
+    token_spec = pl.BlockSpec((tokens, HD), lambda h: (0, first + h))
     key_spec = pl.BlockSpec((rows, HD), lambda h: (0, h))
     value_spec = pl.BlockSpec((rows, HD), lambda h: (0, heads + h))
     part_spec = pl.BlockSpec((rows, 2 * HD), lambda h: (0, h))
+    operands = [queries, grad_out, *blocks, *blocks]
+    in_specs = [token_spec] * 2 + [key_spec] * SIDE + [value_spec] * SIDE
+    aliases = {}
+    if grad_queries is not None:
+        aliases = {len(operands): 0}
+        operands.append(grad_queries)
+        in_specs.append(pl.BlockSpec(memory_space=pl.ANY))
+    scores = heads * tokens * SIDE * rows
     return pl.pallas_call(
         functools.partial(attention_kernel, tokens // 2),
         grid=(heads,),
-        in_specs=[token_spec] * 2 + [key_spec] * SIDE + [value_spec] * SIDE,
+        in_specs=in_specs,
         out_specs=[token_spec] + [part_spec] * SIDE,
         out_shape=[jax.ShapeDtypeStruct(queries.shape, jnp.bfloat16)]
-        + [jax.ShapeDtypeStruct((rows, 2 * width), jnp.bfloat16)] * SIDE,
+        + [jax.ShapeDtypeStruct((rows, columns), jnp.bfloat16)] * SIDE,
         scratch_shapes=[pltpu.VMEM((SIDE * rows, tokens), jnp.bfloat16)] * 2,
-        compiler_params=pltpu.CompilerParams(vmem_limit_bytes=32 * 2**20),
+        input_output_aliases=aliases,
+        compiler_params=pltpu.CompilerParams(vmem_limit_bytes=24 * 2**20),
+        cost_estimate=pl.CostEstimate(
+            flops=10 * HD * scores,
+            bytes_accessed=2 * (3 * tokens * heads * HD + 2 * SIDE * rows * columns),
+            transcendentals=scores,
+        ),
         name="attention_grads",
-    )(queries, grad_out, *blocks, *blocks)
+    )(*operands)
 
 
 def project_kernel(own_ref, a_ref, b_ref, c_ref, key_ref, value_ref, out_ref):
@@ -146,38 +160,60 @@
         in_specs=[sum_spec] * 4 + [weight_spec] * 2,
         out_specs=pl.BlockSpec((rows, block), lambda n: (0, n)),
         out_shape=jax.ShapeDtypeStruct((rows, features), jnp.bfloat16),
-        compiler_params=pltpu.CompilerParams(vmem_limit_bytes=16 * 2**20),
+        compiler_params=pltpu.CompilerParams(vmem_limit_bytes=52 * 2**20),
         name="project_rows",
     )(own, *received, key_weight, value_weight)
 
 
 def shards(queries, ref_keys, ref_values, grad_out, key_weight, value_weight):
-    rows = jnp.concatenate([ref_keys, ref_values], axis=1)
+    groups = 2
+    heads = queries.shape[1] // HD // groups
+    width = heads * HD
+    cuts = [slice(i * width, (i + 1) * width) for i in range(groups)]
+    rows = jnp.concatenate([a[:, c] for c in cuts for a in (ref_keys, ref_values)], axis=1)
     rows = jnp.concatenate(gather(rows, ("z", "z")), axis=0)
-    rows = jnp.concatenate(gather(rows, ("x", "y")), axis=0)
-    blocks = gather(rows, ("y", "x"))
-
-    grad_queries, *parts = attention(queries, grad_out, blocks)
-
-    total = parts[0].astype(jnp.float32)
-    received = scatter(parts, ("y", "x"))
+    pieces = gather(rows, ("x", "y"))
+    rows = [
+        jnp.concatenate([p[:, 2 * c.start : 2 * c.stop] for p in pieces], axis=0) for c in cuts
+    ]
+    blocks = [gather(r, ("y", "x")) for r in rows]
+
+    grad_queries, totals = None, []
+    for i in range(groups):
+        grad_queries, *parts = attention(queries, grad_out, blocks[i], i * heads, grad_queries)
+        total = parts[0].astype(jnp.float32)
+        for r in scatter(parts, ("y", "x")):
+            total += r.astype(jnp.float32)
+        totals.append(total)
+    total = jnp.concatenate(totals, axis=1)
     for axes in (("x", "y"), ("z", "z")):
+        cut = jnp.split(total, SIDE, axis=0)
+        received = scatter([c.astype(jnp.bfloat16) for c in cut], axes)
+        if axes == ("z", "z"):
+            break
+        total = cut[0]
         for r in received:
             total += r.astype(jnp.float32)
-        cut = jnp.split(total, SIDE, axis=0)
-        total = cut[0]
-        received = scatter([c.astype(jnp.bfloat16) for c in cut], axes)
-    result = project(total, received, key_weight, value_weight)
-
+    result = project(cut[0], received, key_weight, value_weight)
+
+    me = lax.axis_index("tensor")
+    half, core = me // CORES, me % CORES
     columns = result.shape[1] // TENSOR
-    me = lax.axis_index("tensor")
-
-    def block_of(flip):
-        return lax.dynamic_slice_in_dim(result, (me ^ flip) * columns, columns, axis=1)
-
-    grad_rows = block_of(0).astype(jnp.float32)
-    for r in [flip_send(block_of(flip), flip) for flip in (1, 2, 3)]:
-        grad_rows += r.astype(jnp.float32)
+
+    def blocks_of(array, index):
+        return jnp.concatenate(
+            [
+                lax.dynamic_slice_in_dim(array, (h * CORES + index) * columns, columns, axis=1)
+                for h in range(TENSOR // CORES)
+            ],
+            axis=1,
+        )
+
+    pair = flip_send(blocks_of(result, 1 - core), 1).astype(jnp.float32)
+    pair += blocks_of(result, core).astype(jnp.float32)
+    away = lax.dynamic_slice_in_dim(pair, (1 - half) * columns, columns, axis=1)
+    here = lax.dynamic_slice_in_dim(pair, half * columns, columns, axis=1)
+    grad_rows = here + flip_send(away.astype(jnp.bfloat16), CORES).astype(jnp.float32)
     return grad_queries, grad_rows.astype(jnp.bfloat16)
 
 

time: 130 us -> 112 us (0.86)
  waiting for transfers between devices: 63.9 us -> 42.6 us
  local copies, waits for them, and re-layouts: 6.42 us -> 0.94 us
  starting transfers between devices: 38.4 us -> 43.3 us
  Pallas kernels: 18.9 us -> 22.7 us
    ppermute x18 -> x24, waiting for transfers between devices: 56.8 us -> 40.5 us  [ring_send(): return lax.ppermute(block, BOTH, ring_pairs(axes, step))]
    unnamed x14 -> x4, local copies, waits for them, and re-layouts: 5.58 us -> 0.01 us
    ppermute x3 -> x2, waiting for transfers between devices: 7.09 us -> 2.1 us  [flip_send(): return lax.ppermute(block, BOTH, pairs)]
    ppermute x18 -> x24, starting transfers between devices: 22.8 us -> 27.6 us  [ring_send(): return lax.ppermute(block, BOTH, ring_pairs(axes, step))]
    pallas_call x1, Pallas kernels: 3.44 us -> 6.61 us  [project(): pl.pallas_call(project_kernel, grid=(features // block,), in_specs=[sum_s...]
    pallas_call x1 -> x2, Pallas kernels: 15.5 us -> 16.1 us  [attention(): pl.pallas_call(functools.partial(attention_kernel, tokens // 2), grid=(he...]
    ppermute x3 -> x2, starting transfers between devices: 15.6 us -> 15.7 us  [flip_send(): return lax.ppermute(block, BOTH, pairs)]
  transfers between devices with their start and end apart: 21 -> 26, of which waited for: 17 -> 15; matrix products, arithmetic and copies ran while one was open for 0% -> 0% of each run, Pallas kernels for 0% -> 14%
where the time goes in v2:
time: 112 us
  starting transfers between devices  43.3 us (39%)
  waiting for transfers between devices  42.6 us (38%)
  Pallas kernels  22.7 us (20%)
  other arithmetic  1.25 us (1%)
    ppermute x24, waiting for transfers between devices, ring_send(): return lax.ppermute(block, BOTH, ring_pairs(axes, step))  40.5 us
    ppermute x24, starting transfers between devices, ring_send(): return lax.ppermute(block, BOTH, ring_pairs(axes, step))  27.6 us
    pallas_call x2, Pallas kernels, attention(): pl.pallas_call(functools.partial(attention_kernel, tokens // 2), grid=(he...  16.1 us
    ppermute x2, starting transfers between devices, flip_send(): return lax.ppermute(block, BOTH, pairs)  15.7 us
    pallas_call x1, Pallas kernels, project(): pl.pallas_call(project_kernel, grid=(features // block,), in_specs=[sum_s...  6.61 us
  transfers between devices with their start and end apart: 26, of which 15 were waited for; matrix products, arithmetic and copies ran while one was open for 0% of the time, Pallas kernels for 14%

profile of v2, /device:TPU:1, one launch (start us, length us, event | category | flops | bytes accessed | tf_op | source)
XLA Modules:
  0.0 111.6 jit_solution(1819960228795937396)
XLA Ops:
  1.4 2.5 %collective-permute-start = (bf16[16,1536]{1,0:T(8,128)(2,1)S(1)}, bf16[16,1536]{1,0:T(8,128)(2,1)S(1)}, u32[]{:S(2)}, u32[]{:S(2)}) collective-permute-start(bf16[16,1536]{1,0:T(8,128)(2,1)S(1)} %pad_maximum_fusion.4), channel_id=1, source_target_pairs={{0,16},{1,17},{2,18},{3,19},{4,20},{5,21},{6,22},{7,23},{8,24},{9,... | collective-permute-start | bytes 147464 | tf_op jit(solution)/shard_map/ppermute | solution.py:47
  3.9 2.8 %collective-permute-start.1 = (bf16[16,1536]{1,0:T(8,128)(2,1)S(1)}, bf16[16,1536]{1,0:T(8,128)(2,1)S(1)}, u32[]{:S(2)}, u32[]{:S(2)}) collective-permute-start(bf16[16,1536]{1,0:T(8,128)(2,1)S(1)} %pad_maximum_fusion.4), channel_id=1, source_target_pairs={{0,48},{1,49},{2,50},{3,51},{4,52},{5,53},{6,54},{7,55},{8,56},{9,... | collective-permute-start | bytes 147464 | tf_op jit(solution)/shard_map/ppermute | solution.py:47
  6.9 1.2 %collective-permute-done = bf16[16,1536]{1,0:T(8,128)(2,1)S(1)} collective-permute-done((bf16[16,1536]{1,0:T(8,128)(2,1)S(1)}, bf16[16,1536]{1,0:T(8,128)(2,1)S(1)}, u32[]{:S(2)}, u32[]{:S(2)}) %collective-permute-start) | collective-permute-done | bytes 49184 | tf_op jit(solution)/shard_map/ppermute | solution.py:47
  8.2 3.6 %collective-permute-done.2 = bf16[16,1536]{1,0:T(8,128)(2,1)S(1)} collective-permute-done((bf16[16,1536]{1,0:T(8,128)(2,1)S(1)}, bf16[16,1536]{1,0:T(8,128)(2,1)S(1)}, u32[]{:S(2)}, u32[]{:S(2)}) %collective-permute-start.2) | collective-permute-done | bytes 49184 | tf_op jit(solution)/shard_map/ppermute | solution.py:47
  12.2 2.4 %collective-permute-start.4 = (bf16[64,1536]{1,0:T(8,128)(2,1)S(1)}, bf16[64,1536]{1,0:T(8,128)(2,1)S(1)}, u32[]{:S(2)}, u32[]{:S(2)}) collective-permute-start(bf16[64,1536]{1,0:T(8,128)(2,1)S(1)} %pad_maximum_fusion.3), channel_id=1, source_target_pairs={{0,12},{1,193},{2,14},{3,195},{4,0},{5,197},{6,2},{7,199},{8,4},{9... | collective-permute-start | bytes 589832 | tf_op jit(solution)/shard_map/ppermute | solution.py:47
  15.3 2.3 %collective-permute-done.3 = bf16[64,1536]{1,0:T(8,128)(2,1)S(1)} collective-permute-done((bf16[64,1536]{1,0:T(8,128)(2,1)S(1)}, bf16[64,1536]{1,0:T(8,128)(2,1)S(1)}, u32[]{:S(2)}, u32[]{:S(2)}) %collective-permute-start.3) | collective-permute-done | bytes 196640 | tf_op jit(solution)/shard_map/ppermute | solution.py:47
  17.6 1.6 %collective-permute-done.4 = bf16[64,1536]{1,0:T(8,128)(2,1)S(1)} collective-permute-done((bf16[64,1536]{1,0:T(8,128)(2,1)S(1)}, bf16[64,1536]{1,0:T(8,128)(2,1)S(1)}, u32[]{:S(2)}, u32[]{:S(2)}) %collective-permute-start.4) | collective-permute-done | bytes 196640 | tf_op jit(solution)/shard_map/ppermute | solution.py:47
  19.3 1.3 %collective-permute-done.5 = bf16[64,1536]{1,0:T(8,128)(2,1)S(1)} collective-permute-done((bf16[64,1536]{1,0:T(8,128)(2,1)S(1)}, bf16[64,1536]{1,0:T(8,128)(2,1)S(1)}, u32[]{:S(2)}, u32[]{:S(2)}) %collective-permute-start.5) | collective-permute-done | bytes 196640 | tf_op jit(solution)/shard_map/ppermute | solution.py:47
  20.6 2.2 %collective-permute-start.10 = (bf16[256,768]{1,0:T(8,128)(2,1)S(1)}, bf16[256,768]{1,0:T(8,128)(2,1)S(1)}, u32[]{:S(2)}, u32[]{:S(2)}) collective-permute-start(bf16[256,768]{1,0:T(8,128)(2,1)S(1)} %pad_maximum_fusion.2.refs_0_.refs_4_), channel_id=1, source_target_pairs={{0,192},{1,13},{2,194},{3,15},{4,196},{5,1},{6,198},{7,3},{8,200},... | collective-permute-start | bytes 1179656 | tf_op jit(solution)/shard_map/ppermute | solution.py:47
  23.7 1.9 %collective-permute-start.6 = (bf16[256,768]{1,0:T(8,128)(2,1)S(1)}, bf16[256,768]{1,0:T(8,128)(2,1)S(1)}, u32[]{:S(2)}, u32[]{:S(2)}) collective-permute-start(bf16[256,768]{1,0:T(8,128)(2,1)S(1)} %pad_maximum_fusion.1.refs_0_.refs_4_), channel_id=1, source_target_pairs={{0,64},{1,5},{2,66},{3,7},{4,68},{5,9},{6,70},{7,11},{8,72},{9,13}... | collective-permute-start | bytes 1179656 | tf_op jit(solution)/shard_map/ppermute | solution.py:47
  25.6 0.9 collective-permute-start.7
  26.5 5.3 %collective-permute-done.10.refs_2_.refs_6_ = bf16[256,768]{1,0:T(8,128)(2,1)S(1)} collective-permute-done((bf16[256,768]{1,0:T(8,128)(2,1)S(1)}, bf16[256,768]{1,0:T(8,128)(2,1)S(1)}, u32[]{:S(2)}, u32[]{:S(2)}) %collective-permute-start.10) | collective-permute-done | bytes 393248 | tf_op jit(solution)/shard_map/ppermute | solution.py:47
  31.8 3.6 %collective-permute-done.9.refs_1_.refs_5_ = bf16[256,768]{1,0:T(8,128)(2,1)S(1)} collective-permute-done((bf16[256,768]{1,0:T(8,128)(2,1)S(1)}, bf16[256,768]{1,0:T(8,128)(2,1)S(1)}, u32[]{:S(2)}, u32[]{:S(2)}) %collective-permute-start.9) | collective-permute-done | bytes 393248 | tf_op jit(solution)/shard_map/ppermute | solution.py:47
  35.5 8.0 %attention_grads.2 = (bf16[512,768]{1,0:T(8,128)(2,1)}, bf16[256,768]{1,0:T(8,128)(2,1)S(1)}, bf16[256,768]{1,0:T(8,128)(2,1)S(1)}, bf16[256,768]{1,0:T(8,128)(2,1)S(1)}, bf16[256,768]{1,0:T(8,128)(2,1)S(1)}) custom-call(bf16[512,768]{1,0:T(8,128)(2,1)S(1)} %copy-done, bf16[512,768]{1,0:T(8,128)(2,1)S(1)} %copy-done.1, ...), custom_call_target="tpu_custom_call" | custom-call | flops 2013265920 | bytes 4325376 | tf_op jit(solution)/shard_map/attention_grads/pallas_call | solution.py:118
  43.9 1.1 collective-permute-start.13
  45.7 8.0 %attention_grads.3 = (bf16[512,768]{1,0:T(8,128)(2,1)}, bf16[256,768]{1,0:T(8,128)(2,1)S(1)}, bf16[256,768]{1,0:T(8,128)(2,1)S(1)}, bf16[256,768]{1,0:T(8,128)(2,1)S(1)}, bf16[256,768]{1,0:T(8,128)(2,1)S(1)}) custom-call(bf16[512,768]{1,0:T(8,128)(2,1)S(1)} %copy-done, bf16[512,768]{1,0:T(8,128)(2,1)S(1)} %copy-done.1, ...), custom_call_target="tpu_custom_call", output_to_operand_aliasing={{0}: (10, {})} | custom-call | flops 2013265920 | bytes 4325376 | tf_op jit(solution)/shard_map/attention_grads/pallas_call | solution.py:118
  53.7 2.1 %collective-permute-start.15 = (bf16[256,768]{1,0:T(8,128)(2,1)S(1)}, bf16[256,768]{1,0:T(8,128)(2,1)S(1)}, u32[]{:S(2)}, u32[]{:S(2)}) collective-permute-start(bf16[256,768]{1,0:T(8,128)(2,1)S(1)} %get-tuple-element.19), channel_id=1, source_target_pairs={{0,192},{1,13},{2,194},{3,15},{4,196},{5,1},{6,198},{7,3},{8,200},... | collective-permute-start | bytes 1179656 | tf_op jit(solution)/shard_map/ppermute | solution.py:47
  55.8 1.6 %collective-permute-start.17 = (bf16[256,768]{1,0:T(8,128)(2,1)S(1)}, bf16[256,768]{1,0:T(8,128)(2,1)S(1)}, u32[]{:S(2)}, u32[]{:S(2)}) collective-permute-start(bf16[256,768]{1,0:T(8,128)(2,1)S(1)} %get-tuple-element.21), channel_id=1, source_target_pairs={{0,128},{1,9},{2,130},{3,11},{4,132},{5,13},{6,134},{7,15},{8,136}... | collective-permute-start | bytes 1179656 | tf_op jit(solution)/shard_map/ppermute | solution.py:47
  57.6 7.1 %collective-permute-done.15 = bf16[256,768]{1,0:T(8,128)(2,1)S(1)} collective-permute-done((bf16[256,768]{1,0:T(8,128)(2,1)S(1)}, bf16[256,768]{1,0:T(8,128)(2,1)S(1)}, u32[]{:S(2)}, u32[]{:S(2)}) %collective-permute-start.15) | collective-permute-done | bytes 393248 | tf_op jit(solution)/shard_map/ppermute | solution.py:47
  64.7 3.4 %collective-permute-done.16 = bf16[256,768]{1,0:T(8,128)(2,1)S(1)} collective-permute-done((bf16[256,768]{1,0:T(8,128)(2,1)S(1)}, bf16[256,768]{1,0:T(8,128)(2,1)S(1)}, u32[]{:S(2)}, u32[]{:S(2)}) %collective-permute-start.16) | collective-permute-done | bytes 393248 | tf_op jit(solution)/shard_map/ppermute | solution.py:47
  68.5 1.7 %collective-permute-start.18 = (bf16[64,1536]{1,0:T(8,128)(2,1)S(1)}, bf16[64,1536]{1,0:T(8,128)(2,1)S(1)}, u32[]{:S(2)}, u32[]{:S(2)}) collective-permute-start(bf16[64,1536]{1,0:T(8,128)(2,1)S(1)} %get-tuple-element.24), channel_id=1, source_target_pairs={{0,12},{1,193},{2,14},{3,195},{4,0},{5,197},{6,2},{7,199},{8,4},{9... | collective-permute-start | bytes 589832 | tf_op jit(solution)/shard_map/ppermute | solution.py:47
  70.2 1.3 %collective-permute-start.20 = (bf16[64,1536]{1,0:T(8,128)(2,1)S(1)}, bf16[64,1536]{1,0:T(8,128)(2,1)S(1)}, u32[]{:S(2)}, u32[]{:S(2)}) collective-permute-start(bf16[64,1536]{1,0:T(8,128)(2,1)S(1)} %get-tuple-element.25), channel_id=1, source_target_pairs={{0,8},{1,129},{2,10},{3,131},{4,12},{5,133},{6,14},{7,135},{8,0},{... | collective-permute-start | bytes 589832 | tf_op jit(solution)/shard_map/ppermute | solution.py:47
  71.4 1.9 %collective-permute-done.18 = bf16[64,1536]{1,0:T(8,128)(2,1)S(1)} collective-permute-done((bf16[64,1536]{1,0:T(8,128)(2,1)S(1)}, bf16[64,1536]{1,0:T(8,128)(2,1)S(1)}, u32[]{:S(2)}, u32[]{:S(2)}) %collective-permute-start.18) | collective-permute-done | bytes 196640 | tf_op jit(solution)/shard_map/ppermute | solution.py:47
  73.4 4.7 %collective-permute-done.19 = bf16[64,1536]{1,0:T(8,128)(2,1)S(1)} collective-permute-done((bf16[64,1536]{1,0:T(8,128)(2,1)S(1)}, bf16[64,1536]{1,0:T(8,128)(2,1)S(1)}, u32[]{:S(2)}, u32[]{:S(2)}) %collective-permute-start.19) | collective-permute-done | bytes 196640 | tf_op jit(solution)/shard_map/ppermute | solution.py:47
  78.2 3.5 %collective-permute-start.21 = (bf16[16,1536]{1,0:T(8,128)(2,1)S(1)}, bf16[16,1536]{1,0:T(8,128)(2,1)S(1)}, u32[]{:S(2)}, u32[]{:S(2)}) collective-permute-start(bf16[16,1536]{1,0:T(8,128)(2,1)S(1)} %get-tuple-element.29), channel_id=1, source_target_pairs={{0,48},{1,49},{2,50},{3,51},{4,52},{5,53},{6,54},{7,55},{8,56},{9,... | collective-permute-start | bytes 147464 | tf_op jit(solution)/shard_map/ppermute | solution.py:47
  82.1 0.8 collective-permute-done.21.a_ref
  82.9 3.6 %collective-permute-done.22.b_ref = bf16[16,1536]{1,0:T(8,128)(2,1)S(1)} collective-permute-done((bf16[16,1536]{1,0:T(8,128)(2,1)S(1)}, bf16[16,1536]{1,0:T(8,128)(2,1)S(1)}, u32[]{:S(2)}, u32[]{:S(2)}) %collective-permute-start.22) | collective-permute-done | bytes 49184 | tf_op jit(solution)/shard_map/ppermute | solution.py:47
  86.4 6.6 %project_rows.1 = bf16[16,3072]{1,0:T(8,128)(2,1)S(1)} custom-call(f32[16,1536]{1,0:T(8,128)S(1)} %split.43.own_ref, bf16[16,1536]{1,0:T(8,128)(2,1)S(1)} %collective-permute-done.21.a_ref, bf16[16,1536]{1,0:T(8,128)(2,1)S(1)} %collective-permute-done.22.b_ref, bf16[16,1536]{1,0:T(8,128)(2,1)S(1)} %collective-permute-done.23.c_ref, ...), custom_call_target="tpu_custom_call" | custom-call | tf_op jit(solution)/shard_map/project_rows/pallas_call | solution.py:157
  93.1 8.8 %collective-permute-start.24 = (bf16[16,1536]{1,0:T(8,128)(2,1)S(1)}, bf16[16,1536]{1,0:T(8,128)(2,1)S(1)}, u32[]{:S(2)}, u32[]{:S(2)}) collective-permute-start(bf16[16,1536]{1,0:T(8,128)(2,1)S(1)} %pad_maximum_fusion.5), channel_id=1, source_target_pairs={{0,1},{1,0},{2,3},{3,2},{4,5},{5,4},{6,7},{7,6},{8,9},{9,8},{10,11... | collective-permute-start | bytes 147464 | tf_op jit(solution)/shard_map/ppermute | solution.py:52
  101.9 0.9 collective-permute-done.24
  102.8 6.9 %collective-permute-start.25 = (bf16[16,768]{1,0:T(8,128)(2,1)S(1)}, bf16[16,768]{1,0:T(8,128)(2,1)S(1)}, u32[]{:S(2)}, u32[]{:S(2)}) collective-permute-start(bf16[16,768]{1,0:T(8,128)(2,1)S(1)} %dynamic-slice_convert_fusion), channel_id=1, source_target_pairs={{0,2},{1,3},{2,0},{3,1},{4,6},{5,7},{6,4},{7,5},{8,10},{9,11},{10,... | collective-permute-start | bytes 73736 | tf_op jit(solution)/shard_map/ppermute | solution.py:52
  109.8 1.2 %collective-permute-done.25 = bf16[16,768]{1,0:T(8,128)(2,1)S(1)} collective-permute-done((bf16[16,768]{1,0:T(8,128)(2,1)S(1)}, bf16[16,768]{1,0:T(8,128)(2,1)S(1)}, u32[]{:S(2)}, u32[]{:S(2)}) %collective-permute-start.25) | collective-permute-done | bytes 24608 | tf_op jit(solution)/shard_map/ppermute | solution.py:52
  (48 shorter events, 5.8 us)
Async XLA Ops:
  1.4 6.8 %collective-permute-start = (bf16[16,1536]{1,0:T(8,128)(2,1)S(1)}, bf16[16,1536]{1,0:T(8,128)(2,1)S(1)}, u32[]{:S(2)}, u32[]{:S(2)}) collective-permute-start(bf16[16,1536]{1,0:T(8,128)(2,1)S(1)} %pad_maximum_fusion.4), channel_id=1, source_target_pairs={{0,16},{1,17},{2,18},{3,19},{4,20},{5,21},{6,22},{7,23},{8,24},{9,... | collective-permute-start | bytes 147464 | tf_op jit(solution)/shard_map/ppermute | solution.py:47
  3.9 4.2 %collective-permute-start.1 = (bf16[16,1536]{1,0:T(8,128)(2,1)S(1)}, bf16[16,1536]{1,0:T(8,128)(2,1)S(1)}, u32[]{:S(2)}, u32[]{:S(2)}) collective-permute-start(bf16[16,1536]{1,0:T(8,128)(2,1)S(1)} %pad_maximum_fusion.4), channel_id=1, source_target_pairs={{0,48},{1,49},{2,50},{3,51},{4,52},{5,53},{6,54},{7,55},{8,56},{9,... | collective-permute-start | bytes 147464 | tf_op jit(solution)/shard_map/ppermute | solution.py:47
  6.7 5.0 %collective-permute-start.2 = (bf16[16,1536]{1,0:T(8,128)(2,1)S(1)}, bf16[16,1536]{1,0:T(8,128)(2,1)S(1)}, u32[]{:S(2)}, u32[]{:S(2)}) collective-permute-start(bf16[16,1536]{1,0:T(8,128)(2,1)S(1)} %pad_maximum_fusion.4), channel_id=1, source_target_pairs={{0,32},{1,33},{2,34},{3,35},{4,36},{5,37},{6,38},{7,39},{8,40},{9,... | collective-permute-start | bytes 147464 | tf_op jit(solution)/shard_map/ppermute | solution.py:47
  11.8 23.7 %copy-start = (bf16[512,768]{1,0:T(8,128)(2,1)S(1)}, bf16[512,768]{1,0:T(8,128)(2,1)}, u32[]{:S(2)}) copy-start(bf16[512,768]{1,0:T(8,128)(2,1)} %q_ref.3) | copy-start | bytes 2359300
  11.8 23.7 %copy-start.1 = (bf16[512,768]{1,0:T(8,128)(2,1)S(1)}, bf16[512,768]{1,0:T(8,128)(2,1)}, u32[]{:S(2)}) copy-start(bf16[512,768]{1,0:T(8,128)(2,1)} %g_ref.3) | copy-start | bytes 2359300
  11.8 5.8 %collective-permute-start.3 = (bf16[64,1536]{1,0:T(8,128)(2,1)S(1)}, bf16[64,1536]{1,0:T(8,128)(2,1)S(1)}, u32[]{:S(2)}, u32[]{:S(2)}) collective-permute-start(bf16[64,1536]{1,0:T(8,128)(2,1)S(1)} %pad_maximum_fusion.3), channel_id=1, source_target_pairs={{0,4},{1,65},{2,6},{3,67},{4,8},{5,69},{6,10},{7,71},{8,12},{9,73}... | collective-permute-start | bytes 589832 | tf_op jit(solution)/shard_map/ppermute | solution.py:47
  12.2 7.1 %collective-permute-start.4 = (bf16[64,1536]{1,0:T(8,128)(2,1)S(1)}, bf16[64,1536]{1,0:T(8,128)(2,1)S(1)}, u32[]{:S(2)}, u32[]{:S(2)}) collective-permute-start(bf16[64,1536]{1,0:T(8,128)(2,1)S(1)} %pad_maximum_fusion.3), channel_id=1, source_target_pairs={{0,12},{1,193},{2,14},{3,195},{4,0},{5,197},{6,2},{7,199},{8,4},{9... | collective-permute-start | bytes 589832 | tf_op jit(solution)/shard_map/ppermute | solution.py:47
  14.6 6.0 %collective-permute-start.5 = (bf16[64,1536]{1,0:T(8,128)(2,1)S(1)}, bf16[64,1536]{1,0:T(8,128)(2,1)S(1)}, u32[]{:S(2)}, u32[]{:S(2)}) collective-permute-start(bf16[64,1536]{1,0:T(8,128)(2,1)S(1)} %pad_maximum_fusion.3), channel_id=1, source_target_pairs={{0,8},{1,129},{2,10},{3,131},{4,12},{5,133},{6,14},{7,135},{8,0},{... | collective-permute-start | bytes 589832 | tf_op jit(solution)/shard_map/ppermute | solution.py:47
  20.6 11.2 %collective-permute-start.10 = (bf16[256,768]{1,0:T(8,128)(2,1)S(1)}, bf16[256,768]{1,0:T(8,128)(2,1)S(1)}, u32[]{:S(2)}, u32[]{:S(2)}) collective-permute-start(bf16[256,768]{1,0:T(8,128)(2,1)S(1)} %pad_maximum_fusion.2.refs_0_.refs_4_), channel_id=1, source_target_pairs={{0,192},{1,13},{2,194},{3,15},{4,196},{5,1},{6,198},{7,3},{8,200},... | collective-permute-start | bytes 1179656 | tf_op jit(solution)/shard_map/ppermute | solution.py:47
  22.9 8.9 %collective-permute-start.11 = (bf16[256,768]{1,0:T(8,128)(2,1)S(1)}, bf16[256,768]{1,0:T(8,128)(2,1)S(1)}, u32[]{:S(2)}, u32[]{:S(2)}) collective-permute-start(bf16[256,768]{1,0:T(8,128)(2,1)S(1)} %pad_maximum_fusion.2.refs_0_.refs_4_), channel_id=1, source_target_pairs={{0,128},{1,9},{2,130},{3,11},{4,132},{5,13},{6,134},{7,15},{8,136}... | collective-permute-start | bytes 1179656 | tf_op jit(solution)/shard_map/ppermute | solution.py:47
  23.1 12.3 %collective-permute-start.9 = (bf16[256,768]{1,0:T(8,128)(2,1)S(1)}, bf16[256,768]{1,0:T(8,128)(2,1)S(1)}, u32[]{:S(2)}, u32[]{:S(2)}) collective-permute-start(bf16[256,768]{1,0:T(8,128)(2,1)S(1)} %pad_maximum_fusion.2.refs_0_.refs_4_), channel_id=1, source_target_pairs={{0,64},{1,5},{2,66},{3,7},{4,68},{5,9},{6,70},{7,11},{8,72},{9,13}... | collective-permute-start | bytes 1179656 | tf_op jit(solution)/shard_map/ppermute | solution.py:47
  23.7 21.2 %collective-permute-start.6 = (bf16[256,768]{1,0:T(8,128)(2,1)S(1)}, bf16[256,768]{1,0:T(8,128)(2,1)S(1)}, u32[]{:S(2)}, u32[]{:S(2)}) collective-permute-start(bf16[256,768]{1,0:T(8,128)(2,1)S(1)} %pad_maximum_fusion.1.refs_0_.refs_4_), channel_id=1, source_target_pairs={{0,64},{1,5},{2,66},{3,7},{4,68},{5,9},{6,70},{7,11},{8,72},{9,13}... | collective-permute-start | bytes 1179656 | tf_op jit(solution)/shard_map/ppermute | solution.py:47
  25.6 20.1 %collective-permute-start.7 = (bf16[256,768]{1,0:T(8,128)(2,1)S(1)}, bf16[256,768]{1,0:T(8,128)(2,1)S(1)}, u32[]{:S(2)}, u32[]{:S(2)}) collective-permute-start(bf16[256,768]{1,0:T(8,128)(2,1)S(1)} %pad_maximum_fusion.1.refs_0_.refs_4_), channel_id=1, source_target_pairs={{0,192},{1,13},{2,194},{3,15},{4,196},{5,1},{6,198},{7,3},{8,200},... | collective-permute-start | bytes 1179656 | tf_op jit(solution)/shard_map/ppermute | solution.py:47
  31.8 13.9 %collective-permute-start.8 = (bf16[256,768]{1,0:T(8,128)(2,1)S(1)}, bf16[256,768]{1,0:T(8,128)(2,1)S(1)}, u32[]{:S(2)}, u32[]{:S(2)}) collective-permute-start(bf16[256,768]{1,0:T(8,128)(2,1)S(1)} %pad_maximum_fusion.1.refs_0_.refs_4_), channel_id=1, source_target_pairs={{0,128},{1,9},{2,130},{3,11},{4,132},{5,13},{6,134},{7,15},{8,136}... | collective-permute-start | bytes 1179656 | tf_op jit(solution)/shard_map/ppermute | solution.py:47
  43.5 12.3 %collective-permute-start.12 = (bf16[256,768]{1,0:T(8,128)(2,1)S(1)}, bf16[256,768]{1,0:T(8,128)(2,1)S(1)}, u32[]{:S(2)}, u32[]{:S(2)}) collective-permute-start(bf16[256,768]{1,0:T(8,128)(2,1)S(1)} %get-tuple-element.15), channel_id=1, source_target_pairs={{0,192},{1,13},{2,194},{3,15},{4,196},{5,1},{6,198},{7,3},{8,200},... | collective-permute-start | bytes 1179656 | tf_op jit(solution)/shard_map/ppermute | solution.py:47
  43.9 13.6 %collective-permute-start.13 = (bf16[256,768]{1,0:T(8,128)(2,1)S(1)}, bf16[256,768]{1,0:T(8,128)(2,1)S(1)}, u32[]{:S(2)}, u32[]{:S(2)}) collective-permute-start(bf16[256,768]{1,0:T(8,128)(2,1)S(1)} %get-tuple-element.16), channel_id=1, source_target_pairs={{0,64},{1,5},{2,66},{3,7},{4,68},{5,9},{6,70},{7,11},{8,72},{9,13}... | collective-permute-start | bytes 1179656 | tf_op jit(solution)/shard_map/ppermute | solution.py:47
  45.0 12.5 %collective-permute-start.14 = (bf16[256,768]{1,0:T(8,128)(2,1)S(1)}, bf16[256,768]{1,0:T(8,128)(2,1)S(1)}, u32[]{:S(2)}, u32[]{:S(2)}) collective-permute-start(bf16[256,768]{1,0:T(8,128)(2,1)S(1)} %get-tuple-element.17), channel_id=1, source_target_pairs={{0,128},{1,9},{2,130},{3,11},{4,132},{5,13},{6,134},{7,15},{8,136}... | collective-permute-start | bytes 1179656 | tf_op jit(solution)/shard_map/ppermute | solution.py:47
  53.7 11.0 %collective-permute-start.15 = (bf16[256,768]{1,0:T(8,128)(2,1)S(1)}, bf16[256,768]{1,0:T(8,128)(2,1)S(1)}, u32[]{:S(2)}, u32[]{:S(2)}) collective-permute-start(bf16[256,768]{1,0:T(8,128)(2,1)S(1)} %get-tuple-element.19), channel_id=1, source_target_pairs={{0,192},{1,13},{2,194},{3,15},{4,196},{5,1},{6,198},{7,3},{8,200},... | collective-permute-start | bytes 1179656 | tf_op jit(solution)/shard_map/ppermute | solution.py:47
  55.8 12.3 %collective-permute-start.16 = (bf16[256,768]{1,0:T(8,128)(2,1)S(1)}, bf16[256,768]{1,0:T(8,128)(2,1)S(1)}, u32[]{:S(2)}, u32[]{:S(2)}) collective-permute-start(bf16[256,768]{1,0:T(8,128)(2,1)S(1)} %get-tuple-element.20), channel_id=1, source_target_pairs={{0,64},{1,5},{2,66},{3,7},{4,68},{5,9},{6,70},{7,11},{8,72},{9,13}... | collective-permute-start | bytes 1179656 | tf_op jit(solution)/shard_map/ppermute | solution.py:47
  55.8 12.3 %collective-permute-start.17 = (bf16[256,768]{1,0:T(8,128)(2,1)S(1)}, bf16[256,768]{1,0:T(8,128)(2,1)S(1)}, u32[]{:S(2)}, u32[]{:S(2)}) collective-permute-start(bf16[256,768]{1,0:T(8,128)(2,1)S(1)} %get-tuple-element.21), channel_id=1, source_target_pairs={{0,128},{1,9},{2,130},{3,11},{4,132},{5,13},{6,134},{7,15},{8,136}... | collective-permute-start | bytes 1179656 | tf_op jit(solution)/shard_map/ppermute | solution.py:47
  68.5 4.9 %collective-permute-start.18 = (bf16[64,1536]{1,0:T(8,128)(2,1)S(1)}, bf16[64,1536]{1,0:T(8,128)(2,1)S(1)}, u32[]{:S(2)}, u32[]{:S(2)}) collective-permute-start(bf16[64,1536]{1,0:T(8,128)(2,1)S(1)} %get-tuple-element.24), channel_id=1, source_target_pairs={{0,12},{1,193},{2,14},{3,195},{4,0},{5,197},{6,2},{7,199},{8,4},{9... | collective-permute-start | bytes 589832 | tf_op jit(solution)/shard_map/ppermute | solution.py:47
  70.2 7.9 %collective-permute-start.19 = (bf16[64,1536]{1,0:T(8,128)(2,1)S(1)}, bf16[64,1536]{1,0:T(8,128)(2,1)S(1)}, u32[]{:S(2)}, u32[]{:S(2)}) collective-permute-start(bf16[64,1536]{1,0:T(8,128)(2,1)S(1)} %get-tuple-element.26), channel_id=1, source_target_pairs={{0,4},{1,65},{2,6},{3,67},{4,8},{5,69},{6,10},{7,71},{8,12},{9,73}... | collective-permute-start | bytes 589832 | tf_op jit(solution)/shard_map/ppermute | solution.py:47
  70.2 7.9 %collective-permute-start.20 = (bf16[64,1536]{1,0:T(8,128)(2,1)S(1)}, bf16[64,1536]{1,0:T(8,128)(2,1)S(1)}, u32[]{:S(2)}, u32[]{:S(2)}) collective-permute-start(bf16[64,1536]{1,0:T(8,128)(2,1)S(1)} %get-tuple-element.25), channel_id=1, source_target_pairs={{0,8},{1,129},{2,10},{3,131},{4,12},{5,133},{6,14},{7,135},{8,0},{... | collective-permute-start | bytes 589832 | tf_op jit(solution)/shard_map/ppermute | solution.py:47
  78.2 4.7 %collective-permute-start.21 = (bf16[16,1536]{1,0:T(8,128)(2,1)S(1)}, bf16[16,1536]{1,0:T(8,128)(2,1)S(1)}, u32[]{:S(2)}, u32[]{:S(2)}) collective-permute-start(bf16[16,1536]{1,0:T(8,128)(2,1)S(1)} %get-tuple-element.29), channel_id=1, source_target_pairs={{0,48},{1,49},{2,50},{3,51},{4,52},{5,53},{6,54},{7,55},{8,56},{9,... | collective-permute-start | bytes 147464 | tf_op jit(solution)/shard_map/ppermute | solution.py:47
  81.7 4.7 %collective-permute-start.22 = (bf16[16,1536]{1,0:T(8,128)(2,1)S(1)}, bf16[16,1536]{1,0:T(8,128)(2,1)S(1)}, u32[]{:S(2)}, u32[]{:S(2)}) collective-permute-start(bf16[16,1536]{1,0:T(8,128)(2,1)S(1)} %get-tuple-element.28), channel_id=1, source_target_pairs={{0,16},{1,17},{2,18},{3,19},{4,20},{5,21},{6,22},{7,23},{8,24},{9,... | collective-permute-start | bytes 147464 | tf_op jit(solution)/shard_map/ppermute | solution.py:47
  81.7 4.7 %collective-permute-start.23 = (bf16[16,1536]{1,0:T(8,128)(2,1)S(1)}, bf16[16,1536]{1,0:T(8,128)(2,1)S(1)}, u32[]{:S(2)}, u32[]{:S(2)}) collective-permute-start(bf16[16,1536]{1,0:T(8,128)(2,1)S(1)} %get-tuple-element.27), channel_id=1, source_target_pairs={{0,32},{1,33},{2,34},{3,35},{4,36},{5,37},{6,38},{7,39},{8,40},{9,... | collective-permute-start | bytes 147464 | tf_op jit(solution)/shard_map/ppermute | solution.py:47
  93.1 9.7 %collective-permute-start.24 = (bf16[16,1536]{1,0:T(8,128)(2,1)S(1)}, bf16[16,1536]{1,0:T(8,128)(2,1)S(1)}, u32[]{:S(2)}, u32[]{:S(2)}) collective-permute-start(bf16[16,1536]{1,0:T(8,128)(2,1)S(1)} %pad_maximum_fusion.5), channel_id=1, source_target_pairs={{0,1},{1,0},{2,3},{3,2},{4,5},{5,4},{6,7},{7,6},{8,9},{9,8},{10,11... | collective-permute-start | bytes 147464 | tf_op jit(solution)/shard_map/ppermute | solution.py:52
  102.8 8.2 %collective-permute-start.25 = (bf16[16,768]{1,0:T(8,128)(2,1)S(1)}, bf16[16,768]{1,0:T(8,128)(2,1)S(1)}, u32[]{:S(2)}, u32[]{:S(2)}) collective-permute-start(bf16[16,768]{1,0:T(8,128)(2,1)S(1)} %dynamic-slice_convert_fusion), channel_id=1, source_target_pairs={{0,2},{1,3},{2,0},{3,1},{4,6},{5,7},{6,4},{7,5},{8,10},{9,11},{10,... | collective-permute-start | bytes 73736 | tf_op jit(solution)/shard_map/ppermute | solution.py:52

commit v3 on v0

v3 whole, which is shorter than its diff:
```python
import functools
import math

import jax
import jax.numpy as jnp
from jax import lax
from jax.experimental import pallas as pl
from jax.experimental.pallas import tpu as pltpu
from jax.sharding import PartitionSpec as P

HD = 128
SCALE = 1.0 / HD**0.5
NN = (((1,), (0,)), ((), ()))
NT = (((1,), (1,)), ((), ()))
TN = (((0,), (0,)), ((), ()))

DEVICES = 256
Y, Z, X, HALF, CORE = 64, 16, 4, 2, 1
LATE = (X, Y)
EARLY = (Y, X)
STEPS = (1, 3, 2)


def swap(block, axes, step=1):
    pairs = [(i, i ^ (step * axes[i % 2])) for i in range(DEVICES)]
    return lax.ppermute(block, ("seq", "tensor"), pairs)


def gather(block, axes):
    return [block] + [swap(block, axes, step) for step in STEPS]


def scatter_sum(blocks, axes):
    total = wide(blocks[0])
    for block, step in zip(blocks[1:], STEPS):
        total += wide(swap(narrow(block), axes, step))
    return total


def wide(array):
    return array.astype(jnp.float32)


def narrow(array):
    return array.astype(jnp.bfloat16)


def dot(a, b, dims=NN):
    return lax.dot_general(a, b, dims, preferred_element_type=jnp.float32)


def join(*rows):
    return jnp.concatenate(rows, axis=0)


def attention_kernel(chunk, parity_ref, *refs):
    queries, grads_out = (refs[0], refs[2]), (refs[1], refs[3])
    keys, values = refs[4:8], refs[8:12]
    grad_queries, parts = refs[12:14], refs[14:18]
    probs_ref, grads_ref = refs[18:]
    rows = keys[0].shape[0]
    tokens = queries[0].shape[0]
    for n in range(2):
        for at in range(0, tokens, chunk):
            q, g = queries[n][pl.ds(at, chunk), :], grads_out[n][pl.ds(at, chunk), :]
            some = pl.ds(n * tokens + at, chunk)
            scores = [dot(k[...], q, NT) for k in keys]
            top = functools.reduce(
                jnp.maximum, [jnp.max(s, axis=0, keepdims=True) for s in scores]
            )
            raised = [jnp.exp2((s - top) * (SCALE * math.log2(math.e))) for s in scores]
            inverse = 1.0 / sum(jnp.sum(e, axis=0, keepdims=True) for e in raised)
            probs = [e * inverse for e in raised]
            grad_probs = [dot(v[...], g, NT) for v in values]
            delta = sum(
                jnp.sum(p * d, axis=0, keepdims=True) for p, d in zip(probs, grad_probs)
            )
            for i, (p, d) in enumerate(zip(probs, grad_probs)):
                here = pl.ds(i * rows, rows)
                probs_ref[here, some] = narrow(p)
                grads_ref[here, some] = narrow(p * (d - delta))
    spans = [pl.ds(n * tokens, tokens) for n in range(2)]
    for i in range(4):
        here = pl.ds(i * rows, rows)
        dk = sum(dot(grads_ref[here, t], q[...]) for t, q in zip(spans, queries))
        dv = sum(dot(probs_ref[here, t], g[...]) for t, g in zip(spans, grads_out))
        parts[i][:, :HD] = narrow(dk * SCALE)
        parts[i][:, HD:] = narrow(dv)
    for t, out_ref in zip(spans, grad_queries):
        dq = sum(dot(k[...], grads_ref[pl.ds(i * rows, rows), t], TN) for i, k in enumerate(keys))
        out_ref[...] = narrow(dq.T * SCALE)


def attention(parity, queries, grad_out, far, blocks, result_shape):
    tokens, width = queries.shape
    rows, columns = blocks[0].shape
    heads = width // HD
    placed = pl.BlockSpec((tokens, HD), lambda h, parity: (0, parity[0] * heads + h))
    token = pl.BlockSpec((tokens, HD), lambda h, parity: (0, h))
    token_second = pl.BlockSpec((tokens, HD), lambda h, parity: (0, heads + h))
    key = pl.BlockSpec((rows, HD), lambda h, parity: (0, h))
    value = pl.BlockSpec((rows, HD), lambda h, parity: (0, heads + h))
    part = pl.BlockSpec((rows, 2 * HD), lambda h, parity: (0, h))
    scores = heads * 2 * tokens * 4 * rows
    shapes = [result_shape, queries.shape] + [b.shape for b in blocks]
    return pl.pallas_call(
        functools.partial(attention_kernel, tokens // 2),
        grid_spec=pltpu.PrefetchScalarGridSpec(
            num_scalar_prefetch=1,
            grid=(heads,),
            in_specs=[token] * 2 + [token, token_second] + [key] * 4 + [value] * 4,
            out_specs=[placed, token] + [part] * 4,
            scratch_shapes=[pltpu.VMEM((4 * rows, 2 * tokens), jnp.bfloat16)] * 2,
        ),
        out_shape=[jax.ShapeDtypeStruct(shape, jnp.bfloat16) for shape in shapes],
        compiler_params=pltpu.CompilerParams(vmem_limit_bytes=24 * 2**20),
        cost_estimate=pl.CostEstimate(
            flops=10 * HD * scores,
            bytes_accessed=2 * (6 * tokens * heads * HD + 8 * rows * columns),
            transcendentals=scores,
        ),
        name="attention_grads",
    )(parity, queries, grad_out, far, far, *blocks, *blocks)


def project_kernel(
    blocks,
    parity_ref,
    mine_ref,
    other_ref,
    key_ref,
    value_ref,
    far_ref,
    _,
    out_ref,
    near_ref,
    key_held,
    value_held,
    weight_sems,
    far_sem,
):
    features = key_ref.shape[0] // blocks
    copies = []
    for n in range(blocks):
        here = pl.ds(n * features, features)
        pairs = ((key_ref, key_held), (value_ref, value_held))
        copies.append(
            [
                pltpu.make_async_copy(a.at[here, :], b.at[here, :], weight_sems.at[i, n])
                for i, (a, b) in enumerate(pairs)
            ]
        )
        for copy in copies[-1]:
            copy.start()
    half = far_ref.shape[1]
    place = pl.ds(pl.multiple_of((1 - parity_ref[0]) * half, half), half)
    far_copy = pltpu.make_async_copy(far_ref, near_ref.at[:, place], far_sem)
    far_copy.start()

    def halves(sums):
        high = narrow(sums)
        return join(high, narrow(sums - wide(high)))

    rows, width = mine_ref.shape
    mine, other = halves(mine_ref[...]), halves(other_ref[...])
    first = parity_ref[0] == 0
    left = jnp.where(first, mine, other)
    right = jnp.where(first, other, mine)

    def both(start):
        picks = range(start, width, 2 * HD)
        return jnp.concatenate([a[:, at : at + HD] for a in (left, right) for at in picks], axis=1)

    keys, values = both(0), both(HD)
    for n in range(blocks):
        here = pl.ds(n * features, features)
        for copy in copies[n]:
            copy.wait()
        result = dot(keys, key_held[here, :], NT) + dot(values, value_held[here, :], NT)
        out_ref[:, here] = narrow(result[:rows] + result[rows:])
    far_copy.wait()


def project(parity, mine, other, key_weight, value_weight, grad_far, grad_queries):
    blocks = 6
    vmem = pl.BlockSpec(memory_space=pltpu.VMEM)
    whole = pl.BlockSpec(memory_space=pl.ANY)
    return pl.pallas_call(
        functools.partial(project_kernel, blocks),
        in_specs=[pl.BlockSpec(memory_space=pltpu.SMEM)] + [vmem] * 2 + [whole] * 4,
        out_specs=[vmem, whole],
        out_shape=[
            jax.ShapeDtypeStruct((mine.shape[0], key_weight.shape[0]), jnp.bfloat16),
            jax.ShapeDtypeStruct(grad_queries.shape, jnp.bfloat16),
        ],
        scratch_shapes=[pltpu.VMEM(key_weight.shape, jnp.bfloat16)] * 2
        + [pltpu.SemaphoreType.DMA((2, blocks)), pltpu.SemaphoreType.DMA],
        input_output_aliases={6: 1},
        compiler_params=pltpu.CompilerParams(vmem_limit_bytes=52 * 2**20),
        name="project_rows",
    )(parity, mine, other, key_weight, value_weight, grad_far, grad_queries)


def shards(queries, ref_keys, ref_values, grad_out, key_weight, value_weight):
    parity = lax.axis_index("seq") // (Z // X) % 2
    half = queries.shape[1] // 2

    def columns(array, which):
        return lax.dynamic_slice_in_dim(array, which * half, half, axis=1)

    mine = jnp.concatenate([columns(ref_keys, parity), columns(ref_values, parity)], axis=1)
    other = jnp.concatenate(
        [columns(ref_keys, 1 - parity), columns(ref_values, 1 - parity)], axis=1
    )
    rows = join(mine, swap(other, (Z, Z), 1), swap(other, (Z, Z), 3), swap(mine, (Z, Z), 2))
    spot = parity.astype(jnp.int32).reshape(1)
    near = [columns(a, parity) for a in (queries, grad_out)]
    far = jnp.concatenate([columns(a, 1 - parity) for a in (queries, grad_out)], axis=1)
    rows, near, far = lax.optimization_barrier((rows, near, far))
    far = swap(far, (Z, Z))
    rows = join(*gather(rows, LATE))
    blocks = gather(rows, EARLY)

    grad_queries, grad_far, *parts = attention(spot, *near, far, blocks, queries.shape)

    total = scatter_sum(parts, EARLY)
    grad_far = swap(grad_far, (Z, Z))
    total, grad_far = lax.optimization_barrier((total, grad_far))
    total = scatter_sum(jnp.split(total, 4), LATE)
    cut = jnp.split(total, 4)
    total = cut[0] + wide(swap(narrow(cut[3]), (Z, Z), 2))
    received = wide(swap(narrow(cut[1]), (Z, Z), 1)) + wide(swap(narrow(cut[2]), (Z, Z), 3))
    result, grad_queries = project(
        spot, total, received, key_weight, value_weight, grad_far, grad_queries
    )

    quarter = result.shape[1] // 4
    me = lax.axis_index("tensor")
    z_half, core = me // 2, me % 2

    def features(array, which):
        return lax.dynamic_slice_in_dim(array, which * quarter, quarter, axis=1)

    def of_core(which):
        return jnp.concatenate([features(result, which), features(result, 2 + which)], axis=1)

    pair = wide(of_core(core)) + wide(swap(of_core(1 - core), (CORE, CORE)))
    away = narrow(features(pair, 1 - z_half))
    grad_rows = features(pair, z_half) + wide(swap(away, (HALF, HALF)))
    return grad_queries, narrow(grad_rows)


def solution(mesh):
    placed = (
        P("seq", "tensor"),
        P("seq", "tensor"),
        P("seq", "tensor"),
        P("seq", "tensor"),
        P(None, "tensor"),
        P(None, "tensor"),
    )
    return jax.shard_map(
        shards,
        mesh=mesh,
        in_specs=placed,
        out_specs=(P("seq", "tensor"), P("seq", "tensor")),
        check_vma=False,
    )
```

time: 1530 us -> 97.7 us (0.06)
  waiting for transfers between devices: 1460 us -> 34.1 us
  starting transfers between devices: 0.42 us -> 40.6 us
  matrix products: 35.2 us -> 0 us
  Pallas kernels: 0 us -> 18.7 us
    unnamed x7 -> x0, waiting for transfers between devices: 729 us -> none
    all_gather x2 -> x0, waiting for transfers between devices: 653 us -> none  [the longest x1 344 us: shards(): lax.all_gather(ref_values, 'seq', axis=0, tiled=True)]
    reduce_scatter x1 -> x0, waiting for transfers between devices: 76.6 us -> none  [shards(): lax.psum_scatter(partial_value.astype(jnp.bfloat16), 'tensor', scatter_di...]
    ppermute x0 -> x22, starting transfers between devices: none -> 40.6 us  [swap(): return lax.ppermute(block, ('seq', 'tensor'), pairs)]
    dot_general x32 -> x0, matrix products: 35.2 us -> none  [the longest x1 6.8 us: project_exact(): jnp.dot(keys_own, key_cols.T, precision=lax.Precision.HIGHEST, preferred_...]
    ppermute x0 -> x22, waiting for transfers between devices: none -> 34.1 us  [swap(): return lax.ppermute(block, ('seq', 'tensor'), pairs)]
    pallas_call x0 -> x2, Pallas kernels: none -> 18.7 us  [the longest x1 13.6 us: attention(): pl.pallas_call(functools.partial(attention_kernel, tokens // 2), grid_spe...]
  transfers between devices with their start and end apart: 5 -> 22, of which waited for: 5 -> 14; matrix products, arithmetic and copies ran while one was open for 1% -> 2% of each run, Pallas kernels for 0% -> 0%
where the time goes in v3:
time: 97.7 us; the launch traced here: 97.6 us
  starting transfers between devices  40.6 us (42%)
  waiting for transfers between devices  34.1 us (35%)
  Pallas kernels  18.7 us (19%)
  local copies, waits for them, and re-layouts  2.38 us (2%)
  other arithmetic  1.03 us (1%)
    ppermute x22, starting transfers between devices, swap(): return lax.ppermute(block, ('seq', 'tensor'), pairs)  40.6 us
    ppermute x22, waiting for transfers between devices, swap(): return lax.ppermute(block, ('seq', 'tensor'), pairs)  34.1 us
    pallas_call x1, Pallas kernels, attention(): pl.pallas_call(functools.partial(attention_kernel, tokens // 2), grid_spe...  13.6 us
    pallas_call x1, Pallas kernels, project(): pl.pallas_call(functools.partial(project_kernel, blocks), in_specs=[pl.Bl...  5.02 us
    dynamic_slice x2, local copies, waits for them, and re-layouts, columns(): return lax.dynamic_slice_in_dim(array, which * half, half, axis=1)  2.28 us
  transfers between devices with their start and end apart: 22, of which 14 were waited for; matrix products, arithmetic and copies ran while one was open for 2% of the time, Pallas kernels for 0%

profile of v3, /device:TPU:1, one launch (start us, length us, event | category | flops | bytes accessed | tf_op | source)
XLA Modules:
  0.0 97.6 jit_solution(14278072698838062672)
XLA Ops:
  1.5 2.6 %collective-permute-start = (bf16[16,768]{1,0:T(8,128)(2,1)S(1)}, bf16[16,768]{1,0:T(8,128)(2,1)S(1)}, u32[]{:S(2)}, u32[]{:S(2)}) collective-permute-start(bf16[16,768]{1,0:T(8,128)(2,1)S(1)} %pad_maximum_fusion.4), channel_id=1, source_target_pairs={{0,16},{1,17},{2,18},{3,19},{4,20},{5,21},{6,22},{7,23},{8,24},{9,... | collective-permute-start | bytes 73736 | tf_op jit(solution)/shard_map/ppermute | solution.py:26
  4.0 2.8 %collective-permute-start.1 = (bf16[16,768]{1,0:T(8,128)(2,1)S(1)}, bf16[16,768]{1,0:T(8,128)(2,1)S(1)}, u32[]{:S(2)}, u32[]{:S(2)}) collective-permute-start(bf16[16,768]{1,0:T(8,128)(2,1)S(1)} %pad_maximum_fusion.4), channel_id=1, source_target_pairs={{0,48},{1,49},{2,50},{3,51},{4,52},{5,53},{6,54},{7,55},{8,56},{9,... | collective-permute-start | bytes 73736 | tf_op jit(solution)/shard_map/ppermute | solution.py:26
  7.0 1.5 %constant_dynamic-slice_fusion.4 = (bf16[512,384]{1,0:T(8,128)(2,1)S(1)}, bf16[512,384]{1,0:T(8,128)(2,1)S(1)}, bf16[512,384]{1,0:T(8,128)(2,1)S(1)}, bf16[512,384]{1,0:T(8,128)(2,1)S(1)}) fusion(bf16[512,768]{1,0:T(8,128)(2,1)} %param.9, s32[]{:T(128)S(6)} %select_n.51, s32[]{:T(128)S(6)} %select_n.50, bf16[512,768]{1,0:T(8,128)(2,1)} %param.6), kind=kLoop, calls=%fused_computation.20 | loop fusion | bytes 3145736 | tf_op jit(solution)/shard_map/dynamic_slice | solution.py:209
  8.6 1.8 %collective-permute-done.2 = bf16[16,768]{1,0:T(8,128)(2,1)S(1)} collective-permute-done((bf16[16,768]{1,0:T(8,128)(2,1)S(1)}, bf16[16,768]{1,0:T(8,128)(2,1)S(1)}, u32[]{:S(2)}, u32[]{:S(2)}) %collective-permute-start.2) | collective-permute-done | bytes 24608 | tf_op jit(solution)/shard_map/ppermute | solution.py:26
  10.4 1.4 %collective-permute-start.4 = (bf16[64,768]{1,0:T(8,128)(2,1)S(1)}, bf16[64,768]{1,0:T(8,128)(2,1)S(1)}, u32[]{:S(2)}, u32[]{:S(2)}) collective-permute-start(bf16[64,768]{1,0:T(8,128)(2,1)S(1)} %pad_maximum_fusion.1), channel_id=1, source_target_pairs={{0,4},{1,65},{2,6},{3,67},{4,0},{5,69},{6,2},{7,71},{8,12},{9,73},... | collective-permute-start | bytes 294920 | tf_op jit(solution)/shard_map/ppermute | solution.py:26
  12.3 2.0 %collective-permute-start.5 = (bf16[64,768]{1,0:T(8,128)(2,1)S(1)}, bf16[64,768]{1,0:T(8,128)(2,1)S(1)}, u32[]{:S(2)}, u32[]{:S(2)}) collective-permute-start(bf16[64,768]{1,0:T(8,128)(2,1)S(1)} %pad_maximum_fusion.1), channel_id=1, source_target_pairs={{0,12},{1,193},{2,14},{3,195},{4,8},{5,197},{6,10},{7,199},{8,4},{... | collective-permute-start | bytes 294920 | tf_op jit(solution)/shard_map/ppermute | solution.py:26
  15.2 1.9 %collective-permute-done.5 = bf16[64,768]{1,0:T(8,128)(2,1)S(1)} collective-permute-done((bf16[64,768]{1,0:T(8,128)(2,1)S(1)}, bf16[64,768]{1,0:T(8,128)(2,1)S(1)}, u32[]{:S(2)}, u32[]{:S(2)}) %collective-permute-start.5) | collective-permute-done | bytes 98336 | tf_op jit(solution)/shard_map/ppermute | solution.py:26
  17.1 2.2 %collective-permute-done.6 = bf16[64,768]{1,0:T(8,128)(2,1)S(1)} collective-permute-done((bf16[64,768]{1,0:T(8,128)(2,1)S(1)}, bf16[64,768]{1,0:T(8,128)(2,1)S(1)}, u32[]{:S(2)}, u32[]{:S(2)}) %collective-permute-start.6) | collective-permute-done | bytes 98336 | tf_op jit(solution)/shard_map/ppermute | solution.py:26
  19.3 1.3 %collective-permute-start.7 = (bf16[256,768]{1,0:T(8,128)(2,1)S(1)}, bf16[256,768]{1,0:T(8,128)(2,1)S(1)}, u32[]{:S(2)}, u32[]{:S(2)}) collective-permute-start(bf16[256,768]{1,0:T(8,128)(2,1)S(1)} %constant_dynamic-update-slice_fusion.refs_4_.refs_8_), channel_id=1, source_target_pairs={{0,64},{1,5},{2,66},{3,7},{4,68},{5,1},{6,70},{7,3},{8,72},{9,13},... | collective-permute-start | bytes 1179656 | tf_op jit(solution)/shard_map/ppermute | solution.py:26
  20.6 1.8 %collective-permute-start.8 = (bf16[256,768]{1,0:T(8,128)(2,1)S(1)}, bf16[256,768]{1,0:T(8,128)(2,1)S(1)}, u32[]{:S(2)}, u32[]{:S(2)}) collective-permute-start(bf16[256,768]{1,0:T(8,128)(2,1)S(1)} %constant_dynamic-update-slice_fusion.refs_4_.refs_8_), channel_id=1, source_target_pairs={{0,192},{1,13},{2,194},{3,15},{4,196},{5,9},{6,198},{7,11},{8,200}... | collective-permute-start | bytes 1179656 | tf_op jit(solution)/shard_map/ppermute | solution.py:26
  23.1 3.3 %collective-permute-done.7.refs_5_.refs_9_ = bf16[256,768]{1,0:T(8,128)(2,1)S(1)} collective-permute-done((bf16[256,768]{1,0:T(8,128)(2,1)S(1)}, bf16[256,768]{1,0:T(8,128)(2,1)S(1)}, u32[]{:S(2)}, u32[]{:S(2)}) %collective-permute-start.7) | collective-permute-done | bytes 393248 | tf_op jit(solution)/shard_map/ppermute | solution.py:26
  26.3 6.6 %collective-permute-done.8.refs_6_.refs_10_ = bf16[256,768]{1,0:T(8,128)(2,1)S(1)} collective-permute-done((bf16[256,768]{1,0:T(8,128)(2,1)S(1)}, bf16[256,768]{1,0:T(8,128)(2,1)S(1)}, u32[]{:S(2)}, u32[]{:S(2)}) %collective-permute-start.8) | collective-permute-done | bytes 393248 | tf_op jit(solution)/shard_map/ppermute | solution.py:26
  33.0 13.6 %attention_grads.1 = (bf16[512,768]{1,0:T(8,128)(2,1)}, bf16[512,384]{1,0:T(8,128)(2,1)S(1)}, bf16[256,768]{1,0:T(8,128)(2,1)S(1)}, bf16[256,768]{1,0:T(8,128)(2...) custom-call(s32[1]{0:T(128)} %bitcast.parity_ref, bf16[512,384]{1,0:T(8,128)(2,1)S(1)} %get-tuple-element.16.refs_0_, ...), custom_call_target="tpu_custom_call" | custom-call | flops 4026531840 | bytes 5505024 | tf_op jit(solution)/shard_map/attention_grads/pallas_call | solution.py:106
  46.6 1.8 %collective-permute-start.11 = (bf16[256,768]{1,0:T(8,128)(2,1)S(1)}, bf16[256,768]{1,0:T(8,128)(2,1)S(1)}, u32[]{:S(2)}, u32[]{:S(2)}) collective-permute-start(bf16[256,768]{1,0:T(8,128)(2,1)S(1)} %get-tuple-element.22), channel_id=1, source_target_pairs={{0,192},{1,13},{2,194},{3,15},{4,196},{5,9},{6,198},{7,11},{8,200}... | collective-permute-start | bytes 1179656 | tf_op jit(solution)/shard_map/ppermute | solution.py:26
  48.4 1.4 %collective-permute-start.12 = (bf16[256,768]{1,0:T(8,128)(2,1)S(1)}, bf16[256,768]{1,0:T(8,128)(2,1)S(1)}, u32[]{:S(2)}, u32[]{:S(2)}) collective-permute-start(bf16[256,768]{1,0:T(8,128)(2,1)S(1)} %get-tuple-element.23), channel_id=1, source_target_pairs={{0,128},{1,9},{2,130},{3,11},{4,132},{5,13},{6,134},{7,15},{8,136}... | collective-permute-start | bytes 1179656 | tf_op jit(solution)/shard_map/ppermute | solution.py:26
  49.9 0.9 collective-permute-start.13
  50.8 2.4 %collective-permute-done.10 = bf16[256,768]{1,0:T(8,128)(2,1)S(1)} collective-permute-done((bf16[256,768]{1,0:T(8,128)(2,1)S(1)}, bf16[256,768]{1,0:T(8,128)(2,1)S(1)}, u32[]{:S(2)}, u32[]{:S(2)}) %collective-permute-start.10) | collective-permute-done | bytes 393248 | tf_op jit(solution)/shard_map/ppermute | solution.py:26
  53.2 4.1 %collective-permute-done.11 = bf16[256,768]{1,0:T(8,128)(2,1)S(1)} collective-permute-done((bf16[256,768]{1,0:T(8,128)(2,1)S(1)}, bf16[256,768]{1,0:T(8,128)(2,1)S(1)}, u32[]{:S(2)}, u32[]{:S(2)}) %collective-permute-start.11) | collective-permute-done | bytes 393248 | tf_op jit(solution)/shard_map/ppermute | solution.py:26
  57.4 1.6 %collective-permute-done.12 = bf16[256,768]{1,0:T(8,128)(2,1)S(1)} collective-permute-done((bf16[256,768]{1,0:T(8,128)(2,1)S(1)}, bf16[256,768]{1,0:T(8,128)(2,1)S(1)}, u32[]{:S(2)}, u32[]{:S(2)}) %collective-permute-start.12) | collective-permute-done | bytes 393248 | tf_op jit(solution)/shard_map/ppermute | solution.py:26
  59.5 1.5 %collective-permute-start.15 = (bf16[64,768]{1,0:T(8,128)(2,1)S(1)}, bf16[64,768]{1,0:T(8,128)(2,1)S(1)}, u32[]{:S(2)}, u32[]{:S(2)}) collective-permute-start(bf16[64,768]{1,0:T(8,128)(2,1)S(1)} %get-tuple-element.38), channel_id=1, source_target_pairs={{0,12},{1,193},{2,14},{3,195},{4,8},{5,197},{6,10},{7,199},{8,4},{... | collective-permute-start | bytes 294920 | tf_op jit(solution)/shard_map/ppermute | solution.py:26
  61.0 1.6 %collective-permute-start.16 = (bf16[64,768]{1,0:T(8,128)(2,1)S(1)}, bf16[64,768]{1,0:T(8,128)(2,1)S(1)}, u32[]{:S(2)}, u32[]{:S(2)}) collective-permute-start(bf16[64,768]{1,0:T(8,128)(2,1)S(1)} %get-tuple-element.37), channel_id=1, source_target_pairs={{0,8},{1,129},{2,10},{3,131},{4,12},{5,133},{6,14},{7,135},{8,0},{... | collective-permute-start | bytes 294920 | tf_op jit(solution)/shard_map/ppermute | solution.py:26
  62.6 1.6 %collective-permute-done.14 = bf16[64,768]{1,0:T(8,128)(2,1)S(1)} collective-permute-done((bf16[64,768]{1,0:T(8,128)(2,1)S(1)}, bf16[64,768]{1,0:T(8,128)(2,1)S(1)}, u32[]{:S(2)}, u32[]{:S(2)}) %collective-permute-start.14) | collective-permute-done | bytes 98336 | tf_op jit(solution)/shard_map/ppermute | solution.py:26
  64.2 2.0 %collective-permute-done.15 = bf16[64,768]{1,0:T(8,128)(2,1)S(1)} collective-permute-done((bf16[64,768]{1,0:T(8,128)(2,1)S(1)}, bf16[64,768]{1,0:T(8,128)(2,1)S(1)}, u32[]{:S(2)}, u32[]{:S(2)}) %collective-permute-start.15) | collective-permute-done | bytes 98336 | tf_op jit(solution)/shard_map/ppermute | solution.py:26
  66.3 1.3 %collective-permute-done.16 = bf16[64,768]{1,0:T(8,128)(2,1)S(1)} collective-permute-done((bf16[64,768]{1,0:T(8,128)(2,1)S(1)}, bf16[64,768]{1,0:T(8,128)(2,1)S(1)}, u32[]{:S(2)}, u32[]{:S(2)}) %collective-permute-start.16) | collective-permute-done | bytes 98336 | tf_op jit(solution)/shard_map/ppermute | solution.py:26
  67.6 1.3 %collective-permute-start.18 = (bf16[16,768]{1,0:T(8,128)(2,1)S(1)}, bf16[16,768]{1,0:T(8,128)(2,1)S(1)}, u32[]{:S(2)}, u32[]{:S(2)}) collective-permute-start(bf16[16,768]{1,0:T(8,128)(2,1)S(1)} %get-tuple-element.43), channel_id=1, source_target_pairs={{0,16},{1,17},{2,18},{3,19},{4,20},{5,21},{6,22},{7,23},{8,24},{9,... | collective-permute-start | bytes 73736 | tf_op jit(solution)/shard_map/ppermute | solution.py:26
  69.6 0.8 collective-permute-start.17
  70.4 3.0 %collective-permute-done.19 = bf16[16,768]{1,0:T(8,128)(2,1)S(1)} collective-permute-done((bf16[16,768]{1,0:T(8,128)(2,1)S(1)}, bf16[16,768]{1,0:T(8,128)(2,1)S(1)}, u32[]{:S(2)}, u32[]{:S(2)}) %collective-permute-start.19) | collective-permute-done | bytes 24608 | tf_op jit(solution)/shard_map/ppermute | solution.py:26
  73.4 5.0 %project_rows.1 = (bf16[16,3072]{1,0:T(8,128)(2,1)S(1)}, bf16[512,768]{1,0:T(8,128)(2,1)}) custom-call(s32[1]{0:T(128)} %bitcast.parity_ref, f32[16,768]{1,0:T(8,128)S(1)} %slice_add_fusion.mine_ref, f32[16,768]{1,0:T(8,128)S(1)} %convert_add_fusion.3.other_ref, bf16[3072,768]{1,0:T(8,128)(2,1)} %key_ref.1, ...), custom_call_target="tpu_custom_call", output_to_operand_aliasing={{1}: (6, {})} | custom-call | tf_op jit(solution)/shard_map/project_rows/pallas_call | solution.py:188
  78.5 10.6 %collective-permute-start.20 = (bf16[16,1536]{1,0:T(8,128)(2,1)S(1)}, bf16[16,1536]{1,0:T(8,128)(2,1)S(1)}, u32[]{:S(2)}, u32[]{:S(2)}) collective-permute-start(bf16[16,1536]{1,0:T(8,128)(2,1)S(1)} %pad_maximum_fusion.2), channel_id=1, source_target_pairs={{0,1},{1,0},{2,3},{3,2},{4,5},{5,4},{6,7},{7,6},{8,9},{9,8},{10,11... | collective-permute-start | bytes 147464 | tf_op jit(solution)/shard_map/ppermute | solution.py:26
  89.1 0.9 collective-permute-done.20
  90.0 5.7 %collective-permute-start.21 = (bf16[16,768]{1,0:T(8,128)(2,1)S(1)}, bf16[16,768]{1,0:T(8,128)(2,1)S(1)}, u32[]{:S(2)}, u32[]{:S(2)}) collective-permute-start(bf16[16,768]{1,0:T(8,128)(2,1)S(1)} %dynamic-slice_convert_fusion), channel_id=1, source_target_pairs={{0,2},{1,3},{2,0},{3,1},{4,6},{5,7},{6,4},{7,5},{8,10},{9,11},{10,... | collective-permute-start | bytes 73736 | tf_op jit(solution)/shard_map/ppermute | solution.py:26
  95.7 1.2 %collective-permute-done.21 = bf16[16,768]{1,0:T(8,128)(2,1)S(1)} collective-permute-done((bf16[16,768]{1,0:T(8,128)(2,1)S(1)}, bf16[16,768]{1,0:T(8,128)(2,1)S(1)}, u32[]{:S(2)}, u32[]{:S(2)}) %collective-permute-start.21) | collective-permute-done | bytes 24608 | tf_op jit(solution)/shard_map/ppermute | solution.py:26
  (36 shorter events, 5.0 us)
Async XLA Ops:
  1.5 7.1 %collective-permute-start = (bf16[16,768]{1,0:T(8,128)(2,1)S(1)}, bf16[16,768]{1,0:T(8,128)(2,1)S(1)}, u32[]{:S(2)}, u32[]{:S(2)}) collective-permute-start(bf16[16,768]{1,0:T(8,128)(2,1)S(1)} %pad_maximum_fusion.4), channel_id=1, source_target_pairs={{0,16},{1,17},{2,18},{3,19},{4,20},{5,21},{6,22},{7,23},{8,24},{9,... | collective-permute-start | bytes 73736 | tf_op jit(solution)/shard_map/ppermute | solution.py:26
  4.0 4.6 %collective-permute-start.1 = (bf16[16,768]{1,0:T(8,128)(2,1)S(1)}, bf16[16,768]{1,0:T(8,128)(2,1)S(1)}, u32[]{:S(2)}, u32[]{:S(2)}) collective-permute-start(bf16[16,768]{1,0:T(8,128)(2,1)S(1)} %pad_maximum_fusion.4), channel_id=1, source_target_pairs={{0,48},{1,49},{2,50},{3,51},{4,52},{5,53},{6,54},{7,55},{8,56},{9,... | collective-permute-start | bytes 73736 | tf_op jit(solution)/shard_map/ppermute | solution.py:26
  6.8 3.6 %collective-permute-start.2 = (bf16[16,768]{1,0:T(8,128)(2,1)S(1)}, bf16[16,768]{1,0:T(8,128)(2,1)S(1)}, u32[]{:S(2)}, u32[]{:S(2)}) collective-permute-start(bf16[16,768]{1,0:T(8,128)(2,1)S(1)} %pad_maximum_fusion.3), channel_id=1, source_target_pairs={{0,32},{1,33},{2,34},{3,35},{4,36},{5,37},{6,38},{7,39},{8,40},{9,... | collective-permute-start | bytes 73736 | tf_op jit(solution)/shard_map/ppermute | solution.py:26
  10.4 4.7 %collective-permute-start.4 = (bf16[64,768]{1,0:T(8,128)(2,1)S(1)}, bf16[64,768]{1,0:T(8,128)(2,1)S(1)}, u32[]{:S(2)}, u32[]{:S(2)}) collective-permute-start(bf16[64,768]{1,0:T(8,128)(2,1)S(1)} %pad_maximum_fusion.1), channel_id=1, source_target_pairs={{0,4},{1,65},{2,6},{3,67},{4,0},{5,69},{6,2},{7,71},{8,12},{9,73},... | collective-permute-start | bytes 294920 | tf_op jit(solution)/shard_map/ppermute | solution.py:26
  11.8 21.2 %collective-permute-start.3 = (bf16[512,768]{1,0:T(8,128)(2,1)S(1)}, bf16[512,768]{1,0:T(8,128)(2,1)S(1)}, u32[]{:S(2)}, u32[]{:S(2)}) collective-permute-start(bf16[512,768]{1,0:T(8,128)(2,1)S(1)} %pad_maximum_fusion), channel_id=1, source_target_pairs={{0,16},{1,17},{2,18},{3,19},{4,20},{5,21},{6,22},{7,23},{8,24},{9,... | collective-permute-start | bytes 2359304 | tf_op jit(solution)/shard_map/ppermute | solution.py:26
  12.3 4.8 %collective-permute-start.5 = (bf16[64,768]{1,0:T(8,128)(2,1)S(1)}, bf16[64,768]{1,0:T(8,128)(2,1)S(1)}, u32[]{:S(2)}, u32[]{:S(2)}) collective-permute-start(bf16[64,768]{1,0:T(8,128)(2,1)S(1)} %pad_maximum_fusion.1), channel_id=1, source_target_pairs={{0,12},{1,193},{2,14},{3,195},{4,8},{5,197},{6,10},{7,199},{8,4},{... | collective-permute-start | bytes 294920 | tf_op jit(solution)/shard_map/ppermute | solution.py:26
  14.3 5.0 %collective-permute-start.6 = (bf16[64,768]{1,0:T(8,128)(2,1)S(1)}, bf16[64,768]{1,0:T(8,128)(2,1)S(1)}, u32[]{:S(2)}, u32[]{:S(2)}) collective-permute-start(bf16[64,768]{1,0:T(8,128)(2,1)S(1)} %pad_maximum_fusion.1), channel_id=1, source_target_pairs={{0,8},{1,129},{2,10},{3,131},{4,12},{5,133},{6,14},{7,135},{8,0},{... | collective-permute-start | bytes 294920 | tf_op jit(solution)/shard_map/ppermute | solution.py:26
  19.3 7.0 %collective-permute-start.7 = (bf16[256,768]{1,0:T(8,128)(2,1)S(1)}, bf16[256,768]{1,0:T(8,128)(2,1)S(1)}, u32[]{:S(2)}, u32[]{:S(2)}) collective-permute-start(bf16[256,768]{1,0:T(8,128)(2,1)S(1)} %constant_dynamic-update-slice_fusion.refs_4_.refs_8_), channel_id=1, source_target_pairs={{0,64},{1,5},{2,66},{3,7},{4,68},{5,1},{6,70},{7,3},{8,72},{9,13},... | collective-permute-start | bytes 1179656 | tf_op jit(solution)/shard_map/ppermute | solution.py:26
  20.6 12.3 %collective-permute-start.8 = (bf16[256,768]{1,0:T(8,128)(2,1)S(1)}, bf16[256,768]{1,0:T(8,128)(2,1)S(1)}, u32[]{:S(2)}, u32[]{:S(2)}) collective-permute-start(bf16[256,768]{1,0:T(8,128)(2,1)S(1)} %constant_dynamic-update-slice_fusion.refs_4_.refs_8_), channel_id=1, source_target_pairs={{0,192},{1,13},{2,194},{3,15},{4,196},{5,9},{6,198},{7,11},{8,200}... | collective-permute-start | bytes 1179656 | tf_op jit(solution)/shard_map/ppermute | solution.py:26
  22.4 10.5 %collective-permute-start.9 = (bf16[256,768]{1,0:T(8,128)(2,1)S(1)}, bf16[256,768]{1,0:T(8,128)(2,1)S(1)}, u32[]{:S(2)}, u32[]{:S(2)}) collective-permute-start(bf16[256,768]{1,0:T(8,128)(2,1)S(1)} %constant_dynamic-update-slice_fusion.refs_4_.refs_8_), channel_id=1, source_target_pairs={{0,128},{1,9},{2,130},{3,11},{4,132},{5,13},{6,134},{7,15},{8,136}... | collective-permute-start | bytes 1179656 | tf_op jit(solution)/shard_map/ppermute | solution.py:26
  46.6 6.6 %collective-permute-start.10 = (bf16[256,768]{1,0:T(8,128)(2,1)S(1)}, bf16[256,768]{1,0:T(8,128)(2,1)S(1)}, u32[]{:S(2)}, u32[]{:S(2)}) collective-permute-start(bf16[256,768]{1,0:T(8,128)(2,1)S(1)} %get-tuple-element.21), channel_id=1, source_target_pairs={{0,64},{1,5},{2,66},{3,7},{4,68},{5,1},{6,70},{7,3},{8,72},{9,13},... | collective-permute-start | bytes 1179656 | tf_op jit(solution)/shard_map/ppermute | solution.py:26
  46.6 10.7 %collective-permute-start.11 = (bf16[256,768]{1,0:T(8,128)(2,1)S(1)}, bf16[256,768]{1,0:T(8,128)(2,1)S(1)}, u32[]{:S(2)}, u32[]{:S(2)}) collective-permute-start(bf16[256,768]{1,0:T(8,128)(2,1)S(1)} %get-tuple-element.22), channel_id=1, source_target_pairs={{0,192},{1,13},{2,194},{3,15},{4,196},{5,9},{6,198},{7,11},{8,200}... | collective-permute-start | bytes 1179656 | tf_op jit(solution)/shard_map/ppermute | solution.py:26
  48.4 10.6 %collective-permute-start.12 = (bf16[256,768]{1,0:T(8,128)(2,1)S(1)}, bf16[256,768]{1,0:T(8,128)(2,1)S(1)}, u32[]{:S(2)}, u32[]{:S(2)}) collective-permute-start(bf16[256,768]{1,0:T(8,128)(2,1)S(1)} %get-tuple-element.23), channel_id=1, source_target_pairs={{0,128},{1,9},{2,130},{3,11},{4,132},{5,13},{6,134},{7,15},{8,136}... | collective-permute-start | bytes 1179656 | tf_op jit(solution)/shard_map/ppermute | solution.py:26
  49.9 9.3 %collective-permute-start.13 = (bf16[512,384]{1,0:T(8,128)(2,1)S(1)}, bf16[512,384]{1,0:T(8,128)(2,1)S(1)}, u32[]{:S(2)}, u32[]{:S(2)}) collective-permute-start(bf16[512,384]{1,0:T(8,128)(2,1)S(1)} %get-tuple-element.24), channel_id=1, source_target_pairs={{0,16},{1,17},{2,18},{3,19},{4,20},{5,21},{6,22},{7,23},{8,24},{9,... | collective-permute-start | bytes 1179656 | tf_op jit(solution)/shard_map/ppermute | solution.py:26
  59.3 5.0 %collective-permute-start.14 = (bf16[64,768]{1,0:T(8,128)(2,1)S(1)}, bf16[64,768]{1,0:T(8,128)(2,1)S(1)}, u32[]{:S(2)}, u32[]{:S(2)}) collective-permute-start(bf16[64,768]{1,0:T(8,128)(2,1)S(1)} %get-tuple-element.36), channel_id=1, source_target_pairs={{0,4},{1,65},{2,6},{3,67},{4,0},{5,69},{6,2},{7,71},{8,12},{9,73},... | collective-permute-start | bytes 294920 | tf_op jit(solution)/shard_map/ppermute | solution.py:26
  59.5 6.8 %collective-permute-start.15 = (bf16[64,768]{1,0:T(8,128)(2,1)S(1)}, bf16[64,768]{1,0:T(8,128)(2,1)S(1)}, u32[]{:S(2)}, u32[]{:S(2)}) collective-permute-start(bf16[64,768]{1,0:T(8,128)(2,1)S(1)} %get-tuple-element.38), channel_id=1, source_target_pairs={{0,12},{1,193},{2,14},{3,195},{4,8},{5,197},{6,10},{7,199},{8,4},{... | collective-permute-start | bytes 294920 | tf_op jit(solution)/shard_map/ppermute | solution.py:26
  61.0 6.6 %collective-permute-start.16 = (bf16[64,768]{1,0:T(8,128)(2,1)S(1)}, bf16[64,768]{1,0:T(8,128)(2,1)S(1)}, u32[]{:S(2)}, u32[]{:S(2)}) collective-permute-start(bf16[64,768]{1,0:T(8,128)(2,1)S(1)} %get-tuple-element.37), channel_id=1, source_target_pairs={{0,8},{1,129},{2,10},{3,131},{4,12},{5,133},{6,14},{7,135},{8,0},{... | collective-permute-start | bytes 294920 | tf_op jit(solution)/shard_map/ppermute | solution.py:26
  67.6 2.8 %collective-permute-start.18 = (bf16[16,768]{1,0:T(8,128)(2,1)S(1)}, bf16[16,768]{1,0:T(8,128)(2,1)S(1)}, u32[]{:S(2)}, u32[]{:S(2)}) collective-permute-start(bf16[16,768]{1,0:T(8,128)(2,1)S(1)} %get-tuple-element.43), channel_id=1, source_target_pairs={{0,16},{1,17},{2,18},{3,19},{4,20},{5,21},{6,22},{7,23},{8,24},{9,... | collective-permute-start | bytes 73736 | tf_op jit(solution)/shard_map/ppermute | solution.py:26
  68.9 4.5 %collective-permute-start.19 = (bf16[16,768]{1,0:T(8,128)(2,1)S(1)}, bf16[16,768]{1,0:T(8,128)(2,1)S(1)}, u32[]{:S(2)}, u32[]{:S(2)}) collective-permute-start(bf16[16,768]{1,0:T(8,128)(2,1)S(1)} %get-tuple-element.44), channel_id=1, source_target_pairs={{0,48},{1,49},{2,50},{3,51},{4,52},{5,53},{6,54},{7,55},{8,56},{9,... | collective-permute-start | bytes 73736 | tf_op jit(solution)/shard_map/ppermute | solution.py:26
  69.6 3.9 %collective-permute-start.17 = (bf16[16,768]{1,0:T(8,128)(2,1)S(1)}, bf16[16,768]{1,0:T(8,128)(2,1)S(1)}, u32[]{:S(2)}, u32[]{:S(2)}) collective-permute-start(bf16[16,768]{1,0:T(8,128)(2,1)S(1)} %get-tuple-element.45), channel_id=1, source_target_pairs={{0,32},{1,33},{2,34},{3,35},{4,36},{5,37},{6,38},{7,39},{8,40},{9,... | collective-permute-start | bytes 73736 | tf_op jit(solution)/shard_map/ppermute | solution.py:26
  78.5 11.5 %collective-permute-start.20 = (bf16[16,1536]{1,0:T(8,128)(2,1)S(1)}, bf16[16,1536]{1,0:T(8,128)(2,1)S(1)}, u32[]{:S(2)}, u32[]{:S(2)}) collective-permute-start(bf16[16,1536]{1,0:T(8,128)(2,1)S(1)} %pad_maximum_fusion.2), channel_id=1, source_target_pairs={{0,1},{1,0},{2,3},{3,2},{4,5},{5,4},{6,7},{7,6},{8,9},{9,8},{10,11... | collective-permute-start | bytes 147464 | tf_op jit(solution)/shard_map/ppermute | solution.py:26
  90.0 6.9 %collective-permute-start.21 = (bf16[16,768]{1,0:T(8,128)(2,1)S(1)}, bf16[16,768]{1,0:T(8,128)(2,1)S(1)}, u32[]{:S(2)}, u32[]{:S(2)}) collective-permute-start(bf16[16,768]{1,0:T(8,128)(2,1)S(1)} %dynamic-slice_convert_fusion), channel_id=1, source_target_pairs={{0,2},{1,3},{2,0},{3,1},{4,6},{5,7},{6,4},{7,5},{8,10},{9,11},{10,... | collective-permute-start | bytes 73736 | tf_op jit(solution)/shard_map/ppermute | solution.py:26

commit v4 on v3

--- a/solution.py
+++ b/solution.py
@@ -56,71 +56,118 @@
 def attention_kernel(chunk, parity_ref, *refs):
     queries, grads_out = (refs[0], refs[2]), (refs[1], refs[3])
     keys, values = refs[4:8], refs[8:12]
-    grad_queries, parts = refs[12:14], refs[14:18]
-    probs_ref, grads_ref = refs[18:]
+    parts, grads_ref = refs[12:16], refs[16]
     rows = keys[0].shape[0]
     tokens = queries[0].shape[0]
-    for n in range(2):
-        for at in range(0, tokens, chunk):
-            q, g = queries[n][pl.ds(at, chunk), :], grads_out[n][pl.ds(at, chunk), :]
-            some = pl.ds(n * tokens + at, chunk)
-            scores = [dot(k[...], q, NT) for k in keys]
-            top = functools.reduce(
-                jnp.maximum, [jnp.max(s, axis=0, keepdims=True) for s in scores]
-            )
-            raised = [jnp.exp2((s - top) * (SCALE * math.log2(math.e))) for s in scores]
-            inverse = 1.0 / sum(jnp.sum(e, axis=0, keepdims=True) for e in raised)
-            probs = [e * inverse for e in raised]
-            grad_probs = [dot(v[...], g, NT) for v in values]
-            delta = sum(
-                jnp.sum(p * d, axis=0, keepdims=True) for p, d in zip(probs, grad_probs)
-            )
-            for i, (p, d) in enumerate(zip(probs, grad_probs)):
-                here = pl.ds(i * rows, rows)
-                probs_ref[here, some] = narrow(p)
-                grads_ref[here, some] = narrow(p * (d - delta))
-    spans = [pl.ds(n * tokens, tokens) for n in range(2)]
+    power = SCALE * math.log2(math.e)
+    key_sums, value_sums = [0.0] * 4, [0.0] * 4
+
+    def products(n, at):
+        q, g = queries[n][pl.ds(at, chunk), :], grads_out[n][pl.ds(at, chunk), :]
+        return q, g, [dot(k[...], q, NT) for k in keys], [dot(v[...], g, NT) for v in values]
+
+    def softmax(scores, grad_probs):
+        top = functools.reduce(jnp.maximum, [jnp.max(s, axis=0, keepdims=True) for s in scores])
+        raised = [jnp.exp2((s - top) * power) for s in scores]
+        inverse = 1.0 / sum(jnp.sum(e, axis=0, keepdims=True) for e in raised)
+        probs = [e * inverse for e in raised]
+        delta = sum(jnp.sum(p * d, axis=0, keepdims=True) for p, d in zip(probs, grad_probs))
+        return [narrow(p) for p in probs], [
+            narrow(p * (d - delta)) for p, d in zip(probs, grad_probs)
+        ]
+
+    def add(n, at, q, g, probs, grads):
+        for i in range(4):
+            grads_ref[pl.ds(i * rows, rows), pl.ds(n * tokens + at, chunk)] = grads[i]
+            key_sums[i] += dot(grads[i], q)
+            value_sums[i] += dot(probs[i], g)
+
+    places = [(n, at) for n in range(2) for at in range(0, tokens, chunk)]
+    ahead, behind = products(*places[0]), None
+    for i, place in enumerate(places):
+        q, g, scores, grad_probs = ahead
+        if i + 1 < len(places):
+            ahead = products(*places[i + 1])
+        probs, grads = softmax(scores, grad_probs)
+        if behind is not None:
+            add(*behind)
+        behind = (*place, q, g, probs, grads)
+    add(*behind)
     for i in range(4):
-        here = pl.ds(i * rows, rows)
-        dk = sum(dot(grads_ref[here, t], q[...]) for t, q in zip(spans, queries))
-        dv = sum(dot(probs_ref[here, t], g[...]) for t, g in zip(spans, grads_out))
-        parts[i][:, :HD] = narrow(dk * SCALE)
-        parts[i][:, HD:] = narrow(dv)
-    for t, out_ref in zip(spans, grad_queries):
-        dq = sum(dot(k[...], grads_ref[pl.ds(i * rows, rows), t], TN) for i, k in enumerate(keys))
-        out_ref[...] = narrow(dq.T * SCALE)
-
-
-def attention(parity, queries, grad_out, far, blocks, result_shape):
-    tokens, width = queries.shape
+        parts[i][:, :HD] = narrow(key_sums[i] * SCALE)
+        parts[i][:, HD:] = narrow(value_sums[i])
+
+
+def attention(parity, queries, grad_out, far, blocks):
+    tokens = queries.shape[0]
     rows, columns = blocks[0].shape
-    heads = width // HD
-    placed = pl.BlockSpec((tokens, HD), lambda h, parity: (0, parity[0] * heads + h))
-    token = pl.BlockSpec((tokens, HD), lambda h, parity: (0, h))
-    token_second = pl.BlockSpec((tokens, HD), lambda h, parity: (0, heads + h))
+    heads = columns // (2 * HD)
+    own = pl.BlockSpec((tokens, HD), lambda h, parity: (0, h))
+    first = pl.BlockSpec((tokens, HD), lambda h, parity: (0, h))
+    second = pl.BlockSpec((tokens, HD), lambda h, parity: (0, heads + h))
     key = pl.BlockSpec((rows, HD), lambda h, parity: (0, h))
     value = pl.BlockSpec((rows, HD), lambda h, parity: (0, heads + h))
     part = pl.BlockSpec((rows, 2 * HD), lambda h, parity: (0, h))
+    grads = pl.BlockSpec((4 * rows, 2 * tokens), lambda h, parity: (h, 0))
     scores = heads * 2 * tokens * 4 * rows
-    shapes = [result_shape, queries.shape] + [b.shape for b in blocks]
+    shapes = [b.shape for b in blocks] + [(heads * 4 * rows, 2 * tokens)]
     return pl.pallas_call(
-        functools.partial(attention_kernel, tokens // 2),
+        functools.partial(attention_kernel, tokens // 4),
         grid_spec=pltpu.PrefetchScalarGridSpec(
             num_scalar_prefetch=1,
             grid=(heads,),
-            in_specs=[token] * 2 + [token, token_second] + [key] * 4 + [value] * 4,
-            out_specs=[placed, token] + [part] * 4,
-            scratch_shapes=[pltpu.VMEM((4 * rows, 2 * tokens), jnp.bfloat16)] * 2,
+            in_specs=[own] * 2 + [first, second] + [key] * 4 + [value] * 4,
+            out_specs=[part] * 4 + [grads],
         ),
         out_shape=[jax.ShapeDtypeStruct(shape, jnp.bfloat16) for shape in shapes],
         compiler_params=pltpu.CompilerParams(vmem_limit_bytes=24 * 2**20),
         cost_estimate=pl.CostEstimate(
-            flops=10 * HD * scores,
-            bytes_accessed=2 * (6 * tokens * heads * HD + 8 * rows * columns),
+            flops=8 * HD * scores,
+            bytes_accessed=2 * (4 * tokens * heads * HD + 8 * rows * columns + scores),
             transcendentals=scores,
         ),
         name="attention_grads",
     )(parity, queries, grad_out, far, far, *blocks, *blocks)
+
+
+def query_kernel(parity_ref, *refs):
+    keys, grads_ref, near_ref, far_ref = refs[0:4], refs[4], refs[5], refs[6]
+    rows = keys[0].shape[0]
+    tokens = near_ref.shape[0]
+    for n, out_ref in enumerate((near_ref, far_ref)):
+        some = pl.ds(n * tokens, tokens)
+        dq = sum(dot(k[...], grads_ref[pl.ds(i * rows, rows), some], TN) for i, k in enumerate(keys))
+        out_ref[...] = narrow(dq.T * SCALE)
+
+
+def query_grads(parity, blocks, grad_scores, shape):
+    tokens, width = shape
+    rows, columns = blocks[0].shape
+    heads = columns // (2 * HD)
+    return pl.pallas_call(
+        query_kernel,
+        grid_spec=pltpu.PrefetchScalarGridSpec(
+            num_scalar_prefetch=1,
+            grid=(heads,),
+            in_specs=[pl.BlockSpec((rows, HD), lambda h, parity: (0, h))] * 4
+            + [pl.BlockSpec((4 * rows, 2 * tokens), lambda h, parity: (h, 0))],
+            out_specs=[
+                pl.BlockSpec((tokens, HD), lambda h, parity: (0, parity[0] * heads + h)),
+                pl.BlockSpec((tokens, HD), lambda h, parity: (0, h)),
+            ],
+        ),
+        out_shape=[
+            jax.ShapeDtypeStruct(shape, jnp.bfloat16),
+            jax.ShapeDtypeStruct((tokens, heads * HD), jnp.bfloat16),
+        ],
+        compiler_params=pltpu.CompilerParams(vmem_limit_bytes=16 * 2**20),
+        cost_estimate=pl.CostEstimate(
+            flops=4 * HD * heads * tokens * 4 * rows,
+            bytes_accessed=2 * heads * tokens * 8 * rows,
+            transcendentals=0,
+        ),
+        name="query_grads",
+    )(parity, *blocks, grad_scores)
 
 
 def project_kernel(
@@ -221,7 +268,8 @@
     rows = join(*gather(rows, LATE))
     blocks = gather(rows, EARLY)
 
-    grad_queries, grad_far, *parts = attention(spot, *near, far, blocks, queries.shape)
+    *parts, grad_scores = attention(spot, *near, far, blocks)
+    grad_queries, grad_far = query_grads(spot, blocks, grad_scores, queries.shape)
 
     total = scatter_sum(parts, EARLY)
     grad_far = swap(grad_far, (Z, Z))

time: 97.7 us -> 96.3 us (0.986)
  waiting for transfers between devices: 34.1 us -> 31.6 us
  Pallas kernels: 18.7 us -> 19.7 us
    ppermute x22, waiting for transfers between devices: 34.1 us -> 31.6 us  [swap(): return lax.ppermute(block, ('seq', 'tensor'), pairs)]
    pallas_call x1 -> x2, Pallas kernels: 13.6 us -> 14.6 us  [the longest x1 12.1 us: attention(): pl.pallas_call(functools.partial(attention_kernel, tokens // 4), grid_spe...]
  transfers between devices with their start and end apart: 22 -> 22, of which waited for: 14 -> 14; matrix products, arithmetic and copies ran while one was open for 2% -> 2% of each run, Pallas kernels for 0% -> 3%
where the time goes in v4:
time: 96.3 us; the launch traced here: 96.1 us
  starting transfers between devices  40.6 us (42%)
  waiting for transfers between devices  31.6 us (33%)
  Pallas kernels  19.7 us (20%)
  local copies, waits for them, and re-layouts  2.38 us (2%)
  other arithmetic  1.01 us (1%)
    ppermute x22, starting transfers between devices, swap(): return lax.ppermute(block, ('seq', 'tensor'), pairs)  40.6 us
    ppermute x22, waiting for transfers between devices, swap(): return lax.ppermute(block, ('seq', 'tensor'), pairs)  31.6 us
    pallas_call x1, Pallas kernels, attention(): pl.pallas_call(functools.partial(attention_kernel, tokens // 4), grid_spe...  12.1 us
    pallas_call x1, Pallas kernels, project(): pl.pallas_call(functools.partial(project_kernel, blocks), in_specs=[pl.Bl...  5.02 us
    pallas_call x1, Pallas kernels, query_grads(): pl.pallas_call(query_kernel, grid_spec=pltpu.PrefetchScalarGridSpec(num_s...  2.52 us
    dynamic_slice x2, local copies, waits for them, and re-layouts, columns(): return lax.dynamic_slice_in_dim(array, which * half, half, axis=1)  2.28 us
  transfers between devices with their start and end apart: 22, of which 14 were waited for; matrix products, arithmetic and copies ran while one was open for 2% of the time, Pallas kernels for 3%

profile of v4, /device:TPU:1, one launch (start us, length us, event | category | flops | bytes accessed | tf_op | source)
XLA Modules:
  0.0 96.1 jit_solution(1555366422650727573)
XLA Ops:
  1.5 2.6 %collective-permute-start = (bf16[16,768]{1,0:T(8,128)(2,1)S(1)}, bf16[16,768]{1,0:T(8,128)(2,1)S(1)}, u32[]{:S(2)}, u32[]{:S(2)}) collective-permute-start(bf16[16,768]{1,0:T(8,128)(2,1)S(1)} %pad_maximum_fusion.4), channel_id=1, source_target_pairs={{0,16},{1,17},{2,18},{3,19},{4,20},{5,21},{6,22},{7,23},{8,24},{9,... | collective-permute-start | bytes 73736 | tf_op jit(solution)/shard_map/ppermute | solution.py:26
  4.0 2.8 %collective-permute-start.1 = (bf16[16,768]{1,0:T(8,128)(2,1)S(1)}, bf16[16,768]{1,0:T(8,128)(2,1)S(1)}, u32[]{:S(2)}, u32[]{:S(2)}) collective-permute-start(bf16[16,768]{1,0:T(8,128)(2,1)S(1)} %pad_maximum_fusion.4), channel_id=1, source_target_pairs={{0,48},{1,49},{2,50},{3,51},{4,52},{5,53},{6,54},{7,55},{8,56},{9,... | collective-permute-start | bytes 73736 | tf_op jit(solution)/shard_map/ppermute | solution.py:26
  7.0 1.5 %constant_dynamic-slice_fusion.4 = (bf16[512,384]{1,0:T(8,128)(2,1)S(1)}, bf16[512,384]{1,0:T(8,128)(2,1)S(1)}, bf16[512,384]{1,0:T(8,128)(2,1)S(1)}, bf16[512,384]{1,0:T(8,128)(2,1)S(1)}) fusion(bf16[512,768]{1,0:T(8,128)(2,1)} %param.9, s32[]{:T(128)S(6)} %select_n.51, s32[]{:T(128)S(6)} %select_n.50, bf16[512,768]{1,0:T(8,128)(2,1)} %param.6), kind=kLoop, calls=%fused_computation.20 | loop fusion | bytes 3145736 | tf_op jit(solution)/shard_map/dynamic_slice | solution.py:256
  8.6 1.8 %collective-permute-done.2 = bf16[16,768]{1,0:T(8,128)(2,1)S(1)} collective-permute-done((bf16[16,768]{1,0:T(8,128)(2,1)S(1)}, bf16[16,768]{1,0:T(8,128)(2,1)S(1)}, u32[]{:S(2)}, u32[]{:S(2)}) %collective-permute-start.2) | collective-permute-done | bytes 24608 | tf_op jit(solution)/shard_map/ppermute | solution.py:26
  10.4 1.4 %collective-permute-start.4 = (bf16[64,768]{1,0:T(8,128)(2,1)S(1)}, bf16[64,768]{1,0:T(8,128)(2,1)S(1)}, u32[]{:S(2)}, u32[]{:S(2)}) collective-permute-start(bf16[64,768]{1,0:T(8,128)(2,1)S(1)} %pad_maximum_fusion.1), channel_id=1, source_target_pairs={{0,4},{1,65},{2,6},{3,67},{4,0},{5,69},{6,2},{7,71},{8,12},{9,73},... | collective-permute-start | bytes 294920 | tf_op jit(solution)/shard_map/ppermute | solution.py:26
  12.3 2.0 %collective-permute-start.5 = (bf16[64,768]{1,0:T(8,128)(2,1)S(1)}, bf16[64,768]{1,0:T(8,128)(2,1)S(1)}, u32[]{:S(2)}, u32[]{:S(2)}) collective-permute-start(bf16[64,768]{1,0:T(8,128)(2,1)S(1)} %pad_maximum_fusion.1), channel_id=1, source_target_pairs={{0,12},{1,193},{2,14},{3,195},{4,8},{5,197},{6,10},{7,199},{8,4},{... | collective-permute-start | bytes 294920 | tf_op jit(solution)/shard_map/ppermute | solution.py:26
  15.2 1.9 %collective-permute-done.5 = bf16[64,768]{1,0:T(8,128)(2,1)S(1)} collective-permute-done((bf16[64,768]{1,0:T(8,128)(2,1)S(1)}, bf16[64,768]{1,0:T(8,128)(2,1)S(1)}, u32[]{:S(2)}, u32[]{:S(2)}) %collective-permute-start.5) | collective-permute-done | bytes 98336 | tf_op jit(solution)/shard_map/ppermute | solution.py:26
  17.1 2.2 %collective-permute-done.6 = bf16[64,768]{1,0:T(8,128)(2,1)S(1)} collective-permute-done((bf16[64,768]{1,0:T(8,128)(2,1)S(1)}, bf16[64,768]{1,0:T(8,128)(2,1)S(1)}, u32[]{:S(2)}, u32[]{:S(2)}) %collective-permute-start.6) | collective-permute-done | bytes 98336 | tf_op jit(solution)/shard_map/ppermute | solution.py:26
  19.3 1.3 %collective-permute-start.7 = (bf16[256,768]{1,0:T(8,128)(2,1)S(1)}, bf16[256,768]{1,0:T(8,128)(2,1)S(1)}, u32[]{:S(2)}, u32[]{:S(2)}) collective-permute-start(bf16[256,768]{1,0:T(8,128)(2,1)S(1)} %constant_dynamic-update-slice_fusion.refs_4_.refs_8_.refs_0_), channel_id=1, source_target_pairs={{0,64},{1,5},{2,66},{3,7},{4,68},{5,1},{6,70},{7,3},{8,72},{9,13},... | collective-permute-start | bytes 1179656 | tf_op jit(solution)/shard_map/ppermute | solution.py:26
  20.6 1.8 %collective-permute-start.8 = (bf16[256,768]{1,0:T(8,128)(2,1)S(1)}, bf16[256,768]{1,0:T(8,128)(2,1)S(1)}, u32[]{:S(2)}, u32[]{:S(2)}) collective-permute-start(bf16[256,768]{1,0:T(8,128)(2,1)S(1)} %constant_dynamic-update-slice_fusion.refs_4_.refs_8_.refs_0_), channel_id=1, source_target_pairs={{0,192},{1,13},{2,194},{3,15},{4,196},{5,9},{6,198},{7,11},{8,200}... | collective-permute-start | bytes 1179656 | tf_op jit(solution)/shard_map/ppermute | solution.py:26
  23.1 3.3 %collective-permute-done.7.refs_5_.refs_9_.refs_1_ = bf16[256,768]{1,0:T(8,128)(2,1)S(1)} collective-permute-done((bf16[256,768]{1,0:T(8,128)(2,1)S(1)}, bf16[256,768]{1,0:T(8,128)(2,1)S(1)}, u32[]{:S(2)}, u32[]{:S(2)}) %collective-permute-start.7) | collective-permute-done | bytes 393248 | tf_op jit(solution)/shard_map/ppermute | solution.py:26
  26.3 6.6 %collective-permute-done.8.refs_6_.refs_10_.refs_2_ = bf16[256,768]{1,0:T(8,128)(2,1)S(1)} collective-permute-done((bf16[256,768]{1,0:T(8,128)(2,1)S(1)}, bf16[256,768]{1,0:T(8,128)(2,1)S(1)}, u32[]{:S(2)}, u32[]{:S(2)}) %collective-permute-start.8) | collective-permute-done | bytes 393248 | tf_op jit(solution)/shard_map/ppermute | solution.py:26
  33.0 12.1 %attention_grads.1 = (bf16[256,768]{1,0:T(8,128)(2,1)S(1)}, bf16[256,768]{1,0:T(8,128)(2,1)S(1)}, bf16[256,768]{1,0:T(8,128)(2,1)S(1)}, bf16[256,768]{1,0:T(8,128)(2,1)S(1)}, bf16[3072,1024]{1,0:T(8,128)(2,1)S(1)}) custom-call(s32[1]{0:T(128)} %bitcast.parity_ref, bf16[512,384]{1,0:T(8,128)(2,1)S(1)} %get-tuple-element.17.refs_0_, ...), custom_call_target="tpu_custom_call" | custom-call | flops 3221225472 | bytes 11010048 | tf_op jit(solution)/shard_map/attention_grads/pallas_call | solution.py:114
  45.2 1.9 %collective-permute-start.11 = (bf16[256,768]{1,0:T(8,128)(2,1)S(1)}, bf16[256,768]{1,0:T(8,128)(2,1)S(1)}, u32[]{:S(2)}, u32[]{:S(2)}) collective-permute-start(bf16[256,768]{1,0:T(8,128)(2,1)S(1)} %get-tuple-element.23), channel_id=1, source_target_pairs={{0,192},{1,13},{2,194},{3,15},{4,196},{5,9},{6,198},{7,11},{8,200}... | collective-permute-start | bytes 1179656 | tf_op jit(solution)/shard_map/ppermute | solution.py:26
  47.1 1.3 %collective-permute-start.12 = (bf16[256,768]{1,0:T(8,128)(2,1)S(1)}, bf16[256,768]{1,0:T(8,128)(2,1)S(1)}, u32[]{:S(2)}, u32[]{:S(2)}) collective-permute-start(bf16[256,768]{1,0:T(8,128)(2,1)S(1)} %get-tuple-element.24), channel_id=1, source_target_pairs={{0,128},{1,9},{2,130},{3,11},{4,132},{5,13},{6,134},{7,15},{8,136}... | collective-permute-start | bytes 1179656 | tf_op jit(solution)/shard_map/ppermute | solution.py:26
  48.4 2.5 %query_grads.1 = (bf16[512,768]{1,0:T(8,128)(2,1)}, bf16[512,384]{1,0:T(8,128)(2,1)S(1)}) custom-call(s32[1]{0:T(128)} %bitcast.parity_ref, bf16[256,768]{1,0:T(8,128)(2,1)S(1)} %constant_dynamic-update-slice_fusion.refs_4_.refs_8_.refs_0_, bf16[256,768]{1,0:T(8,128)(2,1)S(1)} %collective-permute-done.7.refs_5_.refs_9_.refs_1_, ...), custom_call_target="tpu_custom_call" | custom-call | flops 805306368 | bytes 6291456 | tf_op jit(solution)/shard_map/query_grads/pallas_call | solution.py:147
  51.0 0.9 collective-permute-start.13
  51.9 4.1 %collective-permute-done.11 = bf16[256,768]{1,0:T(8,128)(2,1)S(1)} collective-permute-done((bf16[256,768]{1,0:T(8,128)(2,1)S(1)}, bf16[256,768]{1,0:T(8,128)(2,1)S(1)}, u32[]{:S(2)}, u32[]{:S(2)}) %collective-permute-start.11) | collective-permute-done | bytes 393248 | tf_op jit(solution)/shard_map/ppermute | solution.py:26
  56.0 1.5 %collective-permute-done.12 = bf16[256,768]{1,0:T(8,128)(2,1)S(1)} collective-permute-done((bf16[256,768]{1,0:T(8,128)(2,1)S(1)}, bf16[256,768]{1,0:T(8,128)(2,1)S(1)}, u32[]{:S(2)}, u32[]{:S(2)}) %collective-permute-start.12) | collective-permute-done | bytes 393248 | tf_op jit(solution)/shard_map/ppermute | solution.py:26
  58.2 1.5 %collective-permute-start.15 = (bf16[64,768]{1,0:T(8,128)(2,1)S(1)}, bf16[64,768]{1,0:T(8,128)(2,1)S(1)}, u32[]{:S(2)}, u32[]{:S(2)}) collective-permute-start(bf16[64,768]{1,0:T(8,128)(2,1)S(1)} %get-tuple-element.40), channel_id=1, source_target_pairs={{0,12},{1,193},{2,14},{3,195},{4,8},{5,197},{6,10},{7,199},{8,4},{... | collective-permute-start | bytes 294920 | tf_op jit(solution)/shard_map/ppermute | solution.py:26
  59.7 1.6 %collective-permute-start.16 = (bf16[64,768]{1,0:T(8,128)(2,1)S(1)}, bf16[64,768]{1,0:T(8,128)(2,1)S(1)}, u32[]{:S(2)}, u32[]{:S(2)}) collective-permute-start(bf16[64,768]{1,0:T(8,128)(2,1)S(1)} %get-tuple-element.39), channel_id=1, source_target_pairs={{0,8},{1,129},{2,10},{3,131},{4,12},{5,133},{6,14},{7,135},{8,0},{... | collective-permute-start | bytes 294920 | tf_op jit(solution)/shard_map/ppermute | solution.py:26
  61.3 1.6 %collective-permute-done.14 = bf16[64,768]{1,0:T(8,128)(2,1)S(1)} collective-permute-done((bf16[64,768]{1,0:T(8,128)(2,1)S(1)}, bf16[64,768]{1,0:T(8,128)(2,1)S(1)}, u32[]{:S(2)}, u32[]{:S(2)}) %collective-permute-start.14) | collective-permute-done | bytes 98336 | tf_op jit(solution)/shard_map/ppermute | solution.py:26
  62.9 2.0 %collective-permute-done.15 = bf16[64,768]{1,0:T(8,128)(2,1)S(1)} collective-permute-done((bf16[64,768]{1,0:T(8,128)(2,1)S(1)}, bf16[64,768]{1,0:T(8,128)(2,1)S(1)}, u32[]{:S(2)}, u32[]{:S(2)}) %collective-permute-start.15) | collective-permute-done | bytes 98336 | tf_op jit(solution)/shard_map/ppermute | solution.py:26
  64.9 1.3 %collective-permute-done.16 = bf16[64,768]{1,0:T(8,128)(2,1)S(1)} collective-permute-done((bf16[64,768]{1,0:T(8,128)(2,1)S(1)}, bf16[64,768]{1,0:T(8,128)(2,1)S(1)}, u32[]{:S(2)}, u32[]{:S(2)}) %collective-permute-start.16) | collective-permute-done | bytes 98336 | tf_op jit(solution)/shard_map/ppermute | solution.py:26
  66.2 1.3 %collective-permute-start.18 = (bf16[16,768]{1,0:T(8,128)(2,1)S(1)}, bf16[16,768]{1,0:T(8,128)(2,1)S(1)}, u32[]{:S(2)}, u32[]{:S(2)}) collective-permute-start(bf16[16,768]{1,0:T(8,128)(2,1)S(1)} %get-tuple-element.45), channel_id=1, source_target_pairs={{0,16},{1,17},{2,18},{3,19},{4,20},{5,21},{6,22},{7,23},{8,24},{9,... | collective-permute-start | bytes 73736 | tf_op jit(solution)/shard_map/ppermute | solution.py:26
  68.1 0.8 collective-permute-start.17
  69.0 3.0 %collective-permute-done.19 = bf16[16,768]{1,0:T(8,128)(2,1)S(1)} collective-permute-done((bf16[16,768]{1,0:T(8,128)(2,1)S(1)}, bf16[16,768]{1,0:T(8,128)(2,1)S(1)}, u32[]{:S(2)}, u32[]{:S(2)}) %collective-permute-start.19) | collective-permute-done | bytes 24608 | tf_op jit(solution)/shard_map/ppermute | solution.py:26
  72.0 5.0 %project_rows.1 = (bf16[16,3072]{1,0:T(8,128)(2,1)S(1)}, bf16[512,768]{1,0:T(8,128)(2,1)}) custom-call(s32[1]{0:T(128)} %bitcast.parity_ref, f32[16,768]{1,0:T(8,128)S(1)} %slice_add_fusion.mine_ref, f32[16,768]{1,0:T(8,128)S(1)} %convert_add_fusion.3.other_ref, bf16[3072,768]{1,0:T(8,128)(2,1)} %key_ref.1, ...), custom_call_target="tpu_custom_call", output_to_operand_aliasing={{1}: (6, {})} | custom-call | tf_op jit(solution)/shard_map/project_rows/pallas_call | solution.py:235
  77.1 10.6 %collective-permute-start.20 = (bf16[16,1536]{1,0:T(8,128)(2,1)S(1)}, bf16[16,1536]{1,0:T(8,128)(2,1)S(1)}, u32[]{:S(2)}, u32[]{:S(2)}) collective-permute-start(bf16[16,1536]{1,0:T(8,128)(2,1)S(1)} %pad_maximum_fusion.2), channel_id=1, source_target_pairs={{0,1},{1,0},{2,3},{3,2},{4,5},{5,4},{6,7},{7,6},{8,9},{9,8},{10,11... | collective-permute-start | bytes 147464 | tf_op jit(solution)/shard_map/ppermute | solution.py:26
  87.7 0.9 collective-permute-done.20
  88.6 5.7 %collective-permute-start.21 = (bf16[16,768]{1,0:T(8,128)(2,1)S(1)}, bf16[16,768]{1,0:T(8,128)(2,1)S(1)}, u32[]{:S(2)}, u32[]{:S(2)}) collective-permute-start(bf16[16,768]{1,0:T(8,128)(2,1)S(1)} %dynamic-slice_convert_fusion), channel_id=1, source_target_pairs={{0,2},{1,3},{2,0},{3,1},{4,6},{5,7},{6,4},{7,5},{8,10},{9,11},{10,... | collective-permute-start | bytes 73736 | tf_op jit(solution)/shard_map/ppermute | solution.py:26
  94.3 1.2 %collective-permute-done.21 = bf16[16,768]{1,0:T(8,128)(2,1)S(1)} collective-permute-done((bf16[16,768]{1,0:T(8,128)(2,1)S(1)}, bf16[16,768]{1,0:T(8,128)(2,1)S(1)}, u32[]{:S(2)}, u32[]{:S(2)}) %collective-permute-start.21) | collective-permute-done | bytes 24608 | tf_op jit(solution)/shard_map/ppermute | solution.py:26
  (37 shorter events, 5.2 us)
Async XLA Ops:
  1.5 7.1 %collective-permute-start = (bf16[16,768]{1,0:T(8,128)(2,1)S(1)}, bf16[16,768]{1,0:T(8,128)(2,1)S(1)}, u32[]{:S(2)}, u32[]{:S(2)}) collective-permute-start(bf16[16,768]{1,0:T(8,128)(2,1)S(1)} %pad_maximum_fusion.4), channel_id=1, source_target_pairs={{0,16},{1,17},{2,18},{3,19},{4,20},{5,21},{6,22},{7,23},{8,24},{9,... | collective-permute-start | bytes 73736 | tf_op jit(solution)/shard_map/ppermute | solution.py:26
  4.0 4.6 %collective-permute-start.1 = (bf16[16,768]{1,0:T(8,128)(2,1)S(1)}, bf16[16,768]{1,0:T(8,128)(2,1)S(1)}, u32[]{:S(2)}, u32[]{:S(2)}) collective-permute-start(bf16[16,768]{1,0:T(8,128)(2,1)S(1)} %pad_maximum_fusion.4), channel_id=1, source_target_pairs={{0,48},{1,49},{2,50},{3,51},{4,52},{5,53},{6,54},{7,55},{8,56},{9,... | collective-permute-start | bytes 73736 | tf_op jit(solution)/shard_map/ppermute | solution.py:26
  6.8 3.6 %collective-permute-start.2 = (bf16[16,768]{1,0:T(8,128)(2,1)S(1)}, bf16[16,768]{1,0:T(8,128)(2,1)S(1)}, u32[]{:S(2)}, u32[]{:S(2)}) collective-permute-start(bf16[16,768]{1,0:T(8,128)(2,1)S(1)} %pad_maximum_fusion.3), channel_id=1, source_target_pairs={{0,32},{1,33},{2,34},{3,35},{4,36},{5,37},{6,38},{7,39},{8,40},{9,... | collective-permute-start | bytes 73736 | tf_op jit(solution)/shard_map/ppermute | solution.py:26
  10.4 4.7 %collective-permute-start.4 = (bf16[64,768]{1,0:T(8,128)(2,1)S(1)}, bf16[64,768]{1,0:T(8,128)(2,1)S(1)}, u32[]{:S(2)}, u32[]{:S(2)}) collective-permute-start(bf16[64,768]{1,0:T(8,128)(2,1)S(1)} %pad_maximum_fusion.1), channel_id=1, source_target_pairs={{0,4},{1,65},{2,6},{3,67},{4,0},{5,69},{6,2},{7,71},{8,12},{9,73},... | collective-permute-start | bytes 294920 | tf_op jit(solution)/shard_map/ppermute | solution.py:26
  11.8 21.2 %collective-permute-start.3 = (bf16[512,768]{1,0:T(8,128)(2,1)S(1)}, bf16[512,768]{1,0:T(8,128)(2,1)S(1)}, u32[]{:S(2)}, u32[]{:S(2)}) collective-permute-start(bf16[512,768]{1,0:T(8,128)(2,1)S(1)} %pad_maximum_fusion), channel_id=1, source_target_pairs={{0,16},{1,17},{2,18},{3,19},{4,20},{5,21},{6,22},{7,23},{8,24},{9,... | collective-permute-start | bytes 2359304 | tf_op jit(solution)/shard_map/ppermute | solution.py:26
  12.3 4.8 %collective-permute-start.5 = (bf16[64,768]{1,0:T(8,128)(2,1)S(1)}, bf16[64,768]{1,0:T(8,128)(2,1)S(1)}, u32[]{:S(2)}, u32[]{:S(2)}) collective-permute-start(bf16[64,768]{1,0:T(8,128)(2,1)S(1)} %pad_maximum_fusion.1), channel_id=1, source_target_pairs={{0,12},{1,193},{2,14},{3,195},{4,8},{5,197},{6,10},{7,199},{8,4},{... | collective-permute-start | bytes 294920 | tf_op jit(solution)/shard_map/ppermute | solution.py:26
  14.3 5.0 %collective-permute-start.6 = (bf16[64,768]{1,0:T(8,128)(2,1)S(1)}, bf16[64,768]{1,0:T(8,128)(2,1)S(1)}, u32[]{:S(2)}, u32[]{:S(2)}) collective-permute-start(bf16[64,768]{1,0:T(8,128)(2,1)S(1)} %pad_maximum_fusion.1), channel_id=1, source_target_pairs={{0,8},{1,129},{2,10},{3,131},{4,12},{5,133},{6,14},{7,135},{8,0},{... | collective-permute-start | bytes 294920 | tf_op jit(solution)/shard_map/ppermute | solution.py:26
  19.3 7.0 %collective-permute-start.7 = (bf16[256,768]{1,0:T(8,128)(2,1)S(1)}, bf16[256,768]{1,0:T(8,128)(2,1)S(1)}, u32[]{:S(2)}, u32[]{:S(2)}) collective-permute-start(bf16[256,768]{1,0:T(8,128)(2,1)S(1)} %constant_dynamic-update-slice_fusion.refs_4_.refs_8_.refs_0_), channel_id=1, source_target_pairs={{0,64},{1,5},{2,66},{3,7},{4,68},{5,1},{6,70},{7,3},{8,72},{9,13},... | collective-permute-start | bytes 1179656 | tf_op jit(solution)/shard_map/ppermute | solution.py:26
  20.6 12.3 %collective-permute-start.8 = (bf16[256,768]{1,0:T(8,128)(2,1)S(1)}, bf16[256,768]{1,0:T(8,128)(2,1)S(1)}, u32[]{:S(2)}, u32[]{:S(2)}) collective-permute-start(bf16[256,768]{1,0:T(8,128)(2,1)S(1)} %constant_dynamic-update-slice_fusion.refs_4_.refs_8_.refs_0_), channel_id=1, source_target_pairs={{0,192},{1,13},{2,194},{3,15},{4,196},{5,9},{6,198},{7,11},{8,200}... | collective-permute-start | bytes 1179656 | tf_op jit(solution)/shard_map/ppermute | solution.py:26
  22.4 10.5 %collective-permute-start.9 = (bf16[256,768]{1,0:T(8,128)(2,1)S(1)}, bf16[256,768]{1,0:T(8,128)(2,1)S(1)}, u32[]{:S(2)}, u32[]{:S(2)}) collective-permute-start(bf16[256,768]{1,0:T(8,128)(2,1)S(1)} %constant_dynamic-update-slice_fusion.refs_4_.refs_8_.refs_0_), channel_id=1, source_target_pairs={{0,128},{1,9},{2,130},{3,11},{4,132},{5,13},{6,134},{7,15},{8,136}... | collective-permute-start | bytes 1179656 | tf_op jit(solution)/shard_map/ppermute | solution.py:26
  45.1 6.8 %collective-permute-start.10 = (bf16[256,768]{1,0:T(8,128)(2,1)S(1)}, bf16[256,768]{1,0:T(8,128)(2,1)S(1)}, u32[]{:S(2)}, u32[]{:S(2)}) collective-permute-start(bf16[256,768]{1,0:T(8,128)(2,1)S(1)} %get-tuple-element.22), channel_id=1, source_target_pairs={{0,64},{1,5},{2,66},{3,7},{4,68},{5,1},{6,70},{7,3},{8,72},{9,13},... | collective-permute-start | bytes 1179656 | tf_op jit(solution)/shard_map/ppermute | solution.py:26
  45.2 10.8 %collective-permute-start.11 = (bf16[256,768]{1,0:T(8,128)(2,1)S(1)}, bf16[256,768]{1,0:T(8,128)(2,1)S(1)}, u32[]{:S(2)}, u32[]{:S(2)}) collective-permute-start(bf16[256,768]{1,0:T(8,128)(2,1)S(1)} %get-tuple-element.23), channel_id=1, source_target_pairs={{0,192},{1,13},{2,194},{3,15},{4,196},{5,9},{6,198},{7,11},{8,200}... | collective-permute-start | bytes 1179656 | tf_op jit(solution)/shard_map/ppermute | solution.py:26
  47.1 10.5 %collective-permute-start.12 = (bf16[256,768]{1,0:T(8,128)(2,1)S(1)}, bf16[256,768]{1,0:T(8,128)(2,1)S(1)}, u32[]{:S(2)}, u32[]{:S(2)}) collective-permute-start(bf16[256,768]{1,0:T(8,128)(2,1)S(1)} %get-tuple-element.24), channel_id=1, source_target_pairs={{0,128},{1,9},{2,130},{3,11},{4,132},{5,13},{6,134},{7,15},{8,136}... | collective-permute-start | bytes 1179656 | tf_op jit(solution)/shard_map/ppermute | solution.py:26
  51.0 6.9 %collective-permute-start.13 = (bf16[512,384]{1,0:T(8,128)(2,1)S(1)}, bf16[512,384]{1,0:T(8,128)(2,1)S(1)}, u32[]{:S(2)}, u32[]{:S(2)}) collective-permute-start(bf16[512,384]{1,0:T(8,128)(2,1)S(1)} %get-tuple-element.26), channel_id=1, source_target_pairs={{0,16},{1,17},{2,18},{3,19},{4,20},{5,21},{6,22},{7,23},{8,24},{9,... | collective-permute-start | bytes 1179656 | tf_op jit(solution)/shard_map/ppermute | solution.py:26
  58.0 5.0 %collective-permute-start.14 = (bf16[64,768]{1,0:T(8,128)(2,1)S(1)}, bf16[64,768]{1,0:T(8,128)(2,1)S(1)}, u32[]{:S(2)}, u32[]{:S(2)}) collective-permute-start(bf16[64,768]{1,0:T(8,128)(2,1)S(1)} %get-tuple-element.38), channel_id=1, source_target_pairs={{0,4},{1,65},{2,6},{3,67},{4,0},{5,69},{6,2},{7,71},{8,12},{9,73},... | collective-permute-start | bytes 294920 | tf_op jit(solution)/shard_map/ppermute | solution.py:26
  58.2 6.7 %collective-permute-start.15 = (bf16[64,768]{1,0:T(8,128)(2,1)S(1)}, bf16[64,768]{1,0:T(8,128)(2,1)S(1)}, u32[]{:S(2)}, u32[]{:S(2)}) collective-permute-start(bf16[64,768]{1,0:T(8,128)(2,1)S(1)} %get-tuple-element.40), channel_id=1, source_target_pairs={{0,12},{1,193},{2,14},{3,195},{4,8},{5,197},{6,10},{7,199},{8,4},{... | collective-permute-start | bytes 294920 | tf_op jit(solution)/shard_map/ppermute | solution.py:26
  59.7 6.5 %collective-permute-start.16 = (bf16[64,768]{1,0:T(8,128)(2,1)S(1)}, bf16[64,768]{1,0:T(8,128)(2,1)S(1)}, u32[]{:S(2)}, u32[]{:S(2)}) collective-permute-start(bf16[64,768]{1,0:T(8,128)(2,1)S(1)} %get-tuple-element.39), channel_id=1, source_target_pairs={{0,8},{1,129},{2,10},{3,131},{4,12},{5,133},{6,14},{7,135},{8,0},{... | collective-permute-start | bytes 294920 | tf_op jit(solution)/shard_map/ppermute | solution.py:26
  66.2 2.8 %collective-permute-start.18 = (bf16[16,768]{1,0:T(8,128)(2,1)S(1)}, bf16[16,768]{1,0:T(8,128)(2,1)S(1)}, u32[]{:S(2)}, u32[]{:S(2)}) collective-permute-start(bf16[16,768]{1,0:T(8,128)(2,1)S(1)} %get-tuple-element.45), channel_id=1, source_target_pairs={{0,16},{1,17},{2,18},{3,19},{4,20},{5,21},{6,22},{7,23},{8,24},{9,... | collective-permute-start | bytes 73736 | tf_op jit(solution)/shard_map/ppermute | solution.py:26
  67.5 4.5 %collective-permute-start.19 = (bf16[16,768]{1,0:T(8,128)(2,1)S(1)}, bf16[16,768]{1,0:T(8,128)(2,1)S(1)}, u32[]{:S(2)}, u32[]{:S(2)}) collective-permute-start(bf16[16,768]{1,0:T(8,128)(2,1)S(1)} %get-tuple-element.46), channel_id=1, source_target_pairs={{0,48},{1,49},{2,50},{3,51},{4,52},{5,53},{6,54},{7,55},{8,56},{9,... | collective-permute-start | bytes 73736 | tf_op jit(solution)/shard_map/ppermute | solution.py:26
  68.1 3.9 %collective-permute-start.17 = (bf16[16,768]{1,0:T(8,128)(2,1)S(1)}, bf16[16,768]{1,0:T(8,128)(2,1)S(1)}, u32[]{:S(2)}, u32[]{:S(2)}) collective-permute-start(bf16[16,768]{1,0:T(8,128)(2,1)S(1)} %get-tuple-element.47), channel_id=1, source_target_pairs={{0,32},{1,33},{2,34},{3,35},{4,36},{5,37},{6,38},{7,39},{8,40},{9,... | collective-permute-start | bytes 73736 | tf_op jit(solution)/shard_map/ppermute | solution.py:26
  77.1 11.5 %collective-permute-start.20 = (bf16[16,1536]{1,0:T(8,128)(2,1)S(1)}, bf16[16,1536]{1,0:T(8,128)(2,1)S(1)}, u32[]{:S(2)}, u32[]{:S(2)}) collective-permute-start(bf16[16,1536]{1,0:T(8,128)(2,1)S(1)} %pad_maximum_fusion.2), channel_id=1, source_target_pairs={{0,1},{1,0},{2,3},{3,2},{4,5},{5,4},{6,7},{7,6},{8,9},{9,8},{10,11... | collective-permute-start | bytes 147464 | tf_op jit(solution)/shard_map/ppermute | solution.py:26
  88.6 6.9 %collective-permute-start.21 = (bf16[16,768]{1,0:T(8,128)(2,1)S(1)}, bf16[16,768]{1,0:T(8,128)(2,1)S(1)}, u32[]{:S(2)}, u32[]{:S(2)}) collective-permute-start(bf16[16,768]{1,0:T(8,128)(2,1)S(1)} %dynamic-slice_convert_fusion), channel_id=1, source_target_pairs={{0,2},{1,3},{2,0},{3,1},{4,6},{5,7},{6,4},{7,5},{8,10},{9,11},{10,... | collective-permute-start | bytes 73736 | tf_op jit(solution)/shard_map/ppermute | solution.py:26

commit v5 on v4

--- a/solution.py
+++ b/solution.py
@@ -56,7 +56,7 @@
 def attention_kernel(chunk, parity_ref, *refs):
     queries, grads_out = (refs[0], refs[2]), (refs[1], refs[3])
     keys, values = refs[4:8], refs[8:12]
-    parts, grads_ref = refs[12:16], refs[16]
+    parts, grads_ref, probs_ref = refs[12:15], refs[15], refs[16]
     rows = keys[0].shape[0]
     tokens = queries[0].shape[0]
     power = SCALE * math.log2(math.e)
@@ -77,8 +77,10 @@
         ]
 
     def add(n, at, q, g, probs, grads):
+        probs_ref[:, pl.ds(n * tokens + at, chunk)] = probs[0]
         for i in range(4):
             grads_ref[pl.ds(i * rows, rows), pl.ds(n * tokens + at, chunk)] = grads[i]
+        for i in range(1, 4):
             key_sums[i] += dot(grads[i], q)
             value_sums[i] += dot(probs[i], g)
 
@@ -93,9 +95,9 @@
             add(*behind)
         behind = (*place, q, g, probs, grads)
     add(*behind)
-    for i in range(4):
-        parts[i][:, :HD] = narrow(key_sums[i] * SCALE)
-        parts[i][:, HD:] = narrow(value_sums[i])
+    for i in range(1, 4):
+        parts[i - 1][:, :HD] = narrow(key_sums[i] * SCALE)
+        parts[i - 1][:, HD:] = narrow(value_sums[i])
 
 
 def attention(parity, queries, grad_out, far, blocks):
@@ -109,15 +111,17 @@
     value = pl.BlockSpec((rows, HD), lambda h, parity: (0, heads + h))
     part = pl.BlockSpec((rows, 2 * HD), lambda h, parity: (0, h))
     grads = pl.BlockSpec((4 * rows, 2 * tokens), lambda h, parity: (h, 0))
+    probs = pl.BlockSpec((rows, 2 * tokens), lambda h, parity: (h, 0))
     scores = heads * 2 * tokens * 4 * rows
-    shapes = [b.shape for b in blocks] + [(heads * 4 * rows, 2 * tokens)]
+    shapes = [b.shape for b in blocks[1:]]
+    shapes += [(heads * n * rows, 2 * tokens) for n in (4, 1)]
     return pl.pallas_call(
         functools.partial(attention_kernel, tokens // 4),
         grid_spec=pltpu.PrefetchScalarGridSpec(
             num_scalar_prefetch=1,
             grid=(heads,),
             in_specs=[own] * 2 + [first, second] + [key] * 4 + [value] * 4,
-            out_specs=[part] * 4 + [grads],
+            out_specs=[part] * 3 + [grads, probs],
         ),
         out_shape=[jax.ShapeDtypeStruct(shape, jnp.bfloat16) for shape in shapes],
         compiler_params=pltpu.CompilerParams(vmem_limit_bytes=24 * 2**20),
@@ -131,16 +135,22 @@
 
 
 def query_kernel(parity_ref, *refs):
-    keys, grads_ref, near_ref, far_ref = refs[0:4], refs[4], refs[5], refs[6]
+    keys, grads_ref, probs_ref = refs[0:4], refs[4], refs[5]
+    queries, grads_out = (refs[6], refs[8]), (refs[7], refs[9])
+    near_ref, far_ref, own_ref = refs[10:]
     rows = keys[0].shape[0]
     tokens = near_ref.shape[0]
     for n, out_ref in enumerate((near_ref, far_ref)):
         some = pl.ds(n * tokens, tokens)
         dq = sum(dot(k[...], grads_ref[pl.ds(i * rows, rows), some], TN) for i, k in enumerate(keys))
         out_ref[...] = narrow(dq.T * SCALE)
-
-
-def query_grads(parity, blocks, grad_scores, shape):
+    spans = [pl.ds(n * tokens, tokens) for n in range(2)]
+    dk = sum(dot(grads_ref[pl.ds(0, rows), t], q[...]) for t, q in zip(spans, queries))
+    own_ref[:, :HD] = dk * SCALE
+    own_ref[:, HD:] = sum(dot(probs_ref[:, t], g[...]) for t, g in zip(spans, grads_out))
+
+
+def query_grads(parity, blocks, grad_scores, probs, queries, grad_out, far, shape):
     tokens, width = shape
     rows, columns = blocks[0].shape
     heads = columns // (2 * HD)
@@ -150,15 +160,19 @@
             num_scalar_prefetch=1,
             grid=(heads,),
             in_specs=[pl.BlockSpec((rows, HD), lambda h, parity: (0, h))] * 4
-            + [pl.BlockSpec((4 * rows, 2 * tokens), lambda h, parity: (h, 0))],
+            + [pl.BlockSpec((n * rows, 2 * tokens), lambda h, parity: (h, 0)) for n in (4, 1)]
+            + [pl.BlockSpec((tokens, HD), lambda h, parity: (0, h))] * 3
+            + [pl.BlockSpec((tokens, HD), lambda h, parity: (0, heads + h))],
             out_specs=[
                 pl.BlockSpec((tokens, HD), lambda h, parity: (0, parity[0] * heads + h)),
                 pl.BlockSpec((tokens, HD), lambda h, parity: (0, h)),
+                pl.BlockSpec((rows, 2 * HD), lambda h, parity: (0, h)),
             ],
         ),
         out_shape=[
             jax.ShapeDtypeStruct(shape, jnp.bfloat16),
             jax.ShapeDtypeStruct((tokens, heads * HD), jnp.bfloat16),
+            jax.ShapeDtypeStruct((rows, columns), jnp.float32),
         ],
         compiler_params=pltpu.CompilerParams(vmem_limit_bytes=16 * 2**20),
         cost_estimate=pl.CostEstimate(
@@ -167,7 +181,7 @@
             transcendentals=0,
         ),
         name="query_grads",
-    )(parity, *blocks, grad_scores)
+    )(parity, *blocks, grad_scores, probs, queries, grad_out, far, far)
 
 
 def project_kernel(
@@ -268,10 +282,12 @@
     rows = join(*gather(rows, LATE))
     blocks = gather(rows, EARLY)
 
-    *parts, grad_scores = attention(spot, *near, far, blocks)
-    grad_queries, grad_far = query_grads(spot, blocks, grad_scores, queries.shape)
-
-    total = scatter_sum(parts, EARLY)
+    *parts, grad_scores, probs = attention(spot, *near, far, blocks)
+    grad_queries, grad_far, own = query_grads(
+        spot, blocks, grad_scores, probs, *near, far, queries.shape
+    )
+
+    total = scatter_sum([own, *parts], EARLY)
     grad_far = swap(grad_far, (Z, Z))
     total, grad_far = lax.optimization_barrier((total, grad_far))
     total = scatter_sum(jnp.split(total, 4), LATE)

time: 96.3 us -> 96.4 us (level)
  Pallas kernels: 19.7 us -> 20.7 us
  transfers between devices with their start and end apart: 22 -> 22, of which waited for: 14 -> 15; matrix products, arithmetic and copies ran while one was open for 2% -> 2% of each run, Pallas kernels for 3% -> 4%
where the time goes in v5:
time: 96.4 us; the launch traced here: 96.2 us
  starting transfers between devices  40.3 us (42%)
  waiting for transfers between devices  31.1 us (32%)
  Pallas kernels  20.7 us (21%)
  local copies, waits for them, and re-layouts  2.38 us (2%)
  other arithmetic  0.98 us (1%)
    ppermute x22, starting transfers between devices, swap(): return lax.ppermute(block, ('seq', 'tensor'), pairs)  40.3 us
    ppermute x22, waiting for transfers between devices, swap(): return lax.ppermute(block, ('seq', 'tensor'), pairs)  31.1 us
    pallas_call x1, Pallas kernels, attention(): pl.pallas_call(functools.partial(attention_kernel, tokens // 4), grid_spe...  12.3 us
    pallas_call x1, Pallas kernels, project(): pl.pallas_call(functools.partial(project_kernel, blocks), in_specs=[pl.Bl...  5.01 us
    pallas_call x1, Pallas kernels, query_grads(): pl.pallas_call(query_kernel, grid_spec=pltpu.PrefetchScalarGridSpec(num_s...  3.38 us
    dynamic_slice x2, local copies, waits for them, and re-layouts, columns(): return lax.dynamic_slice_in_dim(array, which * half, half, axis=1)  2.28 us
  transfers between devices with their start and end apart: 22, of which 15 were waited for; matrix products, arithmetic and copies ran while one was open for 2% of the time, Pallas kernels for 4%

profile of v5, /device:TPU:1, one launch (start us, length us, event | category | flops | bytes accessed | tf_op | source)
XLA Modules:
  0.0 96.2 jit_solution(15081209065278932448)
XLA Ops:
  1.5 2.6 %collective-permute-start = (bf16[16,768]{1,0:T(8,128)(2,1)S(1)}, bf16[16,768]{1,0:T(8,128)(2,1)S(1)}, u32[]{:S(2)}, u32[]{:S(2)}) collective-permute-start(bf16[16,768]{1,0:T(8,128)(2,1)S(1)} %pad_maximum_fusion.4), channel_id=1, source_target_pairs={{0,16},{1,17},{2,18},{3,19},{4,20},{5,21},{6,22},{7,23},{8,24},{9,... | collective-permute-start | bytes 73736 | tf_op jit(solution)/shard_map/ppermute | solution.py:26
  4.0 2.8 %collective-permute-start.1 = (bf16[16,768]{1,0:T(8,128)(2,1)S(1)}, bf16[16,768]{1,0:T(8,128)(2,1)S(1)}, u32[]{:S(2)}, u32[]{:S(2)}) collective-permute-start(bf16[16,768]{1,0:T(8,128)(2,1)S(1)} %pad_maximum_fusion.4), channel_id=1, source_target_pairs={{0,48},{1,49},{2,50},{3,51},{4,52},{5,53},{6,54},{7,55},{8,56},{9,... | collective-permute-start | bytes 73736 | tf_op jit(solution)/shard_map/ppermute | solution.py:26
  7.0 1.5 %constant_dynamic-slice_fusion.4 = (bf16[512,384]{1,0:T(8,128)(2,1)S(1)}, bf16[512,384]{1,0:T(8,128)(2,1)S(1)}, bf16[512,384]{1,0:T(8,128)(2,1)S(1)}, bf16[512,384]{1,0:T(8,128)(2,1)S(1)}) fusion(bf16[512,768]{1,0:T(8,128)(2,1)} %param.9, s32[]{:T(128)S(6)} %select_n.51, s32[]{:T(128)S(6)} %select_n.50, bf16[512,768]{1,0:T(8,128)(2,1)} %param.6), kind=kLoop, calls=%fused_computation.20 | loop fusion | bytes 3145736 | tf_op jit(solution)/shard_map/dynamic_slice | solution.py:270
  8.6 1.8 %collective-permute-done.2 = bf16[16,768]{1,0:T(8,128)(2,1)S(1)} collective-permute-done((bf16[16,768]{1,0:T(8,128)(2,1)S(1)}, bf16[16,768]{1,0:T(8,128)(2,1)S(1)}, u32[]{:S(2)}, u32[]{:S(2)}) %collective-permute-start.2) | collective-permute-done | bytes 24608 | tf_op jit(solution)/shard_map/ppermute | solution.py:26
  10.4 1.4 %collective-permute-start.3 = (bf16[64,768]{1,0:T(8,128)(2,1)S(1)}, bf16[64,768]{1,0:T(8,128)(2,1)S(1)}, u32[]{:S(2)}, u32[]{:S(2)}) collective-permute-start(bf16[64,768]{1,0:T(8,128)(2,1)S(1)} %pad_maximum_fusion.1), channel_id=1, source_target_pairs={{0,4},{1,65},{2,6},{3,67},{4,0},{5,69},{6,2},{7,71},{8,12},{9,73},... | collective-permute-start | bytes 294920 | tf_op jit(solution)/shard_map/ppermute | solution.py:26
  12.3 2.0 %collective-permute-start.4 = (bf16[64,768]{1,0:T(8,128)(2,1)S(1)}, bf16[64,768]{1,0:T(8,128)(2,1)S(1)}, u32[]{:S(2)}, u32[]{:S(2)}) collective-permute-start(bf16[64,768]{1,0:T(8,128)(2,1)S(1)} %pad_maximum_fusion.1), channel_id=1, source_target_pairs={{0,12},{1,193},{2,14},{3,195},{4,8},{5,197},{6,10},{7,199},{8,4},{... | collective-permute-start | bytes 294920 | tf_op jit(solution)/shard_map/ppermute | solution.py:26
  15.2 1.9 %collective-permute-done.4 = bf16[64,768]{1,0:T(8,128)(2,1)S(1)} collective-permute-done((bf16[64,768]{1,0:T(8,128)(2,1)S(1)}, bf16[64,768]{1,0:T(8,128)(2,1)S(1)}, u32[]{:S(2)}, u32[]{:S(2)}) %collective-permute-start.4) | collective-permute-done | bytes 98336 | tf_op jit(solution)/shard_map/ppermute | solution.py:26
  17.1 2.2 %collective-permute-done.5 = bf16[64,768]{1,0:T(8,128)(2,1)S(1)} collective-permute-done((bf16[64,768]{1,0:T(8,128)(2,1)S(1)}, bf16[64,768]{1,0:T(8,128)(2,1)S(1)}, u32[]{:S(2)}, u32[]{:S(2)}) %collective-permute-start.5) | collective-permute-done | bytes 98336 | tf_op jit(solution)/shard_map/ppermute | solution.py:26
  19.3 1.3 %collective-permute-start.6 = (bf16[256,768]{1,0:T(8,128)(2,1)S(1)}, bf16[256,768]{1,0:T(8,128)(2,1)S(1)}, u32[]{:S(2)}, u32[]{:S(2)}) collective-permute-start(bf16[256,768]{1,0:T(8,128)(2,1)S(1)} %constant_dynamic-update-slice_fusion.refs_4_.refs_8_.refs_0_), channel_id=1, source_target_pairs={{0,64},{1,5},{2,66},{3,7},{4,68},{5,1},{6,70},{7,3},{8,72},{9,13},... | collective-permute-start | bytes 1179656 | tf_op jit(solution)/shard_map/ppermute | solution.py:26
  20.6 1.8 %collective-permute-start.7 = (bf16[256,768]{1,0:T(8,128)(2,1)S(1)}, bf16[256,768]{1,0:T(8,128)(2,1)S(1)}, u32[]{:S(2)}, u32[]{:S(2)}) collective-permute-start(bf16[256,768]{1,0:T(8,128)(2,1)S(1)} %constant_dynamic-update-slice_fusion.refs_4_.refs_8_.refs_0_), channel_id=1, source_target_pairs={{0,192},{1,13},{2,194},{3,15},{4,196},{5,9},{6,198},{7,11},{8,200}... | collective-permute-start | bytes 1179656 | tf_op jit(solution)/shard_map/ppermute | solution.py:26
  23.1 3.3 %collective-permute-done.6.refs_5_.refs_9_.refs_1_ = bf16[256,768]{1,0:T(8,128)(2,1)S(1)} collective-permute-done((bf16[256,768]{1,0:T(8,128)(2,1)S(1)}, bf16[256,768]{1,0:T(8,128)(2,1)S(1)}, u32[]{:S(2)}, u32[]{:S(2)}) %collective-permute-start.6) | collective-permute-done | bytes 393248 | tf_op jit(solution)/shard_map/ppermute | solution.py:26
  26.3 6.6 %collective-permute-done.7.refs_6_.refs_10_.refs_2_ = bf16[256,768]{1,0:T(8,128)(2,1)S(1)} collective-permute-done((bf16[256,768]{1,0:T(8,128)(2,1)S(1)}, bf16[256,768]{1,0:T(8,128)(2,1)S(1)}, u32[]{:S(2)}, u32[]{:S(2)}) %collective-permute-start.7) | collective-permute-done | bytes 393248 | tf_op jit(solution)/shard_map/ppermute | solution.py:26
  33.0 12.3 %attention_grads.1 = (bf16[256,768]{1,0:T(8,128)(2,1)S(1)}, bf16[256,768]{1,0:T(8,128)(2,1)S(1)}, bf16[256,768]{1,0:T(8,128)(2,1)S(1)}, bf16[3072,1024]{1,0:T(8,128)(2,1)S(1)}, bf16[768,1024]{1,0:T(8,128)(2,1)S(1)}) custom-call(s32[1]{0:T(128)} %bitcast.parity_ref, bf16[512,384]{1,0:T(8,128)(2,1)S(1)} %get-tuple-element.19.refs_0_.refs_6_, ...), custom_call_target="tpu_custom_call" | custom-call | flops 3221225472 | bytes 11010048 | tf_op jit(solution)/shard_map/attention_grads/pallas_call | solution.py:118
  45.3 1.9 %collective-permute-start.11 = (bf16[256,768]{1,0:T(8,128)(2,1)S(1)}, bf16[256,768]{1,0:T(8,128)(2,1)S(1)}, u32[]{:S(2)}, u32[]{:S(2)}) collective-permute-start(bf16[256,768]{1,0:T(8,128)(2,1)S(1)} %get-tuple-element.26), channel_id=1, source_target_pairs={{0,192},{1,13},{2,194},{3,15},{4,196},{5,9},{6,198},{7,11},{8,200}... | collective-permute-start | bytes 1179656 | tf_op jit(solution)/shard_map/ppermute | solution.py:26
  47.2 1.3 %collective-permute-start.12 = (bf16[256,768]{1,0:T(8,128)(2,1)S(1)}, bf16[256,768]{1,0:T(8,128)(2,1)S(1)}, u32[]{:S(2)}, u32[]{:S(2)}) collective-permute-start(bf16[256,768]{1,0:T(8,128)(2,1)S(1)} %get-tuple-element.27), channel_id=1, source_target_pairs={{0,128},{1,9},{2,130},{3,11},{4,132},{5,13},{6,134},{7,15},{8,136}... | collective-permute-start | bytes 1179656 | tf_op jit(solution)/shard_map/ppermute | solution.py:26
  48.6 3.4 %query_grads.1 = (bf16[512,768]{1,0:T(8,128)(2,1)}, bf16[512,384]{1,0:T(8,128)(2,1)S(1)}, f32[256,768]{1,0:T(8,128)S(1)}) custom-call(s32[1]{0:T(128)} %bitcast.parity_ref, bf16[256,768]{1,0:T(8,128)(2,1)S(1)} %constant_dynamic-update-slice_fusion.refs_4_.refs_8_.refs_0_, bf16[256,768]{1,0:T(8,128)(2,1)S(1)} %collective-permute-done.6.refs_5_.refs_9_.refs_1_, ...), custom_call_target="tpu_custom_call" | custom-call | flops 805306368 | bytes 6291456 | tf_op jit(solution)/shard_map/query_grads/pallas_call | solution.py:157
  52.0 0.9 collective-permute-start.13
  52.9 3.3 %collective-permute-done.11 = bf16[256,768]{1,0:T(8,128)(2,1)S(1)} collective-permute-done((bf16[256,768]{1,0:T(8,128)(2,1)S(1)}, bf16[256,768]{1,0:T(8,128)(2,1)S(1)}, u32[]{:S(2)}, u32[]{:S(2)}) %collective-permute-start.11) | collective-permute-done | bytes 393248 | tf_op jit(solution)/shard_map/ppermute | solution.py:26
  56.2 1.5 %collective-permute-done.12 = bf16[256,768]{1,0:T(8,128)(2,1)S(1)} collective-permute-done((bf16[256,768]{1,0:T(8,128)(2,1)S(1)}, bf16[256,768]{1,0:T(8,128)(2,1)S(1)}, u32[]{:S(2)}, u32[]{:S(2)}) %collective-permute-start.12) | collective-permute-done | bytes 393248 | tf_op jit(solution)/shard_map/ppermute | solution.py:26
  57.9 1.0 %collective-permute-done.13.far_ref = bf16[512,384]{1,0:T(8,128)(2,1)S(1)} collective-permute-done((bf16[512,384]{1,0:T(8,128)(2,1)S(1)}, bf16[512,384]{1,0:T(8,128)(2,1)S(1)}, u32[]{:S(2)}, u32[]{:S(2)}) %collective-permute-start.13) | collective-permute-done | bytes 393248 | tf_op jit(solution)/shard_map/ppermute | solution.py:26
  59.1 1.5 %collective-permute-start.15 = (bf16[64,768]{1,0:T(8,128)(2,1)S(1)}, bf16[64,768]{1,0:T(8,128)(2,1)S(1)}, u32[]{:S(2)}, u32[]{:S(2)}) collective-permute-start(bf16[64,768]{1,0:T(8,128)(2,1)S(1)} %get-tuple-element.42), channel_id=1, source_target_pairs={{0,12},{1,193},{2,14},{3,195},{4,8},{5,197},{6,10},{7,199},{8,4},{... | collective-permute-start | bytes 294920 | tf_op jit(solution)/shard_map/ppermute | solution.py:26
  60.7 1.6 %collective-permute-start.16 = (bf16[64,768]{1,0:T(8,128)(2,1)S(1)}, bf16[64,768]{1,0:T(8,128)(2,1)S(1)}, u32[]{:S(2)}, u32[]{:S(2)}) collective-permute-start(bf16[64,768]{1,0:T(8,128)(2,1)S(1)} %get-tuple-element.41), channel_id=1, source_target_pairs={{0,8},{1,129},{2,10},{3,131},{4,12},{5,133},{6,14},{7,135},{8,0},{... | collective-permute-start | bytes 294920 | tf_op jit(solution)/shard_map/ppermute | solution.py:26
  62.3 1.5 %collective-permute-done.14 = bf16[64,768]{1,0:T(8,128)(2,1)S(1)} collective-permute-done((bf16[64,768]{1,0:T(8,128)(2,1)S(1)}, bf16[64,768]{1,0:T(8,128)(2,1)S(1)}, u32[]{:S(2)}, u32[]{:S(2)}) %collective-permute-start.14) | collective-permute-done | bytes 98336 | tf_op jit(solution)/shard_map/ppermute | solution.py:26
  63.8 1.3 %collective-permute-done.15 = bf16[64,768]{1,0:T(8,128)(2,1)S(1)} collective-permute-done((bf16[64,768]{1,0:T(8,128)(2,1)S(1)}, bf16[64,768]{1,0:T(8,128)(2,1)S(1)}, u32[]{:S(2)}, u32[]{:S(2)}) %collective-permute-start.15) | collective-permute-done | bytes 98336 | tf_op jit(solution)/shard_map/ppermute | solution.py:26
  65.1 1.5 %collective-permute-done.16 = bf16[64,768]{1,0:T(8,128)(2,1)S(1)} collective-permute-done((bf16[64,768]{1,0:T(8,128)(2,1)S(1)}, bf16[64,768]{1,0:T(8,128)(2,1)S(1)}, u32[]{:S(2)}, u32[]{:S(2)}) %collective-permute-start.16) | collective-permute-done | bytes 98336 | tf_op jit(solution)/shard_map/ppermute | solution.py:26
  67.5 1.2 %collective-permute-start.19 = (bf16[16,768]{1,0:T(8,128)(2,1)S(1)}, bf16[16,768]{1,0:T(8,128)(2,1)S(1)}, u32[]{:S(2)}, u32[]{:S(2)}) collective-permute-start(bf16[16,768]{1,0:T(8,128)(2,1)S(1)} %get-tuple-element.48), channel_id=1, source_target_pairs={{0,48},{1,49},{2,50},{3,51},{4,52},{5,53},{6,54},{7,55},{8,56},{9,... | collective-permute-start | bytes 73736 | tf_op jit(solution)/shard_map/ppermute | solution.py:26
  69.4 2.5 %collective-permute-done.19 = bf16[16,768]{1,0:T(8,128)(2,1)S(1)} collective-permute-done((bf16[16,768]{1,0:T(8,128)(2,1)S(1)}, bf16[16,768]{1,0:T(8,128)(2,1)S(1)}, u32[]{:S(2)}, u32[]{:S(2)}) %collective-permute-start.19) | collective-permute-done | bytes 24608 | tf_op jit(solution)/shard_map/ppermute | solution.py:26
  72.5 5.0 %project_rows.1 = (bf16[16,3072]{1,0:T(8,128)(2,1)S(1)}, bf16[512,768]{1,0:T(8,128)(2,1)}) custom-call(s32[1]{0:T(128)} %bitcast.parity_ref, f32[16,768]{1,0:T(8,128)S(1)} %slice_add_fusion.mine_ref, f32[16,768]{1,0:T(8,128)S(1)} %convert_add_fusion.3.other_ref, bf16[3072,768]{1,0:T(8,128)(2,1)} %key_ref.1, ...), custom_call_target="tpu_custom_call", output_to_operand_aliasing={{1}: (6, {})} | custom-call | tf_op jit(solution)/shard_map/project_rows/pallas_call | solution.py:249
  77.5 10.2 %collective-permute-start.20 = (bf16[16,1536]{1,0:T(8,128)(2,1)S(1)}, bf16[16,1536]{1,0:T(8,128)(2,1)S(1)}, u32[]{:S(2)}, u32[]{:S(2)}) collective-permute-start(bf16[16,1536]{1,0:T(8,128)(2,1)S(1)} %pad_maximum_fusion.2), channel_id=1, source_target_pairs={{0,1},{1,0},{2,3},{3,2},{4,5},{5,4},{6,7},{7,6},{8,9},{9,8},{10,11... | collective-permute-start | bytes 147464 | tf_op jit(solution)/shard_map/ppermute | solution.py:26
  87.8 0.9 collective-permute-done.20
  88.7 5.7 %collective-permute-start.21 = (bf16[16,768]{1,0:T(8,128)(2,1)S(1)}, bf16[16,768]{1,0:T(8,128)(2,1)S(1)}, u32[]{:S(2)}, u32[]{:S(2)}) collective-permute-start(bf16[16,768]{1,0:T(8,128)(2,1)S(1)} %dynamic-slice_convert_fusion), channel_id=1, source_target_pairs={{0,2},{1,3},{2,0},{3,1},{4,6},{5,7},{6,4},{7,5},{8,10},{9,11},{10,... | collective-permute-start | bytes 73736 | tf_op jit(solution)/shard_map/ppermute | solution.py:26
  94.4 1.2 %collective-permute-done.21 = bf16[16,768]{1,0:T(8,128)(2,1)S(1)} collective-permute-done((bf16[16,768]{1,0:T(8,128)(2,1)S(1)}, bf16[16,768]{1,0:T(8,128)(2,1)S(1)}, u32[]{:S(2)}, u32[]{:S(2)}) %collective-permute-start.21) | collective-permute-done | bytes 24608 | tf_op jit(solution)/shard_map/ppermute | solution.py:26
  (37 shorter events, 6.4 us)
Async XLA Ops:
  1.5 7.1 %collective-permute-start = (bf16[16,768]{1,0:T(8,128)(2,1)S(1)}, bf16[16,768]{1,0:T(8,128)(2,1)S(1)}, u32[]{:S(2)}, u32[]{:S(2)}) collective-permute-start(bf16[16,768]{1,0:T(8,128)(2,1)S(1)} %pad_maximum_fusion.4), channel_id=1, source_target_pairs={{0,16},{1,17},{2,18},{3,19},{4,20},{5,21},{6,22},{7,23},{8,24},{9,... | collective-permute-start | bytes 73736 | tf_op jit(solution)/shard_map/ppermute | solution.py:26
  4.0 4.6 %collective-permute-start.1 = (bf16[16,768]{1,0:T(8,128)(2,1)S(1)}, bf16[16,768]{1,0:T(8,128)(2,1)S(1)}, u32[]{:S(2)}, u32[]{:S(2)}) collective-permute-start(bf16[16,768]{1,0:T(8,128)(2,1)S(1)} %pad_maximum_fusion.4), channel_id=1, source_target_pairs={{0,48},{1,49},{2,50},{3,51},{4,52},{5,53},{6,54},{7,55},{8,56},{9,... | collective-permute-start | bytes 73736 | tf_op jit(solution)/shard_map/ppermute | solution.py:26
  6.8 3.6 %collective-permute-start.2 = (bf16[16,768]{1,0:T(8,128)(2,1)S(1)}, bf16[16,768]{1,0:T(8,128)(2,1)S(1)}, u32[]{:S(2)}, u32[]{:S(2)}) collective-permute-start(bf16[16,768]{1,0:T(8,128)(2,1)S(1)} %pad_maximum_fusion.3), channel_id=1, source_target_pairs={{0,32},{1,33},{2,34},{3,35},{4,36},{5,37},{6,38},{7,39},{8,40},{9,... | collective-permute-start | bytes 73736 | tf_op jit(solution)/shard_map/ppermute | solution.py:26
  10.4 4.7 %collective-permute-start.3 = (bf16[64,768]{1,0:T(8,128)(2,1)S(1)}, bf16[64,768]{1,0:T(8,128)(2,1)S(1)}, u32[]{:S(2)}, u32[]{:S(2)}) collective-permute-start(bf16[64,768]{1,0:T(8,128)(2,1)S(1)} %pad_maximum_fusion.1), channel_id=1, source_target_pairs={{0,4},{1,65},{2,6},{3,67},{4,0},{5,69},{6,2},{7,71},{8,12},{9,73},... | collective-permute-start | bytes 294920 | tf_op jit(solution)/shard_map/ppermute | solution.py:26
  11.8 21.2 %collective-permute-start.9 = (bf16[512,768]{1,0:T(8,128)(2,1)S(1)}, bf16[512,768]{1,0:T(8,128)(2,1)S(1)}, u32[]{:S(2)}, u32[]{:S(2)}) collective-permute-start(bf16[512,768]{1,0:T(8,128)(2,1)S(1)} %pad_maximum_fusion), channel_id=1, source_target_pairs={{0,16},{1,17},{2,18},{3,19},{4,20},{5,21},{6,22},{7,23},{8,24},{9,... | collective-permute-start | bytes 2359304 | tf_op jit(solution)/shard_map/ppermute | solution.py:26
  12.3 4.8 %collective-permute-start.4 = (bf16[64,768]{1,0:T(8,128)(2,1)S(1)}, bf16[64,768]{1,0:T(8,128)(2,1)S(1)}, u32[]{:S(2)}, u32[]{:S(2)}) collective-permute-start(bf16[64,768]{1,0:T(8,128)(2,1)S(1)} %pad_maximum_fusion.1), channel_id=1, source_target_pairs={{0,12},{1,193},{2,14},{3,195},{4,8},{5,197},{6,10},{7,199},{8,4},{... | collective-permute-start | bytes 294920 | tf_op jit(solution)/shard_map/ppermute | solution.py:26
  14.3 5.0 %collective-permute-start.5 = (bf16[64,768]{1,0:T(8,128)(2,1)S(1)}, bf16[64,768]{1,0:T(8,128)(2,1)S(1)}, u32[]{:S(2)}, u32[]{:S(2)}) collective-permute-start(bf16[64,768]{1,0:T(8,128)(2,1)S(1)} %pad_maximum_fusion.1), channel_id=1, source_target_pairs={{0,8},{1,129},{2,10},{3,131},{4,12},{5,133},{6,14},{7,135},{8,0},{... | collective-permute-start | bytes 294920 | tf_op jit(solution)/shard_map/ppermute | solution.py:26
  19.3 7.0 %collective-permute-start.6 = (bf16[256,768]{1,0:T(8,128)(2,1)S(1)}, bf16[256,768]{1,0:T(8,128)(2,1)S(1)}, u32[]{:S(2)}, u32[]{:S(2)}) collective-permute-start(bf16[256,768]{1,0:T(8,128)(2,1)S(1)} %constant_dynamic-update-slice_fusion.refs_4_.refs_8_.refs_0_), channel_id=1, source_target_pairs={{0,64},{1,5},{2,66},{3,7},{4,68},{5,1},{6,70},{7,3},{8,72},{9,13},... | collective-permute-start | bytes 1179656 | tf_op jit(solution)/shard_map/ppermute | solution.py:26
  20.6 12.3 %collective-permute-start.7 = (bf16[256,768]{1,0:T(8,128)(2,1)S(1)}, bf16[256,768]{1,0:T(8,128)(2,1)S(1)}, u32[]{:S(2)}, u32[]{:S(2)}) collective-permute-start(bf16[256,768]{1,0:T(8,128)(2,1)S(1)} %constant_dynamic-update-slice_fusion.refs_4_.refs_8_.refs_0_), channel_id=1, source_target_pairs={{0,192},{1,13},{2,194},{3,15},{4,196},{5,9},{6,198},{7,11},{8,200}... | collective-permute-start | bytes 1179656 | tf_op jit(solution)/shard_map/ppermute | solution.py:26
  22.4 10.5 %collective-permute-start.8 = (bf16[256,768]{1,0:T(8,128)(2,1)S(1)}, bf16[256,768]{1,0:T(8,128)(2,1)S(1)}, u32[]{:S(2)}, u32[]{:S(2)}) collective-permute-start(bf16[256,768]{1,0:T(8,128)(2,1)S(1)} %constant_dynamic-update-slice_fusion.refs_4_.refs_8_.refs_0_), channel_id=1, source_target_pairs={{0,128},{1,9},{2,130},{3,11},{4,132},{5,13},{6,134},{7,15},{8,136}... | collective-permute-start | bytes 1179656 | tf_op jit(solution)/shard_map/ppermute | solution.py:26
  45.2 7.7 %collective-permute-start.10 = (bf16[256,768]{1,0:T(8,128)(2,1)S(1)}, bf16[256,768]{1,0:T(8,128)(2,1)S(1)}, u32[]{:S(2)}, u32[]{:S(2)}) collective-permute-start(bf16[256,768]{1,0:T(8,128)(2,1)S(1)} %get-tuple-element.25), channel_id=1, source_target_pairs={{0,64},{1,5},{2,66},{3,7},{4,68},{5,1},{6,70},{7,3},{8,72},{9,13},... | collective-permute-start | bytes 1179656 | tf_op jit(solution)/shard_map/ppermute | solution.py:26
  45.3 10.8 %collective-permute-start.11 = (bf16[256,768]{1,0:T(8,128)(2,1)S(1)}, bf16[256,768]{1,0:T(8,128)(2,1)S(1)}, u32[]{:S(2)}, u32[]{:S(2)}) collective-permute-start(bf16[256,768]{1,0:T(8,128)(2,1)S(1)} %get-tuple-element.26), channel_id=1, source_target_pairs={{0,192},{1,13},{2,194},{3,15},{4,196},{5,9},{6,198},{7,11},{8,200}... | collective-permute-start | bytes 1179656 | tf_op jit(solution)/shard_map/ppermute | solution.py:26
  47.2 10.5 %collective-permute-start.12 = (bf16[256,768]{1,0:T(8,128)(2,1)S(1)}, bf16[256,768]{1,0:T(8,128)(2,1)S(1)}, u32[]{:S(2)}, u32[]{:S(2)}) collective-permute-start(bf16[256,768]{1,0:T(8,128)(2,1)S(1)} %get-tuple-element.27), channel_id=1, source_target_pairs={{0,128},{1,9},{2,130},{3,11},{4,132},{5,13},{6,134},{7,15},{8,136}... | collective-permute-start | bytes 1179656 | tf_op jit(solution)/shard_map/ppermute | solution.py:26
  52.0 6.9 %collective-permute-start.13 = (bf16[512,384]{1,0:T(8,128)(2,1)S(1)}, bf16[512,384]{1,0:T(8,128)(2,1)S(1)}, u32[]{:S(2)}, u32[]{:S(2)}) collective-permute-start(bf16[512,384]{1,0:T(8,128)(2,1)S(1)} %get-tuple-element.28), channel_id=1, source_target_pairs={{0,16},{1,17},{2,18},{3,19},{4,20},{5,21},{6,22},{7,23},{8,24},{9,... | collective-permute-start | bytes 1179656 | tf_op jit(solution)/shard_map/ppermute | solution.py:26
  58.9 4.9 %collective-permute-start.14 = (bf16[64,768]{1,0:T(8,128)(2,1)S(1)}, bf16[64,768]{1,0:T(8,128)(2,1)S(1)}, u32[]{:S(2)}, u32[]{:S(2)}) collective-permute-start(bf16[64,768]{1,0:T(8,128)(2,1)S(1)} %get-tuple-element.40), channel_id=1, source_target_pairs={{0,4},{1,65},{2,6},{3,67},{4,0},{5,69},{6,2},{7,71},{8,12},{9,73},... | collective-permute-start | bytes 294920 | tf_op jit(solution)/shard_map/ppermute | solution.py:26
  59.1 6.0 %collective-permute-start.15 = (bf16[64,768]{1,0:T(8,128)(2,1)S(1)}, bf16[64,768]{1,0:T(8,128)(2,1)S(1)}, u32[]{:S(2)}, u32[]{:S(2)}) collective-permute-start(bf16[64,768]{1,0:T(8,128)(2,1)S(1)} %get-tuple-element.42), channel_id=1, source_target_pairs={{0,12},{1,193},{2,14},{3,195},{4,8},{5,197},{6,10},{7,199},{8,4},{... | collective-permute-start | bytes 294920 | tf_op jit(solution)/shard_map/ppermute | solution.py:26
  60.7 5.9 %collective-permute-start.16 = (bf16[64,768]{1,0:T(8,128)(2,1)S(1)}, bf16[64,768]{1,0:T(8,128)(2,1)S(1)}, u32[]{:S(2)}, u32[]{:S(2)}) collective-permute-start(bf16[64,768]{1,0:T(8,128)(2,1)S(1)} %get-tuple-element.41), channel_id=1, source_target_pairs={{0,8},{1,129},{2,10},{3,131},{4,12},{5,133},{6,14},{7,135},{8,0},{... | collective-permute-start | bytes 294920 | tf_op jit(solution)/shard_map/ppermute | solution.py:26
  66.7 2.8 %collective-permute-start.18 = (bf16[16,768]{1,0:T(8,128)(2,1)S(1)}, bf16[16,768]{1,0:T(8,128)(2,1)S(1)}, u32[]{:S(2)}, u32[]{:S(2)}) collective-permute-start(bf16[16,768]{1,0:T(8,128)(2,1)S(1)} %get-tuple-element.47), channel_id=1, source_target_pairs={{0,16},{1,17},{2,18},{3,19},{4,20},{5,21},{6,22},{7,23},{8,24},{9,... | collective-permute-start | bytes 73736 | tf_op jit(solution)/shard_map/ppermute | solution.py:26
  67.5 4.5 %collective-permute-start.19 = (bf16[16,768]{1,0:T(8,128)(2,1)S(1)}, bf16[16,768]{1,0:T(8,128)(2,1)S(1)}, u32[]{:S(2)}, u32[]{:S(2)}) collective-permute-start(bf16[16,768]{1,0:T(8,128)(2,1)S(1)} %get-tuple-element.48), channel_id=1, source_target_pairs={{0,48},{1,49},{2,50},{3,51},{4,52},{5,53},{6,54},{7,55},{8,56},{9,... | collective-permute-start | bytes 73736 | tf_op jit(solution)/shard_map/ppermute | solution.py:26
  68.7 3.8 %collective-permute-start.17 = (bf16[16,768]{1,0:T(8,128)(2,1)S(1)}, bf16[16,768]{1,0:T(8,128)(2,1)S(1)}, u32[]{:S(2)}, u32[]{:S(2)}) collective-permute-start(bf16[16,768]{1,0:T(8,128)(2,1)S(1)} %get-tuple-element.49), channel_id=1, source_target_pairs={{0,32},{1,33},{2,34},{3,35},{4,36},{5,37},{6,38},{7,39},{8,40},{9,... | collective-permute-start | bytes 73736 | tf_op jit(solution)/shard_map/ppermute | solution.py:26
  77.5 11.1 %collective-permute-start.20 = (bf16[16,1536]{1,0:T(8,128)(2,1)S(1)}, bf16[16,1536]{1,0:T(8,128)(2,1)S(1)}, u32[]{:S(2)}, u32[]{:S(2)}) collective-permute-start(bf16[16,1536]{1,0:T(8,128)(2,1)S(1)} %pad_maximum_fusion.2), channel_id=1, source_target_pairs={{0,1},{1,0},{2,3},{3,2},{4,5},{5,4},{6,7},{7,6},{8,9},{9,8},{10,11... | collective-permute-start | bytes 147464 | tf_op jit(solution)/shard_map/ppermute | solution.py:26
  88.7 6.9 %collective-permute-start.21 = (bf16[16,768]{1,0:T(8,128)(2,1)S(1)}, bf16[16,768]{1,0:T(8,128)(2,1)S(1)}, u32[]{:S(2)}, u32[]{:S(2)}) collective-permute-start(bf16[16,768]{1,0:T(8,128)(2,1)S(1)} %dynamic-slice_convert_fusion), channel_id=1, source_target_pairs={{0,2},{1,3},{2,0},{3,1},{4,6},{5,7},{6,4},{7,5},{8,10},{9,11},{10,... | collective-permute-start | bytes 73736 | tf_op jit(solution)/shard_map/ppermute | solution.py:26
